TPU v7x, 32 devices: a whole 2x2x4 slice. The times are simulated.
32 devices in a mesh: groups: 2 (over x), attn: 16 (over z, y, core).
Axes of the slice: x: 2, y: 2, z: 4, core: 2. Of those that a mesh axis runs over, the one named last changes fastest.
Arguments:
- hidden_states: bfloat16 [16, 16384], P('groups', 'attn'), parts along dimension 0, may hold values from -6 to 6
- norm_gain: float32 [16384], replicated, may hold values from 0.1 to 1.9
- w_query: bfloat16 [16384, 8192], P(None, 'attn'), may hold values from -0.046875 to 0.046875
- w_kv: bfloat16 [16384, 1024], P('attn'), may hold values from -0.046875 to 0.046875
- w_out: bfloat16 [8192, 16384], P('attn'), may hold values from -0.5 to 0.5
- k_cache: bfloat16 [1152, 128, 128], P(('groups', 'attn')), parts along dimension 0, may hold values from -130 to 130
- v_cache: bfloat16 [1152, 128, 128], P(('groups', 'attn')), parts along dimension 0, may hold values from -6 to 6
- block_table: int32 [16, 4, 32], P('groups'), parts along dimension 0, may hold values from -1 to 575, as said below
- lengths: int32 [16], P('groups'), parts along dimension 0, may hold values from 1 to 4096, as said below
Outputs:
- attn_out: bfloat16 [16, 16384], P('groups', 'attn'), parts along dimension 0
- new_entries: bfloat16 [16, 1024], P('groups'), parts along dimension 0
There are 2 independent parts, one for each index of `groups`. A program takes and returns all parts, laid end to end along the dimension named above; an argument that names none is the same for every part. Nothing has to cross between parts.
Inputs may be any that keep to these rules, and one draw needn't show every extreme that they name: `lengths`: every request has one to 2048 positions except one request that has exactly 4096. `block_table`: entry [r, g, p] is the global slot (device index along attn times 36 plus local slot) holding page p of request r and key-value head g when p * 128 < lengths[r], and -1 otherwise; no slot is named twice. The slots of one request, all key-value heads together, are consecutive modulo 576: head by head, pages in order.
All inputs are finite; a program needn't handle non-finite values.
Results may differ from a plain program's by a relative error of at most 0.0055.
The roundings to bfloat16 on the way count: a program that leaves them out, or rounds other values in their place, can miss the bound.
Values may be sent and summed in bfloat16 or wider, within the bound.
No kernel may reach another device: no remote copies, remote signals or barrier semaphores. Data moves between devices by JAX's collectives and lax.ppermute only.
A program may use at most 128 MiB of HBM per device.

v0:
```python
import math

import jax
import jax.numpy as jnp
from jax import lax
from jax.sharding import PartitionSpec as P

HD = 128
H = 64
KVH = 4


lowest = -1e30
rope_base = 500000.0


def normalize(states, norm_gain):
    values = states.astype(jnp.float32)
    square_mean = jnp.mean(values * values, axis=-1, keepdims=True)
    return (values * lax.rsqrt(square_mean + 1e-05) * norm_gain).astype(jnp.bfloat16)


def rotate(vectors, position):
    half_size = vectors.shape[-1] // 2
    freqs = jnp.exp(
        jnp.arange(half_size, dtype=jnp.float32) * (-2.0 * math.log(rope_base) / vectors.shape[-1])
    )
    angles = position[:, None, None] * freqs[None, None, :]
    cosine = jnp.cos(angles)
    sine = jnp.sin(angles)
    first = vectors[..., :half_size]
    second = vectors[..., half_size:]
    return jnp.concatenate(
        [first * cosine - second * sine, second * cosine + first * sine], axis=-1
    )


def local(hidden_states, norm_gain, w_query, w_kv, w_out, k_cache, v_cache, block_table, lengths):
    device = lax.axis_index("attn")
    requests = hidden_states.shape[0]
    head_count = w_query.shape[1] // HD
    group_heads = H // KVH
    slot_count = k_cache.shape[0]
    page_size = k_cache.shape[1]
    page_count = block_table.shape[2]
    score_scale = 1.0 / math.sqrt(HD)
    gathered = lax.all_gather(hidden_states, "attn", axis=1, tiled=True)
    normed = normalize(gathered, norm_gain)
    row_count = w_kv.shape[0]
    own_rows = lax.dynamic_slice_in_dim(normed, device * row_count, row_count, 1)
    key_value = lax.psum(jnp.dot(own_rows, w_kv, preferred_element_type=jnp.float32), "attn")
    position = (lengths - 1).astype(jnp.float32)
    new_keys = rotate(key_value[:, : KVH * HD].reshape(requests, KVH, HD), position).astype(
        jnp.bfloat16
    )
    new_values = key_value[:, KVH * HD :].reshape(requests, KVH, HD).astype(jnp.bfloat16)
    new_entries = jnp.concatenate(
        [new_keys.reshape(requests, KVH * HD), new_values.reshape(requests, KVH * HD)], axis=1
    )
    my_queries = rotate(
        jnp.dot(normed, w_query, preferred_element_type=jnp.float32).reshape(
            requests, head_count, HD
        ),
        position,
    ).astype(jnp.bfloat16)
    all_queries = lax.all_gather(
        my_queries.reshape(requests, head_count * HD), "attn", axis=1, tiled=True
    )
    slot_ids = device * slot_count + jnp.arange(slot_count, dtype=jnp.int32)
    flat_table = block_table.reshape(-1)
    matches = flat_table[None, :] == slot_ids[:, None]
    in_use = jnp.any(matches, axis=1)
    entry = jnp.sum(
        jnp.where(matches, jnp.arange(flat_table.shape[0], dtype=jnp.int32)[None, :], 0), axis=1
    )
    request_of = entry // (KVH * page_count)
    group_of = entry // page_count % KVH
    page_of = entry % page_count
    grouped_queries = all_queries.reshape(requests, KVH, group_heads, HD)[request_of, group_of]
    scores = (
        jnp.einsum("sjd,std->sjt", grouped_queries, k_cache, preferred_element_type=jnp.float32)
        * score_scale
    )
    places = page_of[:, None] * page_size + jnp.arange(page_size, dtype=jnp.int32)[None, :]
    live = in_use[:, None] & (places < (lengths[request_of] - 1)[:, None])
    slot_peak = jnp.max(jnp.where(live[:, None, :], scores, lowest), axis=-1)
    weights = jnp.where(live[:, None, :], jnp.exp(scores - slot_peak[..., None]), 0.0)
    slot_total = jnp.sum(weights, axis=-1)
    slot_out = jnp.einsum(
        "sjt,std->sjd", weights.astype(jnp.bfloat16), v_cache, preferred_element_type=jnp.float32
    )
    pair_of = request_of * KVH + group_of
    belongs = (jnp.arange(requests * KVH, dtype=jnp.int32)[:, None] == pair_of[None, :]) & in_use[
        None, :
    ]
    pair_peak = jnp.max(jnp.where(belongs[:, :, None], slot_peak[None, :, :], lowest), axis=1)
    slot_weight = jnp.exp(slot_peak - pair_peak[pair_of])
    belong_float = belongs.astype(jnp.float32)
    pair_total = jnp.einsum(
        "ks,sj->kj", belong_float, slot_total * slot_weight, precision=lax.Precision.HIGHEST
    )
    pair_out = jnp.einsum(
        "ks,sjd->kjd",
        belong_float,
        slot_out * slot_weight[..., None],
        precision=lax.Precision.HIGHEST,
    )
    peaks_dev = pair_peak.reshape(requests, H)
    totals_dev = pair_total.reshape(requests, H)
    partial_dev = pair_out.reshape(requests, H, HD)
    head_start = device * head_count
    my_groups = (head_start + jnp.arange(head_count, dtype=jnp.int32)) // group_heads
    my_keys = new_keys[:, my_groups]
    my_values = new_values[:, my_groups].astype(jnp.float32)
    new_score = (
        jnp.einsum("rhd,rhd->rh", my_queries, my_keys, preferred_element_type=jnp.float32)
        * score_scale
    )
    parts_out, parts_peak, parts_total = (
        lax.all_to_all(partial_dev[None], "attn", split_axis=2, concat_axis=0, tiled=True),
        lax.all_to_all(peaks_dev[None], "attn", split_axis=2, concat_axis=0, tiled=True),
        lax.all_to_all(totals_dev[None], "attn", split_axis=2, concat_axis=0, tiled=True),
    )
    top = jnp.maximum(jnp.max(parts_peak, axis=0), new_score)
    part_weight = jnp.exp(parts_peak - top[None])
    new_weight = jnp.exp(new_score - top)
    total = jnp.sum(parts_total * part_weight, axis=0) + new_weight
    mixed = jnp.sum(parts_out * part_weight[..., None], axis=0) + new_weight[..., None] * my_values
    attention = (mixed / total[..., None]).astype(jnp.bfloat16).reshape(requests, head_count * HD)
    terms = jnp.dot(attention, w_out, preferred_element_type=jnp.float32)
    attn_out = lax.psum_scatter(terms, "attn", scatter_dimension=1, tiled=True).astype(jnp.bfloat16)
    return (attn_out, new_entries)


def solution(mesh):
    in_specs = (
        P("groups", "attn"),
        P(),
        P(None, "attn"),
        P("attn", None),
        P("attn", None),
        P(("groups", "attn"), None, None),
        P(("groups", "attn"), None, None),
        P("groups", None, None),
        P("groups"),
    )
    out_specs = (P("groups", "attn"), P("groups", None))
    return jax.shard_map(local, mesh=mesh, in_specs=in_specs, out_specs=out_specs, check_vma=False)
```

profile of v0, /device:TPU:0, one launch (start us, length us, event | category | flops | bytes accessed | tf_op | source)
XLA Modules:
  0.0 230.1 jit_solution(1607268082411404580)
XLA Ops:
  7.2 0.9 eq.36
  8.6 0.7 add_convert_fusion
  9.3 1.4 gather_fusion
  10.7 24.1 %all_gather.6 = bf16[8,16384]{1,0:T(8,128)(2,1)S(1)} all-gather(bf16[8,1024]{1,0:T(8,128)(2,1)} %param.9), channel_id=1, replica_groups=mesh['groups'=2,'attn'=16] {'attn'}, dimensions={1}, use_global_device_ids=true | all-gather | bytes 278528 | tf_op jit(solution)/shard_map/all_gather | solution.py:47
  35.0 1.0 fusion.2
  36.0 8.0 %convolution_bitcast_fusion = f32[8,4,128]{2,0,1:T(8,128)S(1)} fusion(bf16[8,16384]{1,0:T(8,128)(2,1)S(1)} %fusion.2, bf16[16384,512]{1,0:T(8,128)(2,1)} %param.11), kind=kOutput, calls=%fused_computation.7 | convolution fusion | flops 134217728 | bytes 17055744 | tf_op jit(solution)/shard_map/dot_general | solution.py:61
  44.4 57.8 %psum.7 = f32[8,1024]{1,0:T(8,128)S(1)} all-reduce(f32[8,1024]{1,0:T(8,128)S(1)} %fusion.20), channel_id=1, replica_groups=mesh['groups'=2,'attn'=16] {'attn'}, use_global_device_ids=true, to_apply=%region_6.7 | all-reduce | flops 8192 | bytes 65536 | tf_op jit(solution)/shard_map/psum | solution.py:51
  103.3 17.5 %all_gather.7 = bf16[8,8192]{1,0:T(8,128)(2,1)S(1)} all-gather(bf16[8,512]{1,0:T(8,128)(2,1)S(1)} %bitcast.98), channel_id=1, replica_groups=mesh['groups'=2,'attn'=16] {'attn'}, dimensions={1}, use_global_device_ids=true | all-gather | bytes 139264 | tf_op jit(solution)/shard_map/all_gather | solution.py:66
  120.9 0.9 gather_fusion.1
  121.7 2.1 select_reduce_fusion
  124.1 0.7 copy.42
  124.8 3.5 %all-to-all-start.1 = ((f32[1,8,64]{1,0,2:T(1,128)}), f32[1,8,64]{1,0,2:T(1,128)S(1)}, u32[]{:S(2)}, u32[]{:S(2)}) async-start(f32[1,8,64]{1,0,2:T(1,128)} %copy.42), calls=%async_computation.1 | async-start | bytes 65536 | tf_op jit(solution)/shard_map/all_to_all | solution.py:121
  129.2 1.7 convolution_multiply_fusion
  131.5 0.7 copy.46
  132.2 2.7 %all-to-all-done.1 = f32[1,8,64]{1,0,2:T(1,128)S(1)} async-done(((f32[1,8,64]{1,0,2:T(1,128)}), f32[1,8,64]{1,0,2:T(1,128)S(1)}, u32[]{:S(2)}, u32[]{:S(2)}) %all-to-all-start.1) | async-done | bytes 2080 | tf_op jit(solution)/shard_map/all_to_all | solution.py:121
  134.9 3.5 %all-to-all-start.2 = ((f32[1,8,64]{1,0,2:T(1,128)}), f32[1,8,64]{1,0,2:T(1,128)S(1)}, u32[]{:S(2)}, u32[]{:S(2)}) async-start(f32[1,8,64]{1,0,2:T(1,128)} %copy.46), calls=%async_computation.2 | async-start | bytes 65536 | tf_op jit(solution)/shard_map/all_to_all | solution.py:122
  139.1 0.8 copy.40
  140.0 5.0 %all-to-all-done.2 = f32[1,8,64]{1,0,2:T(1,128)S(1)} async-done(((f32[1,8,64]{1,0,2:T(1,128)}), f32[1,8,64]{1,0,2:T(1,128)S(1)}, u32[]{:S(2)}, u32[]{:S(2)}) %all-to-all-start.2) | async-done | bytes 2080 | tf_op jit(solution)/shard_map/all_to_all | solution.py:122
  145.0 3.5 %all-to-all-start = ((f32[1,8,64,128]{3,1,0,2:T(8,128)}), f32[1,8,64,128]{3,1,0,2:T(8,128)S(1)}, u32[]{:S(2)}, u32[]{:S(2)}) async-start(f32[1,8,64,128]{3,1,0,2:T(8,128)} %copy.40), calls=%async_computation | async-start | bytes 524288 | tf_op jit(solution)/shard_map/all_to_all | solution.py:120
  148.8 9.7 %all-to-all-done = f32[1,8,64,128]{3,1,0,2:T(8,128)S(1)} async-done(((f32[1,8,64,128]{3,1,0,2:T(8,128)}), f32[1,8,64,128]{3,1,0,2:T(8,128)S(1)}, u32[]{:S(2)}, u32[]{:S(2)}) %all-to-all-start) | async-done | bytes 262176 | tf_op jit(solution)/shard_map/all_to_all | solution.py:120
  158.8 8.9 %fusion.24 = f32[8,16384]{1,0:T(8,128)} fusion(bf16[512,16384]{1,0:T(8,128)(2,1)} %param.13, f32[8,4,128]{2,1,0:T(4,128)S(1)} %fusion.5, bf16[4,8,128]{2,1,0:T(8,128)(2,1)S(1)} %gather_fusion.4, f32[8,4]{0,1:T(4,128)S(1)} %get-tuple-element.2, f32[8,4]{0,1:T(4,128)S(1)} %get-tuple-element.3), kind=kOutput, calls=%fused_computation.55 | convolution fusion | flops 134238208 | bytes 17326336 | tf_op jit(solution)/shard_map/dot_general | solution.py:130
  167.8 0.6 pad_maximum_fusion
  168.4 53.5 %reduce-scatter.2.cloned.1.call-done = f32[8,1024]{1,0:T(8,128)} async-done(((f32[8,16384]{1,0:T(8,128)}), f32[8,1024]{1,0:T(8,128)}) %reduce-scatter.2.cloned.1.call-update) | async-done | bytes 32784 | tf_op jit(solution)/shard_map/reduce_scatter | solution.py:131
  221.9 1.4 convert_element_type.54
  (46 shorter events, 5.3 us)
Async XLA Ops:
  7.2 36.9 %copy-start = (bf16[1024,1024]{1,0:T(8,128)(2,1)S(1)}, bf16[1024,1024]{1,0:T(8,128)(2,1)}, u32[]{:S(2)}) copy-start(bf16[1024,1024]{1,0:T(8,128)(2,1)} %param.12) | copy-start | bytes 6291460
  124.8 10.1 %all-to-all-start.1 = ((f32[1,8,64]{1,0,2:T(1,128)}), f32[1,8,64]{1,0,2:T(1,128)S(1)}, u32[]{:S(2)}, u32[]{:S(2)}) async-start(f32[1,8,64]{1,0,2:T(1,128)} %copy.42), calls=%async_computation.1 | async-start | bytes 65536 | tf_op jit(solution)/shard_map/all_to_all | solution.py:121
  134.9 10.1 %all-to-all-start.2 = ((f32[1,8,64]{1,0,2:T(1,128)}), f32[1,8,64]{1,0,2:T(1,128)S(1)}, u32[]{:S(2)}, u32[]{:S(2)}) async-start(f32[1,8,64]{1,0,2:T(1,128)} %copy.46), calls=%async_computation.2 | async-start | bytes 65536 | tf_op jit(solution)/shard_map/all_to_all | solution.py:122
  145.0 13.5 %all-to-all-start = ((f32[1,8,64,128]{3,1,0,2:T(8,128)}), f32[1,8,64,128]{3,1,0,2:T(8,128)S(1)}, u32[]{:S(2)}, u32[]{:S(2)}) async-start(f32[1,8,64,128]{3,1,0,2:T(8,128)} %copy.40), calls=%async_computation | async-start | bytes 524288 | tf_op jit(solution)/shard_map/all_to_all | solution.py:120
  148.5 73.4 %reduce-scatter.2.cloned.1.call-start = ((), (), s32[]{:S(2)}) async-start(), calls=%async_computation.4 | async-start | bytes 557056 | tf_op jit(solution)/shard_map/reduce_scatter | solution.py:131
Sparse Core Ops, SparseCore 0:
  167.8 54.0 reduce-scatter.1
where the time goes:
time: 231 us; the launch traced here: 230 us
  blocking collectives  99.3 us (43%)
  waiting for transfers between devices  71 us (31%)
  matrix products  21.6 us (9%)
  between operations  14.2 us (6%)
  starting transfers between devices  10.5 us (5%)
  local copies, waits for them, and re-layouts  7.77 us (3%)
  other arithmetic  5.66 us (2%)
    psum x1, blocking collectives, local(): lax.psum(jnp.dot(own_rows, w_kv, preferred_element_type=jnp.float32), 'at...  57.8 us
    reduce_scatter x1, waiting for transfers between devices, local(): lax.psum_scatter(terms, 'attn', scatter_dimension=1, tiled=True)  53.5 us
    all_gather x1, blocking collectives, local(): gathered = lax.all_gather(hidden_states, 'attn', axis=1, tiled=True)  24.1 us
    all_gather x1, blocking collectives, local(): lax.all_gather(my_queries.reshape(requests, head_count * HD), 'attn', axi...  17.5 us
    all_to_all x1, waiting for transfers between devices, local(): lax.all_to_all(partial_dev[None], 'attn', split_axis=2, concat_axis=0, ti...  9.72 us
    dot_general x1, matrix products, local(): terms = jnp.dot(attention, w_out, preferred_element_type=jnp.float32)  8.88 us
    dot_general x1, matrix products, local(): jnp.dot(normed, w_query, preferred_element_type=jnp.float32)  8.03 us
    all_to_all x1, waiting for transfers between devices, local(): lax.all_to_all(totals_dev[None], 'attn', split_axis=2, concat_axis=0, til...  4.98 us
  transfers between devices with their start and end apart: 4, of which 4 were waited for; matrix products, arithmetic and copies ran while one was open for 3% of the time, Pallas kernels for 0%

commit v1 on v0

v1 whole, which is shorter than its diff:
```python
import math

import jax
import jax.numpy as jnp
from jax import lax
from jax.sharding import PartitionSpec as P

HD = 128
H = 64
KVH = 4
GH = H // KVH

lowest = -1e30
rope_base = 500000.0
score_scale = 1.0 / math.sqrt(HD)
bf16 = jnp.bfloat16
f32 = jnp.float32


def rope_tables(position):
    half = HD // 2
    freqs = jnp.exp(jnp.arange(half, dtype=f32) * (-2.0 * math.log(rope_base) / HD))
    angles = position[:, None] * freqs[None, :]
    cosine, sine = jnp.cos(angles), jnp.sin(angles)
    return jnp.concatenate([cosine, cosine], 1), jnp.concatenate([-sine, sine], 1)


def rotate(vectors, cosine, sine):
    return vectors * cosine + jnp.roll(vectors, HD // 2, axis=-1) * sine


def pieces(value, count):
    out = []
    for _ in range(count):
        piece = lax.reduce_precision(value, 8, 7)
        out.append(piece.astype(bf16))
        value = value - piece
    return out


def exchange(buffer):
    return lax.all_to_all(buffer, "attn", 0, 0, tiled=True)


def local(hidden, gain, w_query, w_kv, w_out, k_cache, v_cache, block_table, lengths):
    device = lax.axis_index("attn")
    n = lax.axis_size("attn")
    requests, width = hidden.shape
    columns = w_query.shape[1]
    heads = columns // HD
    slots, page = k_cache.shape[:2]
    pages = block_table.shape[2]
    pairs = requests * KVH
    assert 2 * requests == n

    hs = exchange(jnp.broadcast_to(hidden[None], (n, requests, width)))
    values = hs.astype(f32)
    square = jnp.sum(values * values, axis=(0, 2)) / (n * width)
    scale = lax.rsqrt(square + 1e-05)
    normed = (values * scale[None, :, None] * gain.reshape(n, 1, width)).astype(bf16)
    own = lax.dynamic_index_in_dim(normed, device, 0, keepdims=False)
    normed = normed.transpose(1, 0, 2).reshape(requests, n * width)

    kv = jnp.dot(own, w_kv, preferred_element_type=f32)
    position = (lengths - 1).astype(f32)
    cosine, sine = rope_tables(position)
    query = jnp.dot(normed, w_query, preferred_element_type=f32).reshape(requests, heads, HD)
    query = rotate(query, cosine[:, None], sine[:, None]).astype(bf16)
    flat_query = query.reshape(requests, columns)

    kv_rows = kv.reshape(n, KVH, HD)
    kv_block = jnp.concatenate(pieces(kv_rows, 2), axis=1)
    kv_block = jnp.pad(kv_block, ((0, 0), (0, requests - 2 * KVH), (0, 0)))
    send = jnp.concatenate(
        [jnp.broadcast_to(flat_query[None], (n, requests, columns)), kv_block], axis=2
    )
    got = exchange(send)

    kv_sum = jnp.sum(got[:, : 2 * KVH, columns:].astype(f32), axis=0)
    kv_sum = kv_sum[:KVH] + kv_sum[KVH:]
    own_request = device // 2
    turned = rotate(kv_sum, cosine[own_request][None], sine[own_request][None])
    kv_row = jnp.where(device % 2 == 0, turned, kv_sum).astype(bf16)

    queries = got[:, :, :columns].reshape(n, requests, heads, HD).transpose(1, 0, 2, 3)
    queries = queries.reshape(pairs, GH, HD)
    slot_ids = device * slots + jnp.arange(slots, dtype=jnp.int32)
    matches = block_table.reshape(-1)[None, :] == slot_ids[:, None]
    in_use = jnp.any(matches, axis=1)
    entry = jnp.sum(
        jnp.where(matches, jnp.arange(matches.shape[1], dtype=jnp.int32)[None, :], 0), axis=1
    )
    pair_of = entry // pages
    live_count = jnp.where(
        in_use, jnp.repeat(lengths, KVH)[pair_of] - 1 - (entry % pages) * page, 0
    )
    scores = (
        jnp.einsum("sjd,std->sjt", queries[pair_of], k_cache, preferred_element_type=f32)
        * score_scale
    )
    live = (jnp.arange(page, dtype=jnp.int32)[None, :] < live_count[:, None])[:, None, :]
    peak = jnp.max(jnp.where(live, scores, lowest), axis=-1)
    weights = jnp.where(live, jnp.exp(scores - peak[..., None]), 0.0)
    total = jnp.sum(weights, axis=-1)
    out = jnp.einsum("sjt,std->sjd", weights.astype(bf16), v_cache, preferred_element_type=f32)
    belongs = (jnp.arange(pairs, dtype=jnp.int32)[:, None] == pair_of[None, :]) & in_use[None, :]
    pair_peak = jnp.max(jnp.where(belongs[:, :, None], peak[None], lowest), axis=1)
    factor = jnp.exp(peak - pair_peak[pair_of])
    belongs = belongs.astype(f32)
    highest = lax.Precision.HIGHEST
    pair_total = jnp.einsum("ks,sj->kj", belongs, total * factor, precision=highest)
    pair_out = jnp.einsum("ks,sjd->kjd", belongs, out * factor[..., None], precision=highest)

    def by_head(array):
        return array.reshape((requests, n, heads) + array.shape[2:]).swapaxes(0, 1)

    stats = jnp.concatenate(
        pieces(by_head(pair_peak), 3) + pieces(by_head(pair_total), 3), axis=2
    )
    stats = jnp.pad(stats, ((0, 0), (0, 0), (0, HD // 2 - 6 * heads)))
    kv_lanes = jnp.concatenate([kv_row[:, : HD // 2], kv_row[:, HD // 2 :]], axis=0)
    kv_lanes = jnp.pad(kv_lanes, ((0, requests - 2 * KVH), (0, 0)))
    send = jnp.concatenate(
        [
            by_head(pair_out).astype(bf16).reshape(n, requests, columns),
            stats,
            jnp.broadcast_to(kv_lanes[None], (n,) + kv_lanes.shape),
        ],
        axis=2,
    )
    got = exchange(send)

    kv_lanes = got[:, : 2 * KVH, columns + HD // 2 :].reshape(requests, 2, 2, KVH, HD // 2)
    entries = kv_lanes.transpose(0, 1, 3, 2, 4).reshape(requests, 2, KVH, HD)
    new_entries = entries.reshape(requests, 2 * KVH * HD)
    group_of = (device * heads + jnp.arange(heads, dtype=jnp.int32)) // GH
    own_keys, own_values = entries[:, 0][:, group_of], entries[:, 1][:, group_of].astype(f32)
    new_score = jnp.sum(query.astype(f32) * own_keys.astype(f32), axis=-1) * score_scale
    parts_out = got[:, :, :columns].reshape(n, requests, heads, HD).astype(f32)
    parts = got[:, :, columns : columns + 6 * heads].reshape(n, requests, 6, heads).astype(f32)
    parts_peak = parts[:, :, 0] + parts[:, :, 1] + parts[:, :, 2]
    parts_total = parts[:, :, 3] + parts[:, :, 4] + parts[:, :, 5]
    top = jnp.maximum(jnp.max(parts_peak, axis=0), new_score)
    part_weight = jnp.exp(parts_peak - top[None])
    new_weight = jnp.exp(new_score - top)
    total = jnp.sum(parts_total * part_weight, axis=0) + new_weight
    mixed = jnp.sum(parts_out * part_weight[..., None], axis=0) + new_weight[..., None] * own_values
    attention = (mixed / total[..., None]).astype(bf16).reshape(requests, columns)
    terms = jnp.dot(attention, w_out, preferred_element_type=f32).astype(bf16)
    got = exchange(terms.reshape(requests, n, width).swapaxes(0, 1))
    attn_out = jnp.sum(got.astype(f32), axis=0).astype(bf16)
    return attn_out, new_entries


def solution(mesh):
    in_specs = (
        P("groups", "attn"),
        P(),
        P(None, "attn"),
        P("attn", None),
        P("attn", None),
        P(("groups", "attn"), None, None),
        P(("groups", "attn"), None, None),
        P("groups", None, None),
        P("groups"),
    )
    out_specs = (P("groups", "attn"), P("groups", None))
    return jax.shard_map(local, mesh=mesh, in_specs=in_specs, out_specs=out_specs, check_vma=False)
```

time: 231 us -> 104 us (0.45)
  blocking collectives: 99.3 us -> 11.1 us
  waiting for transfers between devices: 71 us -> 17.6 us
  local copies, waits for them, and re-layouts: 7.77 us -> 30.3 us
  between operations: 14.2 us -> 0.98 us
  starting transfers between devices: 10.5 us -> 16.9 us
    psum x1 -> x0, blocking collectives: 57.8 us -> none  [local(): lax.psum(jnp.dot(own_rows, w_kv, preferred_element_type=jnp.float32), 'at...]
    reduce_scatter x1 -> x0, waiting for transfers between devices: 53.5 us -> none  [local(): lax.psum_scatter(terms, 'attn', scatter_dimension=1, tiled=True)]
    all_gather x2 -> x0, blocking collectives: 41.5 us -> none  [the longest x1 24.1 us: local(): gathered = lax.all_gather(hidden_states, 'attn', axis=1, tiled=True)]
    dot_general x1, local copies, waits for them, and re-layouts: 0.16 us -> 21.3 us  [local(): jnp.dot(normed, w_query, preferred_element_type=f32)]
    all_to_all x0 -> x1, blocking collectives: none -> 11.1 us  [exchange(): return lax.all_to_all(buffer, 'attn', 0, 0, tiled=True)]
    all_to_all x3, starting transfers between devices: 10.5 us -> 16.9 us  [exchange(): return lax.all_to_all(buffer, 'attn', 0, 0, tiled=True)]
  transfers between devices with their start and end apart: 4 -> 3, of which waited for: 4 -> 2; matrix products, arithmetic and copies ran while one was open for 3% -> 25% of each run, Pallas kernels for 0% -> 0%
where the time goes in v1:
time: 104 us; the launch traced here: 103 us
  local copies, waits for them, and re-layouts  30.3 us (29%)
  matrix products  21.5 us (21%)
  waiting for transfers between devices  17.6 us (17%)
  starting transfers between devices  16.9 us (16%)
  blocking collectives  11.1 us (11%)
  other arithmetic  4.54 us (4%)
    dot_general x1, local copies, waits for them, and re-layouts, local(): jnp.dot(normed, w_query, preferred_element_type=f32)  21.3 us
    all_to_all x3, waiting for transfers between devices, exchange(): return lax.all_to_all(buffer, 'attn', 0, 0, tiled=True)  17.6 us
    all_to_all x3, starting transfers between devices, exchange(): return lax.all_to_all(buffer, 'attn', 0, 0, tiled=True)  16.9 us
    all_to_all x1, blocking collectives, exchange(): return lax.all_to_all(buffer, 'attn', 0, 0, tiled=True)  11.1 us
    dot_general x1, matrix products, local(): terms = jnp.dot(attention, w_out, preferred_element_type=f32).astype(bf16)  8.78 us
    dot_general x1, matrix products, local(): jnp.dot(normed, w_query, preferred_element_type=f32)  8.04 us
  transfers between devices with their start and end apart: 3, of which 2 were waited for; matrix products, arithmetic and copies ran while one was open for 25% of the time, Pallas kernels for 0%

profile of v1, /device:TPU:0, one launch (start us, length us, event | category | flops | bytes accessed | tf_op | source)
XLA Modules:
  0.0 103.0 jit_solution(8200241005375441683)
XLA Ops:
  0.6 1.6 %broadcast_in_dim.66 = bf16[16,8,1024]{2,1,0:T(8,128)(2,1)} broadcast(bf16[8,1024]{1,0:T(8,128)(2,1)} %param.9), dimensions={1,2} | broadcast | bytes 278528 | tf_op jit(solution)/shard_map/broadcast_in_dim | solution.py:56
  2.2 7.4 %all-to-all-start = ((bf16[16,8,1024]{2,1,0:T(8,128)(2,1)}), bf16[16,8,1024]{2,1,0:T(8,128)(2,1)S(1)}, u32[]{:S(2)}, u32[]{:S(2)}) async-start(bf16[16,8,1024]{2,1,0:T(8,128)(2,1)} %broadcast_in_dim.66), calls=%async_computation | async-start | bytes 524288 | tf_op jit(solution)/shard_map/all_to_all | solution.py:42
  9.7 0.8 eq.40
  10.8 0.7 add_convert_fusion
  11.8 0.9 mul.165
  12.6 21.3 %copy.96 = bf16[512,16384]{1,0:T(8,128)(2,1)} copy(bf16[512,16384]{0,1:T(8,128)(2,1)} %bitcast.120) | data formatting | bytes 33554432 | tf_op jit(solution)/shard_map/dot_general | solution.py:67
  34.1 0.8 gather_fusion
  35.3 8.0 %fusion.59 = f32[8,4,128]{2,0,1:T(8,128)S(1)} fusion(bf16[8,16384,1]{1,0,2:T(8,128)(2,1)S(1)} %bitcast.121, bf16[4,128,16384]{2,1,0:T(8,128)(2,1)} %bitcast.119), kind=kOutput, calls=%fused_computation.140 | convolution fusion | flops 134217728 | bytes 17055744 | tf_op jit(solution)/shard_map/dot_general | solution.py:67
  43.5 0.4 fusion.33
  44.0 0.7 maximum_maximum_fusion
  44.7 6.0 %all-to-all-start.1 = ((bf16[16,8,640]{2,1,0:T(8,128)(2,1)}), bf16[16,8,640]{2,1,0:T(8,128)(2,1)S(1)}, u32[]{:S(2)}, u32[]{:S(2)}) async-start(bf16[16,8,640]{2,1,0:T(8,128)(2,1)} %maximum_maximum_fusion), calls=%async_computation.1 | async-start | bytes 327680 | tf_op jit(solution)/shard_map/all_to_all | solution.py:42
  50.8 8.4 %all-to-all-done.1 = bf16[16,8,640]{2,1,0:T(8,128)(2,1)S(1)} async-done(((bf16[16,8,640]{2,1,0:T(8,128)(2,1)}), bf16[16,8,640]{2,1,0:T(8,128)(2,1)S(1)}, u32[]{:S(2)}, u32[]{:S(2)}) %all-to-all-start.1) | async-done | bytes 163872 | tf_op jit(solution)/shard_map/all_to_all | solution.py:42
  59.2 0.6 gather_fusion.1
  59.8 2.1 %select_reduce_fusion = (f32[36,16]{1,0:T(8,128)S(1)}, f32[36,16,128]{2,1,0:T(8,128)S(1)}) fusion(pred[36,128]{1,0:T(8,128)(4,1)S(1)} %iota_compare_fusion.2, bf16[36,16,128]{2,1,0:T(8,128)(2,1)S(1)} %gather_fusion.1, bf16[36,128,128]{2,1,0:T(8,128)(2,1)} %param.14), kind=kOutput, calls=%fused_computation.20 | convolution fusion | flops 19094976 | bytes 1628928 | tf_op jit(solution)/shard_map/sjd,std->sjt/dot_general | solution.py:98
  62.1 0.6 gather_fusion.2
  63.1 1.7 %convolution_multiply_fusion = f32[36,16,128]{2,1,0:T(8,128)S(1)} fusion(bf16[36,128,128]{2,1,0:T(8,128)(2,1)} %param.15, f32[36,16,128]{2,1,0:T(8,128)S(1)} %get-tuple-element.22, f32[36,16]{1,0:T(8,128)S(1)} %subtract_exponential_fusion, f32[36,16]{1,0:T(8,128)S(1)} %get-tuple-element.21, pred[36,128]{1,0:T(8,128)(4,1)S(1)} %iota_compare_fusion.2), kind=kOutput, calls=%fused_computation.6 | convolution fusion | flops 19169280 | bytes 1778688 | tf_op jit(solution)/shard_map/sjt,std->sjd/dot_general | solution.py:105
  66.5 11.1 %all_to_all.20 = bf16[16,8,640]{2,1,0:T(8,128)(2,1)S(1)} all-to-all(bf16[16,8,640]{2,1,0:T(8,128)(2,1)S(1)} %fusion.12), channel_id=1, replica_groups=mesh['groups'=2,'attn'=16] {'attn'}, dimensions={0} | all-to-all | bytes 327680 | tf_op jit(solution)/shard_map/all_to_all | solution.py:42
  77.8 0.6 gather_fusion.3
  78.8 0.6 gather_fusion.4
  80.0 8.8 %convolution_convert_fusion = bf16[8,16384]{1,0:T(8,128)(2,1)} fusion(bf16[8,512]{0,1:T(8,128)(2,1)S(1)} %fusion.6, bf16[512,16384]{1,0:T(8,128)(2,1)} %param.13), kind=kOutput, calls=%fused_computation.5 | convolution fusion | flops 134348800 | bytes 17047552 | tf_op jit(solution)/shard_map/dot_general | solution.py:149
  88.8 3.5 %all-to-all-start.3 = ((bf16[16,8,1024]{2,1,0:T(8,128)(2,1)}), bf16[16,8,1024]{2,1,0:T(8,128)(2,1)S(1)}, u32[]{:S(2)}, u32[]{:S(2)}) async-start(bf16[16,8,1024]{2,1,0:T(8,128)(2,1)} %bitcast.34), calls=%async_computation.3 | async-start | bytes 524288 | tf_op jit(solution)/shard_map/all_to_all | solution.py:42
  92.4 0.7 reshape_reshape.3
  93.1 9.3 %all-to-all-done.3 = bf16[16,8,1024]{2,1,0:T(8,128)(2,1)S(1)} async-done(((bf16[16,8,1024]{2,1,0:T(8,128)(2,1)}), bf16[16,8,1024]{2,1,0:T(8,128)(2,1)S(1)}, u32[]{:S(2)}, u32[]{:S(2)}) %all-to-all-start.3) | async-done | bytes 262176 | tf_op jit(solution)/shard_map/all_to_all | solution.py:42
  102.3 0.6 reduce_sum.85
  (78 shorter events, 5.0 us)
Async XLA Ops:
  0.6 42.8 %copy-start = (bf16[1024,1024]{1,0:T(8,128)(2,1)S(1)}, bf16[1024,1024]{1,0:T(8,128)(2,1)}, u32[]{:S(2)}) copy-start(bf16[1024,1024]{1,0:T(8,128)(2,1)} %param.12) | copy-start | bytes 6291460
  2.2 32.7 %all-to-all-start = ((bf16[16,8,1024]{2,1,0:T(8,128)(2,1)}), bf16[16,8,1024]{2,1,0:T(8,128)(2,1)S(1)}, u32[]{:S(2)}, u32[]{:S(2)}) async-start(bf16[16,8,1024]{2,1,0:T(8,128)(2,1)} %broadcast_in_dim.66), calls=%async_computation | async-start | bytes 524288 | tf_op jit(solution)/shard_map/all_to_all | solution.py:42
  12.6 21.3 %copy-start.1 = (s32[8]{0:T(128)S(1)}, s32[8]{0:T(128)}, u32[]{:S(2)}) copy-start(s32[8]{0:T(128)} %param.17) | copy-start | bytes 100
  44.7 14.5 %all-to-all-start.1 = ((bf16[16,8,640]{2,1,0:T(8,128)(2,1)}), bf16[16,8,640]{2,1,0:T(8,128)(2,1)S(1)}, u32[]{:S(2)}, u32[]{:S(2)}) async-start(bf16[16,8,640]{2,1,0:T(8,128)(2,1)} %maximum_maximum_fusion), calls=%async_computation.1 | async-start | bytes 327680 | tf_op jit(solution)/shard_map/all_to_all | solution.py:42
  88.8 13.5 %all-to-all-start.3 = ((bf16[16,8,1024]{2,1,0:T(8,128)(2,1)}), bf16[16,8,1024]{2,1,0:T(8,128)(2,1)S(1)}, u32[]{:S(2)}, u32[]{:S(2)}) async-start(bf16[16,8,1024]{2,1,0:T(8,128)(2,1)} %bitcast.34), calls=%async_computation.3 | async-start | bytes 524288 | tf_op jit(solution)/shard_map/all_to_all | solution.py:42

commit v2 on v1

v2 whole, which is shorter than its diff:
```python
import functools
import math

import jax
import jax.numpy as jnp
from jax import lax
from jax.experimental import pallas as pl
from jax.experimental.pallas import tpu as pltpu
from jax.sharding import PartitionSpec as P

HD = 128
H = 64
KVH = 4
GH = H // KVH

lowest = -1e30
rope_base = 500000.0
score_scale = 1.0 / math.sqrt(HD)
bf16 = jnp.bfloat16
f32 = jnp.float32
VMEM = pltpu.MemorySpace.VMEM
SMEM = pltpu.MemorySpace.SMEM
KV = KVH * HD
HALF = HD // 2


def pin(array):
    return pltpu.with_memory_space_constraint(array, VMEM)


def rope_tables(position):
    freqs = jnp.exp(jnp.arange(HALF, dtype=f32) * (-2.0 * math.log(rope_base) / HD))
    angles = position[:, None] * freqs[None, :]
    cosine, sine = jnp.cos(angles), jnp.sin(angles)
    return jnp.concatenate([cosine, cosine], 1), jnp.concatenate([-sine, sine], 1)


def rotate(vectors, cosine, sine):
    return vectors * cosine + pltpu.roll(vectors, HALF, 1) * sine


def pieces(value):
    out = []
    for _ in range(3):
        piece = value.astype(bf16).astype(f32)
        out.append(piece)
        value = value - piece
    return out


def exchange(buffer):
    return lax.all_to_all(buffer, "attn", 0, 0, tiled=True)


def lane_of(shape):
    return lax.broadcasted_iota(jnp.int32, shape, 1)


def project_kernel(device, hs, gain, w_query, w_kv, cosine, sine, send, query, normed, kv_rows):
    n, requests, width = hs.shape
    columns = w_query.shape[1]
    square = jnp.zeros((requests, width), f32)
    for k in range(n):
        values = hs[k].astype(f32)
        square = square + values * values
    scale = lax.rsqrt(jnp.sum(square, axis=1, keepdims=True) / (n * width) + 1e-05)
    product = jnp.zeros((requests, columns), f32)
    for k in range(n):
        part = (hs[k].astype(f32) * scale * gain[k : k + 1, :]).astype(bf16)
        normed[k] = part
        product = product + jnp.dot(
            part, w_query[k * width : (k + 1) * width, :], preferred_element_type=f32
        )
    kv = jnp.dot(normed[device[0]], w_kv[...], preferred_element_type=f32)
    for row in range(2 * KVH):
        half, group = divmod(row, KVH)
        value = kv[:, row * HD : (row + 1) * HD]
        upper = value.astype(bf16).astype(f32)
        start = half * 2 * KVH + group
        kv_rows[pl.ds(start, requests, stride=4 * KVH), :] = upper
        kv_rows[pl.ds(start + KVH, requests, stride=4 * KVH), :] = value - upper
    for c in range(columns // HD):
        turned = rotate(product[:, c * HD : (c + 1) * HD], cosine[...], sine[...])
        query[:, c * HD : (c + 1) * HD] = turned.astype(bf16)
    whole = query[...]
    for j in range(n):
        send[j, :, :columns] = whole
        rows = kv_rows[j * 2 * KVH : (j + 1) * 2 * KVH, :]
        if requests > 2 * KVH:
            rows = jnp.concatenate([rows, jnp.zeros((requests - 2 * KVH, HD), f32)], axis=0)
        send[j, :, columns:] = rows.astype(bf16)


def attend_kernel(
    pair_of, live, got, k_cache, v_cache, cosine, sine, send,
    queries, outs, slot_peak, slot_total, peak, total, mixed, kv_block,
):
    n, requests, wide = got.shape
    columns = wide - HD
    heads = columns // HD
    slots, page = k_cache.shape[:2]
    for h in range(H):
        src, c = divmod(h, heads)
        queries[pl.ds(h, requests, stride=H), :] = got[src, :, c * HD : (c + 1) * HD].astype(f32)
    peak[...] = jnp.full_like(peak, lowest)
    total[...] = jnp.zeros_like(total)
    mixed[...] = jnp.zeros_like(mixed)
    places = lane_of((GH, page))
    for s in range(slots):
        rows = pl.ds(pl.multiple_of(pair_of[s] * GH, GH), GH)
        scores = lax.dot_general(
            queries[rows, :].astype(bf16), k_cache[s], (((1,), (1,)), ((), ())),
            preferred_element_type=f32,
        )
        alive = places < live[s]
        scores = jnp.where(alive, scores * score_scale, lowest)
        top = jnp.max(scores, axis=1, keepdims=True)
        weights = jnp.where(alive, jnp.exp(scores - top), 0.0)
        slot_peak[s] = jnp.broadcast_to(top, (GH, HD))
        slot_total[s] = jnp.broadcast_to(jnp.sum(weights, axis=1, keepdims=True), (GH, HD))
        outs[s] = jnp.dot(weights.astype(bf16), v_cache[s], preferred_element_type=f32)
    for s in range(slots):
        rows = pl.ds(pl.multiple_of(pair_of[s] * GH, GH), GH)
        peak[rows, :] = jnp.maximum(peak[rows, :], slot_peak[s])
    for s in range(slots):
        rows = pl.ds(pl.multiple_of(pair_of[s] * GH, GH), GH)
        factor = jnp.exp(slot_peak[s] - peak[rows, :])
        total[rows, :] = total[rows, :] + factor * slot_total[s]
        mixed[rows, :] = mixed[rows, :] + factor * outs[s]

    kv = jnp.zeros((2 * KVH, HD), f32)
    for src in range(n):
        kv = kv + got[src, : 2 * KVH, columns:].astype(f32)
    kv = kv + pltpu.roll(kv, KVH, 0)
    kv = rotate(kv, cosine[...], sine[...])
    upper = lax.broadcasted_iota(jnp.int32, kv.shape, 0) < KVH
    kv = jnp.where(upper, pltpu.roll(kv, HALF, 1), kv)
    if requests > 2 * KVH:
        kv_block[...] = jnp.zeros_like(kv_block)
    kv_block[: 2 * KVH, :] = kv
    lanes = lane_of((requests, HD))
    for j in range(n):
        block = kv_block[...]
        for c in range(heads):
            rows = pl.ds(j * heads + c, requests, stride=H)
            send[j, :, c * HD : (c + 1) * HD] = mixed[rows, :].astype(bf16)
            for i, piece in enumerate(pieces(peak[rows, :]) + pieces(total[rows, :])):
                block = jnp.where(lanes == i * heads + c, piece, block)
        send[j, :, columns:] = block.astype(bf16)


def output_kernel(group_of, got, query, w_out, send, new_entries, entries, attention):
    n, requests, wide = got.shape
    columns = wide - HD
    heads = columns // HD
    width = send.shape[2]
    lanes = lane_of((requests, HD))
    narrow = lane_of((2 * KVH, HD)) < HALF
    for row in range(n):
        request, half = divmod(row, 2)
        block = got[row, : 2 * KVH, columns:].astype(f32)
        block = jnp.where(narrow, pltpu.roll(block, HALF, 1), pltpu.roll(block, KVH, 0))
        rows = pl.ds(half * KVH * requests + request, KVH, stride=requests)
        entries[rows, :] = block[:KVH]
    for i in range(2 * KVH):
        new_entries[:, i * HD : (i + 1) * HD] = entries[
            i * requests : (i + 1) * requests, :
        ].astype(bf16)

    def own(c, half):
        start = (group_of[c] + half * KVH) * requests
        return entries[pl.ds(pl.multiple_of(start, 8), requests), :]

    new_score = jnp.full((requests, HD), lowest, f32)
    for c in range(heads):
        score = query[:, c * HD : (c + 1) * HD].astype(f32) * own(c, 0)
        score = jnp.sum(score, axis=1, keepdims=True) * score_scale
        new_score = jnp.where(lanes == c, score, new_score)
    peaks, totals = [], []
    for src in range(n):
        stats = got[src, :, columns:].astype(f32)
        stats = (
            stats + pltpu.roll(stats, HD - heads, 1) + pltpu.roll(stats, HD - 2 * heads, 1)
        )
        peaks.append(stats)
        totals.append(pltpu.roll(stats, HD - 3 * heads, 1))
    top = new_score
    for value in peaks:
        top = jnp.maximum(top, value)
    weights = [jnp.exp(value - top) for value in peaks]
    new_weight = jnp.exp(new_score - top)
    total = new_weight
    for weight, value in zip(weights, totals):
        total = total + weight * value
    inverse = 1.0 / total
    weights = [weight * inverse for weight in weights]
    new_weight = new_weight * inverse
    for c in range(heads):
        mixed = new_weight[:, c : c + 1] * own(c, 1)
        for src in range(n):
            mixed = mixed + weights[src][:, c : c + 1] * got[
                src, :, c * HD : (c + 1) * HD
            ].astype(f32)
        attention[:, c * HD : (c + 1) * HD] = mixed.astype(bf16)
    whole = attention[...]
    for j in range(n):
        send[j] = jnp.dot(
            whole, w_out[:, j * width : (j + 1) * width], preferred_element_type=f32
        ).astype(bf16)


def call(kernel, out_shape, in_spaces, scratch, limit):
    out_count = len(out_shape)
    return pl.pallas_call(
        kernel,
        out_shape=out_shape,
        in_specs=[pl.BlockSpec(memory_space=space) for space in in_spaces],
        out_specs=[pl.BlockSpec(memory_space=VMEM)] * out_count,
        scratch_shapes=scratch,
        compiler_params=pltpu.CompilerParams(vmem_limit_bytes=limit << 20),
    )


def local(hidden, gain, w_query, w_kv, w_out, k_cache, v_cache, block_table, lengths):
    device = lax.axis_index("attn")
    n = lax.axis_size("attn")
    requests, width = hidden.shape
    columns = w_query.shape[1]
    heads = columns // HD
    slots, page = k_cache.shape[:2]
    pages = block_table.shape[2]
    pairs = requests * KVH
    assert 2 * requests == n

    hs = exchange(jnp.broadcast_to(hidden[None], (n, requests, width)))
    cosine, sine = rope_tables((lengths - 1).astype(f32))
    keys_here = device % 2 == 0
    own_cosine = jnp.where(keys_here, lax.dynamic_slice_in_dim(cosine, device // 2, 1), 1.0)
    own_sine = jnp.where(keys_here, lax.dynamic_slice_in_dim(sine, device // 2, 1), 0.0)
    slot_ids = device * slots + jnp.arange(slots, dtype=jnp.int32)
    matches = block_table.reshape(-1)[None, :] == slot_ids[:, None]
    length_of = jnp.broadcast_to(lengths[:, None, None], block_table.shape).reshape(-1)
    index = jnp.arange(pairs * pages, dtype=jnp.int32)
    live_of = length_of - 1 - index % pages * page
    live = jnp.sum(jnp.where(matches, live_of[None, :], 0), axis=1)
    pair_of = jnp.sum(jnp.where(matches, index[None, :] // pages, 0), axis=1)
    group_of = (device * heads + jnp.arange(heads, dtype=jnp.int32)) // GH

    wide = jax.ShapeDtypeStruct((n, requests, columns + HD), bf16)
    send, query = call(
        project_kernel,
        [wide, jax.ShapeDtypeStruct((requests, columns), bf16)],
        [SMEM] + [VMEM] * 6,
        [pltpu.VMEM(hs.shape, bf16), pltpu.VMEM((n * 2 * KVH, HD), f32)],
        6,
    )(device.reshape(1), hs, gain.reshape(n, width), pin(w_query), pin(w_kv), cosine, sine)
    got = exchange(send)
    stat = pltpu.VMEM((pairs * GH, HD), f32)
    slot_stat = pltpu.VMEM((slots, GH, HD), f32)
    (send,) = call(
        attend_kernel,
        [wide],
        [SMEM] * 2 + [VMEM] * 5,
        [stat] + [slot_stat] * 3 + [stat] * 3 + [pltpu.VMEM((requests, HD), f32)],
        8,
    )(pair_of, live, got, pin(k_cache), pin(v_cache), own_cosine, own_sine)
    got = exchange(send)
    send, new_entries = call(
        output_kernel,
        [
            jax.ShapeDtypeStruct((n, requests, width), bf16),
            jax.ShapeDtypeStruct((requests, 2 * KV), bf16),
        ],
        [SMEM] + [VMEM] * 3,
        [pltpu.VMEM((2 * KVH * requests, HD), f32), pltpu.VMEM((requests, columns), bf16)],
        6,
    )(group_of, got, query, pin(w_out))
    got = exchange(send)
    attn_out = jnp.sum(got.astype(f32), axis=0).astype(bf16)
    return attn_out, new_entries


def solution(mesh):
    in_specs = (
        P("groups", "attn"),
        P(),
        P(None, "attn"),
        P("attn", None),
        P("attn", None),
        P(("groups", "attn"), None, None),
        P(("groups", "attn"), None, None),
        P("groups", None, None),
        P("groups"),
    )
    out_specs = (P("groups", "attn"), P("groups", None))
    return jax.shard_map(local, mesh=mesh, in_specs=in_specs, out_specs=out_specs, check_vma=False)
```

time: 104 us -> 87.5 us (0.84)
  matrix products: 21.5 us -> 0 us
  Pallas kernels: 0 us -> 16.9 us
  local copies, waits for them, and re-layouts: 30.3 us -> 16.4 us
  waiting for transfers between devices: 17.6 us -> 23.9 us
  other arithmetic: 4.54 us -> 1.75 us
  starting transfers between devices: 16.9 us -> 14.4 us
  blocking collectives: 11.1 us -> 12.6 us
    dot_general x7 -> x0, matrix products: 21.5 us -> none  [the longest x1 8.78 us: local(): terms = jnp.dot(attention, w_out, preferred_element_type=f32).astype(bf16)]
    dot_general x1 -> x0, local copies, waits for them, and re-layouts: 21.3 us -> none  [local(): jnp.dot(normed, w_query, preferred_element_type=f32)]
    pallas_call x0 -> x3, Pallas kernels: none -> 16.9 us  [the longest x1 10.4 us: local(): call(attend_kernel, [wide], [SMEM] * 2 + [VMEM] * 5, [stat] + [slot_stat]...]
    unnamed x7 -> x10, local copies, waits for them, and re-layouts: 0.37 us -> 13.1 us
    all_to_all x3, waiting for transfers between devices: 17.6 us -> 23.9 us  [exchange(): return lax.all_to_all(buffer, 'attn', 0, 0, tiled=True)]
    gather x5 -> x0, local copies, waits for them, and re-layouts: 3.08 us -> none  [the longest x1 0.78 us: local(): jnp.repeat(lengths, KVH)[pair_of] - 1 - entry % pages * page]
    all_to_all x3, starting transfers between devices: 16.9 us -> 14.4 us  [exchange(): return lax.all_to_all(buffer, 'attn', 0, 0, tiled=True)]
    all_to_all x1, blocking collectives: 11.1 us -> 12.6 us  [exchange(): return lax.all_to_all(buffer, 'attn', 0, 0, tiled=True)]
  transfers between devices with their start and end apart: 3 -> 3, of which waited for: 2 -> 3; matrix products, arithmetic and copies ran while one was open for 25% -> 3% of each run, Pallas kernels for 0% -> 0%
where the time goes in v2:
time: 87.5 us; the launch traced here: 86.8 us
  waiting for transfers between devices  23.9 us (27%)
  Pallas kernels  16.9 us (19%)
  local copies, waits for them, and re-layouts  16.4 us (19%)
  starting transfers between devices  14.4 us (16%)
  blocking collectives  12.6 us (14%)
  other arithmetic  1.75 us (2%)
    all_to_all x3, waiting for transfers between devices, exchange(): return lax.all_to_all(buffer, 'attn', 0, 0, tiled=True)  23.9 us
    all_to_all x3, starting transfers between devices, exchange(): return lax.all_to_all(buffer, 'attn', 0, 0, tiled=True)  14.4 us
    unnamed x10, local copies, waits for them, and re-layouts  13.1 us
    all_to_all x1, blocking collectives, exchange(): return lax.all_to_all(buffer, 'attn', 0, 0, tiled=True)  12.6 us
    pallas_call x1, Pallas kernels, local(): call(attend_kernel, [wide], [SMEM] * 2 + [VMEM] * 5, [stat] + [slot_stat]...  10.4 us
    pallas_call x1, Pallas kernels, local(): call(project_kernel, [wide, jax.ShapeDtypeStruct((requests, columns), bf1...  3.3 us
    pallas_call x1, Pallas kernels, local(): call(output_kernel, [jax.ShapeDtypeStruct((n, requests, width), bf16), ja...  3.2 us
  transfers between devices with their start and end apart: 3, of which 3 were waited for; matrix products, arithmetic and copies ran while one was open for 3% of the time, Pallas kernels for 0%

profile of v2, /device:TPU:0, one launch (start us, length us, event | category | flops | bytes accessed | tf_op | source)
XLA Modules:
  0.0 86.8 jit_solution(3767730428488429713)
XLA Ops:
  0.6 1.4 %broadcast_in_dim.46 = bf16[16,8,1024]{2,1,0:T(8,128)(2,1)} broadcast(bf16[8,1024]{1,0:T(8,128)(2,1)} %param.9), dimensions={1,2} | broadcast | bytes 278528 | tf_op jit(solution)/shard_map/broadcast_in_dim | solution.py:235
  2.1 7.4 %all-to-all-start = ((bf16[16,8,1024]{2,1,0:T(8,128)(2,1)}), bf16[16,8,1024]{2,1,0:T(8,128)(2,1)S(1)}, u32[]{:S(2)}, u32[]{:S(2)}) async-start(bf16[16,8,1024]{2,1,0:T(8,128)(2,1)} %broadcast_in_dim.46), calls=%async_computation | async-start | bytes 524288 | tf_op jit(solution)/shard_map/all_to_all | solution.py:52
  9.5 0.7 fusion.12
  10.1 0.1 fusion.11
  10.3 0.9 reshape.80.gain
  11.1 0.1 broadcast_in_dim.44
  11.2 0.1 sub.32
  11.3 0.8 eq.22
  12.1 0.1 pad_maximum_fusion
  12.2 7.3 %all-to-all-done.hs = bf16[16,8,1024]{2,1,0:T(8,128)(2,1)S(1)} async-done(((bf16[16,8,1024]{2,1,0:T(8,128)(2,1)}), bf16[16,8,1024]{2,1,0:T(8,128)(2,1)S(1)}, u32[]{:S(2)}, u32[]{:S(2)}) %all-to-all-start) | async-done | bytes 262176 | tf_op jit(solution)/shard_map/all_to_all | solution.py:52
  19.5 5.8 %copy-done = bf16[16384,512]{1,0:T(8,128)(2,1)S(1)} copy-done((bf16[16384,512]{1,0:T(8,128)(2,1)S(1)}, bf16[16384,512]{1,0:T(8,128)(2,1)}, u32[]{:S(2)}) %copy-start) | copy-done | bytes 16777240
  25.3 1.6 %copy-done.2 = bf16[1024,1024]{1,0:T(8,128)(2,1)S(1)} copy-done((bf16[1024,1024]{1,0:T(8,128)(2,1)S(1)}, bf16[1024,1024]{1,0:T(8,128)(2,1)}, u32[]{:S(2)}) %copy-start.2) | copy-done | bytes 2097176
  26.9 3.3 %shard_map.104 = (bf16[16,8,640]{2,1,0:T(8,128)(2,1)}, bf16[8,512]{1,0:T(8,128)(2,1)S(1)}) custom-call(s32[1]{0:T(128)} %bitcast.device, bf16[16,8,1024]{2,1,0:T(8,128)(2,1)S(1)} %all-to-all-done.hs, f32[16,1024]{1,0:T(8,128)S(1)} %reshape.80.gain, bf16[16384,512]{1,0:T(8,128)(2,1)S(1)} %copy-done, bf16[1024,1024]{1,0:T(8,128)(2,1)S(1)} %copy-done.2, ...), custom_call_target="tpu_custom_call" | custom-call | tf_op jit(solution)/shard_map/pallas_call | solution.py:250
  30.2 3.5 %all-to-all-start.1 = ((bf16[16,8,640]{2,1,0:T(8,128)(2,1)}), bf16[16,8,640]{2,1,0:T(8,128)(2,1)S(1)}, u32[]{:S(2)}, u32[]{:S(2)}) async-start(bf16[16,8,640]{2,1,0:T(8,128)(2,1)} %get-tuple-element.6), calls=%async_computation.1 | async-start | bytes 327680 | tf_op jit(solution)/shard_map/all_to_all | solution.py:52
  33.7 0.2 fusion.1
  33.9 8.2 %all-to-all-done.1.got = bf16[16,8,640]{2,1,0:T(8,128)(2,1)S(1)} async-done(((bf16[16,8,640]{2,1,0:T(8,128)(2,1)}), bf16[16,8,640]{2,1,0:T(8,128)(2,1)S(1)}, u32[]{:S(2)}, u32[]{:S(2)}) %all-to-all-start.1) | async-done | bytes 163872 | tf_op jit(solution)/shard_map/all_to_all | solution.py:52
  42.1 0.0 copy-done.3
  42.1 10.4 %shard_map.105 = bf16[16,8,640]{2,1,0:T(8,128)(2,1)} custom-call(s32[36]{0:T(128)S(1)} %get-tuple-element.11.pair_of, s32[36]{0:T(128)S(1)} %get-tuple-element.10.live, bf16[16,8,640]{2,1,0:T(8,128)(2,1)S(1)} %all-to-all-done.1.got, bf16[36,128,128]{2,1,0:T(8,128)(2,1)S(1)} %copy-done.3, bf16[36,128,128]{2,1,0:T(8,128)(2,1)S(1)} %copy-done.4, ...), custom_call_target="tpu_custom_call" | custom-call | tf_op jit(solution)/shard_map/pallas_call | solution.py:260
  52.6 3.5 %all-to-all-start.2 = ((bf16[16,8,640]{2,1,0:T(8,128)(2,1)}), bf16[16,8,640]{2,1,0:T(8,128)(2,1)S(1)}, u32[]{:S(2)}, u32[]{:S(2)}) async-start(bf16[16,8,640]{2,1,0:T(8,128)(2,1)} %shard_map.105), calls=%async_computation.2 | async-start | bytes 327680 | tf_op jit(solution)/shard_map/all_to_all | solution.py:52
  56.1 8.4 %all-to-all-done.2.got = bf16[16,8,640]{2,1,0:T(8,128)(2,1)S(1)} async-done(((bf16[16,8,640]{2,1,0:T(8,128)(2,1)}), bf16[16,8,640]{2,1,0:T(8,128)(2,1)S(1)}, u32[]{:S(2)}, u32[]{:S(2)}) %all-to-all-start.2) | async-done | bytes 163872 | tf_op jit(solution)/shard_map/all_to_all | solution.py:52
  64.5 5.8 %copy-done.1 = bf16[512,16384]{1,0:T(8,128)(2,1)S(1)} copy-done((bf16[512,16384]{1,0:T(8,128)(2,1)S(1)}, bf16[512,16384]{1,0:T(8,128)(2,1)}, u32[]{:S(2)}) %copy-start.1) | copy-done | bytes 16777240
  70.3 3.2 %shard_map.106 = (bf16[16,8,1024]{2,1,0:T(8,128)(2,1)S(1)}, bf16[8,1024]{1,0:T(8,128)(2,1)}) custom-call(s32[4]{0:T(128)S(1)} %and_select_fusion.group_of, bf16[16,8,640]{2,1,0:T(8,128)(2,1)S(1)} %all-to-all-done.2.got, bf16[8,512]{1,0:T(8,128)(2,1)S(1)} %get-tuple-element.7.query, bf16[512,16384]{1,0:T(8,128)(2,1)S(1)} %copy-done.1), custom_call_target="tpu_custom_call" | custom-call | tf_op jit(solution)/shard_map/pallas_call | solution.py:268
  73.5 12.6 %all_to_all.20 = bf16[16,8,1024]{2,1,0:T(8,128)(2,1)S(1)} all-to-all(bf16[16,8,1024]{2,1,0:T(8,128)(2,1)S(1)} %get-tuple-element.8), channel_id=1, replica_groups=mesh['groups'=2,'attn'=16] {'attn'}, dimensions={0} | all-to-all | bytes 524288 | tf_op jit(solution)/shard_map/all_to_all | solution.py:52
  86.1 0.6 reduce_sum.32
  (12 shorter events, 0.1 us)
Async XLA Ops:
  2.1 17.4 %all-to-all-start = ((bf16[16,8,1024]{2,1,0:T(8,128)(2,1)}), bf16[16,8,1024]{2,1,0:T(8,128)(2,1)S(1)}, u32[]{:S(2)}, u32[]{:S(2)}) async-start(bf16[16,8,1024]{2,1,0:T(8,128)(2,1)} %broadcast_in_dim.46), calls=%async_computation | async-start | bytes 524288 | tf_op jit(solution)/shard_map/all_to_all | solution.py:52
  19.5 5.8 %copy-start = (bf16[16384,512]{1,0:T(8,128)(2,1)S(1)}, bf16[16384,512]{1,0:T(8,128)(2,1)}, u32[]{:S(2)}) copy-start(bf16[16384,512]{1,0:T(8,128)(2,1)} %w_query.1) | copy-start | bytes 50331652
  25.3 1.6 %copy-start.2 = (bf16[1024,1024]{1,0:T(8,128)(2,1)S(1)}, bf16[1024,1024]{1,0:T(8,128)(2,1)}, u32[]{:S(2)}) copy-start(bf16[1024,1024]{1,0:T(8,128)(2,1)} %w_kv.1) | copy-start | bytes 6291460
  26.9 15.3 %copy-start.3 = (bf16[36,128,128]{2,1,0:T(8,128)(2,1)S(1)}, bf16[36,128,128]{2,1,0:T(8,128)(2,1)}, u32[]{:S(2)}) copy-start(bf16[36,128,128]{2,1,0:T(8,128)(2,1)} %k_cache.1) | copy-start | bytes 3538948
  26.9 15.3 %copy-start.4 = (bf16[36,128,128]{2,1,0:T(8,128)(2,1)S(1)}, bf16[36,128,128]{2,1,0:T(8,128)(2,1)}, u32[]{:S(2)}) copy-start(bf16[36,128,128]{2,1,0:T(8,128)(2,1)} %v_cache.1) | copy-start | bytes 3538948
  30.2 11.9 %all-to-all-start.1 = ((bf16[16,8,640]{2,1,0:T(8,128)(2,1)}), bf16[16,8,640]{2,1,0:T(8,128)(2,1)S(1)}, u32[]{:S(2)}, u32[]{:S(2)}) async-start(bf16[16,8,640]{2,1,0:T(8,128)(2,1)} %get-tuple-element.6), calls=%async_computation.1 | async-start | bytes 327680 | tf_op jit(solution)/shard_map/all_to_all | solution.py:52
  52.6 11.9 %all-to-all-start.2 = ((bf16[16,8,640]{2,1,0:T(8,128)(2,1)}), bf16[16,8,640]{2,1,0:T(8,128)(2,1)S(1)}, u32[]{:S(2)}, u32[]{:S(2)}) async-start(bf16[16,8,640]{2,1,0:T(8,128)(2,1)} %shard_map.105), calls=%async_computation.2 | async-start | bytes 327680 | tf_op jit(solution)/shard_map/all_to_all | solution.py:52
  64.5 5.8 %copy-start.1 = (bf16[512,16384]{1,0:T(8,128)(2,1)S(1)}, bf16[512,16384]{1,0:T(8,128)(2,1)}, u32[]{:S(2)}) copy-start(bf16[512,16384]{1,0:T(8,128)(2,1)} %w_out.1) | copy-start | bytes 50331652

commit v3 on v2

v3 whole, which is shorter than its diff:
```python
import functools
import math

import jax
import jax.numpy as jnp
from jax import lax
from jax.experimental import pallas as pl
from jax.experimental.pallas import tpu as pltpu
from jax.sharding import PartitionSpec as P

HD = 128
H = 64
KVH = 4
GH = H // KVH

lowest = -1e30
rope_base = 500000.0
score_scale = 1.0 / math.sqrt(HD)
bf16 = jnp.bfloat16
f32 = jnp.float32
VMEM = pltpu.MemorySpace.VMEM
SMEM = pltpu.MemorySpace.SMEM
KV = KVH * HD
PAGE = 128
HALF = HD // 2


def rotate(vectors, cosine, sine):
    return vectors * cosine + pltpu.roll(vectors, HALF, 1) * sine


def exchange(buffer):
    return lax.all_to_all(buffer, "attn", 0, 0, tiled=True)


def lane_of(shape):
    return lax.broadcasted_iota(jnp.int32, shape, 1)


def spread_kernel(device, hidden, send):
    for j in range(send.shape[0]):
        send[j] = hidden[...]


def add_kernel(got, out):
    total = got[0].astype(f32)
    for src in range(1, got.shape[0]):
        total = total + got[src].astype(f32)
    out[...] = total.astype(bf16)


def place_slots(device, lengths, table, pair_of, live, slots, total):
    requests = table.shape[0]
    slot = device * slots + lane_of((1, HD))
    pair = jnp.full((1, HD), requests * KVH, jnp.int32)
    alive = jnp.zeros((1, HD), jnp.int32)
    for r in range(requests):
        pages = lax.div(lengths[r] + PAGE - 1, PAGE)
        offset = slot - table[r, 0, 0]
        offset = jnp.where(offset < 0, offset + total, offset)
        here = offset < KVH * pages
        group = jnp.zeros((1, HD), jnp.int32)
        for g in range(1, KVH):
            group = group + (offset >= g * pages).astype(jnp.int32)
        pair = jnp.where(here, r * KVH + group, pair)
        alive = jnp.where(here, lengths[r] - 1 - (offset - group * pages) * PAGE, alive)
    pair_of[...] = pair
    live[...] = alive


def project_kernel(
    device, lengths, table, hs, gain, w_query, w_kv,
    send, query, own_tables, pair_of, live, normed, kv_rows, tables, *, slots,
):
    n, requests, width = hs.shape
    columns = w_query.shape[1]
    square = jnp.zeros((requests, width), f32)
    for k in range(n):
        values = hs[k].astype(f32)
        square = square + values * values
    scale = lax.rsqrt(jnp.sum(square, axis=1, keepdims=True) / (n * width) + 1e-05)

    row, lane = lax.broadcasted_iota(jnp.int32, (requests, HD), 0), lane_of((requests, HD))
    position = jnp.zeros((requests, HD), f32)
    for r in range(requests):
        position = jnp.where(row == r, (lengths[r] - 1).astype(f32), position)
    index = jnp.where(lane < HALF, lane, lane - HALF).astype(f32)
    angles = position * jnp.exp(index * (-2.0 * math.log(rope_base) / HD))
    cosine = jnp.cos(angles)
    sine = jnp.sin(angles)
    sine = jnp.where(lane < HALF, -sine, sine)
    tables[:requests] = cosine
    tables[requests:] = sine
    mine = lax.div(device[0], 2)
    keys_here = lax.rem(device[0], 2) == 0
    own_tables[0:1, :] = jnp.where(keys_here, tables[pl.ds(mine, 1), :], 1.0)
    own_tables[1:2, :] = jnp.where(keys_here, tables[pl.ds(requests + mine, 1), :], 0.0)
    place_slots(device[0], lengths, table, pair_of, live, slots, n * slots)

    product = jnp.zeros((requests, columns), f32)
    for k in range(n):
        part = hs[k].astype(f32) * scale * gain[:, k * width : (k + 1) * width]
        part = part.astype(bf16)
        normed[k] = part
        product = product + jnp.dot(
            part, w_query[k * width : (k + 1) * width, :], preferred_element_type=f32
        )
    kv = jnp.dot(normed[device[0]], w_kv[...], preferred_element_type=f32)
    for i in range(2 * KVH):
        half, group = divmod(i, KVH)
        value = kv[:, i * HD : (i + 1) * HD]
        upper = value.astype(bf16).astype(f32)
        start = half * 2 * KVH + group
        kv_rows[pl.ds(start, requests, stride=4 * KVH), :] = upper
        kv_rows[pl.ds(start + KVH, requests, stride=4 * KVH), :] = value - upper
    for c in range(columns // HD):
        turned = rotate(product[:, c * HD : (c + 1) * HD], cosine, sine)
        query[:, c * HD : (c + 1) * HD] = turned.astype(bf16)
    whole = query[...]
    for j in range(n):
        send[j, :, :columns] = whole
        rows = kv_rows[j * 2 * KVH : (j + 1) * 2 * KVH, :]
        if requests > 2 * KVH:
            rows = jnp.concatenate([rows, jnp.zeros((requests - 2 * KVH, HD), f32)], axis=0)
        send[j, :, columns:] = rows.astype(bf16)


def attend_kernel(
    pair_of, live, got, k_cache, v_cache, own_tables, send,
    queries, slot_score, slot_weight, slot_out, slot_peak, slot_total, peak, total, mixed, kv_block,
):
    n, requests, wide = got.shape
    columns = wide - HD
    heads = columns // HD
    slots, page = k_cache.shape[:2]
    for h in range(H):
        src, c = divmod(h, heads)
        queries[pl.ds(h, requests, stride=H), :] = got[src, :, c * HD : (c + 1) * HD].astype(f32)
    queries[requests * H :, :] = jnp.zeros((GH, HD), f32)
    peak[...] = jnp.full_like(peak, lowest)
    total[...] = jnp.zeros_like(total)
    mixed[...] = jnp.zeros_like(mixed)

    def rows_of(s):
        return pl.ds(pl.multiple_of(pair_of[0, s] * GH, GH), GH)

    for s in range(slots):
        slot_score[s] = lax.dot_general(
            queries[rows_of(s), :].astype(bf16), k_cache[s], (((1,), (1,)), ((), ())),
            preferred_element_type=f32,
        )
    places = lane_of((GH, page))
    for s in range(slots):
        alive = places < live[0, s]
        scores = jnp.where(alive, slot_score[s] * score_scale, lowest)
        top = jnp.max(scores, axis=1, keepdims=True)
        weights = jnp.where(alive, jnp.exp(scores - top), 0.0)
        slot_weight[s] = weights.astype(bf16)
        slot_peak[s] = jnp.broadcast_to(top, (GH, HD))
        slot_total[s] = jnp.broadcast_to(jnp.sum(weights, axis=1, keepdims=True), (GH, HD))
    for s in range(slots):
        slot_out[s] = jnp.dot(slot_weight[s], v_cache[s], preferred_element_type=f32)
    running = slot_peak[0]
    peak[rows_of(0), :] = running
    for s in range(1, slots):
        value = slot_peak[s]
        same = pair_of[0, s] == pair_of[0, s - 1]
        running = jnp.maximum(value, jnp.where(same, running, lowest))
        peak[rows_of(s), :] = running
    run_total = jnp.zeros((GH, HD), f32)
    run_mixed = jnp.zeros((GH, HD), f32)
    for s in range(slots):
        factor = jnp.exp(slot_peak[s] - peak[rows_of(s), :])
        keep = jnp.where(pair_of[0, s] == pair_of[0, max(s - 1, 0)], 1.0, 0.0)
        run_total = keep * run_total + factor * slot_total[s]
        run_mixed = keep * run_mixed + factor * slot_out[s]
        total[rows_of(s), :] = run_total
        mixed[rows_of(s), :] = run_mixed

    kv = jnp.zeros((2 * KVH, HD), f32)
    for src in range(n):
        kv = kv + got[src, : 2 * KVH, columns:].astype(f32)
    kv = kv + pltpu.roll(kv, KVH, 0)
    kv = rotate(kv, own_tables[0:1, :], own_tables[1:2, :])
    upper = lax.broadcasted_iota(jnp.int32, kv.shape, 0) < KVH
    kv = jnp.where(upper, pltpu.roll(kv, HALF, 1), kv)
    if requests > 2 * KVH:
        kv_block[...] = jnp.zeros_like(kv_block)
    kv_block[: 2 * KVH, :] = kv
    lanes = lane_of((requests, HD))
    order = lax.rem(lanes, heads)
    kind = lax.div(lanes, heads)
    for j in range(n):
        stats = jnp.zeros((requests, HD), f32)
        for c in range(heads):
            rows = pl.ds(j * heads + c, requests, stride=H)
            send[j, :, c * HD : (c + 1) * HD] = mixed[rows, :].astype(bf16)
            value = jnp.where(kind < 3, peak[rows, :], total[rows, :])
            stats = jnp.where(order == c, value, stats)
        first = stats.astype(bf16).astype(f32)
        stats = stats - first
        second = stats.astype(bf16).astype(f32)
        third = stats - second
        kinds = lax.rem(kind, 3)
        stats = jnp.where(kinds == 0, first, jnp.where(kinds == 1, second, third))
        send[j, :, columns:] = jnp.where(kind < 6, stats, kv_block[...]).astype(bf16)


def output_kernel(device, got, query, w_out, send, new_entries, entries, attention):
    n, requests, wide = got.shape
    columns = wide - HD
    heads = columns // HD
    width = send.shape[2]
    lanes = lane_of((requests, HD))
    narrow = lane_of((2 * KVH, HD)) < HALF
    for row in range(n):
        request, half = divmod(row, 2)
        block = got[row, : 2 * KVH, columns:].astype(f32)
        block = jnp.where(narrow, pltpu.roll(block, HALF, 1), pltpu.roll(block, KVH, 0))
        rows = pl.ds(half * KVH * requests + request, KVH, stride=requests)
        entries[rows, :] = block[:KVH]
    for i in range(2 * KVH):
        new_entries[:, i * HD : (i + 1) * HD] = entries[
            i * requests : (i + 1) * requests, :
        ].astype(bf16)

    def own(c, half):
        start = (lax.div(device[0] * heads + c, GH) + half * KVH) * requests
        return entries[pl.ds(pl.multiple_of(start, 8), requests), :]

    new_score = jnp.full((requests, HD), lowest, f32)
    for c in range(heads):
        score = query[:, c * HD : (c + 1) * HD].astype(f32) * own(c, 0)
        score = jnp.sum(score, axis=1, keepdims=True) * score_scale
        new_score = jnp.where(lanes == c, score, new_score)
    peaks, totals = [], []
    for src in range(n):
        stats = got[src, :, columns:].astype(f32)
        stats = (
            stats + pltpu.roll(stats, HD - heads, 1) + pltpu.roll(stats, HD - 2 * heads, 1)
        )
        peaks.append(stats)
        totals.append(pltpu.roll(stats, HD - 3 * heads, 1))
    top = new_score
    for value in peaks:
        top = jnp.maximum(top, value)
    weights = [jnp.exp(value - top) for value in peaks]
    new_weight = jnp.exp(new_score - top)
    total = new_weight
    for weight, value in zip(weights, totals):
        total = total + weight * value
    inverse = 1.0 / total
    weights = [weight * inverse for weight in weights]
    new_weight = new_weight * inverse
    for c in range(heads):
        mixed = new_weight[:, c : c + 1] * own(c, 1)
        for src in range(n):
            mixed = mixed + weights[src][:, c : c + 1] * got[
                src, :, c * HD : (c + 1) * HD
            ].astype(f32)
        attention[:, c * HD : (c + 1) * HD] = mixed.astype(bf16)
    whole = attention[...]
    for j in range(n):
        send[j] = jnp.dot(
            whole, w_out[:, j * width : (j + 1) * width], preferred_element_type=f32
        ).astype(bf16)


def call(kernel, out_shape, in_spaces, out_spaces, scratch, limit, moved=None):
    return pl.pallas_call(
        kernel,
        out_shape=out_shape,
        in_specs=[pl.BlockSpec(memory_space=space) for space in in_spaces],
        out_specs=[pl.BlockSpec(memory_space=space) for space in out_spaces],
        scratch_shapes=scratch,
        compiler_params=pltpu.CompilerParams(vmem_limit_bytes=limit << 20),
        cost_estimate=moved
        and pl.CostEstimate(flops=moved * 512, bytes_accessed=moved, transcendentals=0),
    )


def local(hidden, gain, w_query, w_kv, w_out, k_cache, v_cache, block_table, lengths):
    device = lax.axis_index("attn").astype(jnp.int32).reshape(1)
    n = lax.axis_size("attn")
    requests, width = hidden.shape
    columns = w_query.shape[1]
    slots = k_cache.shape[0]
    pairs = requests * KVH
    assert 2 * requests == n

    shape = jax.ShapeDtypeStruct
    (send,) = call(
        spread_kernel,
        [shape((n, requests, width), bf16)],
        [SMEM, VMEM],
        [VMEM],
        [],
        2,
        2 * (w_query.nbytes + w_kv.nbytes),
    )(device, hidden)
    hs = exchange(send)
    wide = shape((n, requests, columns + HD), bf16)
    send, query, own_tables, pair_of, live = call(
        functools.partial(project_kernel, slots=slots),
        [
            wide,
            shape((requests, columns), bf16),
            shape((2, HD), f32),
            shape((1, HD), jnp.int32),
            shape((1, HD), jnp.int32),
        ],
        [SMEM] * 3 + [VMEM] * 4,
        [VMEM] * 5,
        [
            pltpu.VMEM(hs.shape, bf16),
            pltpu.VMEM((n * 2 * KVH, HD), f32),
            pltpu.VMEM((2 * requests, HD), f32),
        ],
        4,
    )(device, lengths, block_table, hs, gain.reshape(1, n * width), w_query, w_kv)
    got = exchange(send)
    rows = pltpu.VMEM(((pairs + 1) * GH, HD), f32)
    slot_rows = pltpu.VMEM((slots, GH, HD), f32)
    (send,) = call(
        attend_kernel,
        [wide],
        [SMEM] * 2 + [VMEM] * 4,
        [VMEM],
        [rows, slot_rows, pltpu.VMEM((slots, GH, HD), bf16)]
        + [slot_rows] * 3
        + [rows] * 3
        + [pltpu.VMEM((requests, HD), f32)],
        8,
    )(pair_of, live, got, k_cache, v_cache, own_tables)
    got = exchange(send)
    send, new_entries = call(
        output_kernel,
        [shape((n, requests, width), bf16), shape((requests, 2 * KV), bf16)],
        [SMEM] + [VMEM] * 3,
        [VMEM] * 2,
        [pltpu.VMEM((2 * KVH * requests, HD), f32), pltpu.VMEM((requests, columns), bf16)],
        4,
    )(device, got, query, w_out)
    got = exchange(send)
    (attn_out,) = call(add_kernel, [shape((requests, width), bf16)], [VMEM], [VMEM], [], 4)(got)
    return attn_out, new_entries


def solution(mesh):
    in_specs = (
        P("groups", "attn"),
        P(),
        P(None, "attn"),
        P("attn", None),
        P("attn", None),
        P(("groups", "attn"), None, None),
        P(("groups", "attn"), None, None),
        P("groups", None, None),
        P("groups"),
    )
    out_specs = (P("groups", "attn"), P("groups", None))
    return jax.shard_map(local, mesh=mesh, in_specs=in_specs, out_specs=out_specs, check_vma=False)
```

time: 87.5 us -> 63.4 us (0.72)
  blocking collectives: 12.6 us -> 52.4 us
  waiting for transfers between devices: 23.9 us -> 0 us
  local copies, waits for them, and re-layouts: 16.4 us -> 0.92 us
  starting transfers between devices: 14.4 us -> 0 us
  Pallas kernels: 16.9 us -> 8.88 us
  other arithmetic: 1.75 us -> 0.01 us
    all_to_all x1 -> x4, blocking collectives: 12.6 us -> 52.4 us  [exchange(): return lax.all_to_all(buffer, 'attn', 0, 0, tiled=True)]
    all_to_all x3 -> x0, waiting for transfers between devices: 23.9 us -> none  [exchange(): return lax.all_to_all(buffer, 'attn', 0, 0, tiled=True)]
    all_to_all x3 -> x0, starting transfers between devices: 14.4 us -> none  [exchange(): return lax.all_to_all(buffer, 'attn', 0, 0, tiled=True)]
    unnamed x10 -> x30, local copies, waits for them, and re-layouts: 13.1 us -> 0.92 us
    pallas_call x3 -> x5, Pallas kernels: 16.9 us -> 8.88 us  [the longest x1 3.45 us: local(): call(functools.partial(project_kernel, slots=slots), [wide, shape((reques...]
    broadcast_in_dim x2 -> x0, local copies, waits for them, and re-layouts: 1.51 us -> none  [the longest x1 1.44 us: local(): hs = exchange(jnp.broadcast_to(hidden[None], (n, requests, width)))]
  transfers between devices with their start and end apart: 3 -> 0, of which waited for: 3 -> 0; matrix products, arithmetic and copies ran while one was open for 3% -> 0% of each run, Pallas kernels for 0% -> 0%
where the time goes in v3:
time: 63.4 us; the launch traced here: 63 us
  blocking collectives  52.4 us (83%)
  Pallas kernels  8.88 us (14%)
  local copies, waits for them, and re-layouts  0.92 us (1%)
  between operations  0.82 us (1%)
    all_to_all x4, blocking collectives, exchange(): return lax.all_to_all(buffer, 'attn', 0, 0, tiled=True)  52.4 us
    pallas_call x1, Pallas kernels, local(): call(functools.partial(project_kernel, slots=slots), [wide, shape((reques...  3.45 us
    pallas_call x1, Pallas kernels, local(): call(output_kernel, [shape((n, requests, width), bf16), shape((requests,...  2.67 us
    pallas_call x1, Pallas kernels, local(): call(attend_kernel, [wide], [SMEM] * 2 + [VMEM] * 4, [VMEM], [rows, slot_...  2.09 us

profile of v3, /device:TPU:0, one launch (start us, length us, event | category | flops | bytes accessed | tf_op | source)
XLA Modules:
  0.0 63.0 jit_solution(4315875495217755134)
XLA Ops:
  0.6 0.0 slice-start
  0.6 0.0 slice-start.4
  0.7 0.0 copy-start.6
  0.7 0.9 %copy-done.6 = bf16[8,1024]{1,0:T(8,128)(2,1)S(1)} copy-done((bf16[8,1024]{1,0:T(8,128)(2,1)S(1)}, bf16[8,1024]{1,0:T(8,128)(2,1)}, u32[]{:S(2)}) %copy-start.6) | copy-done | bytes 16408
  1.5 0.0 copy-start.3
  1.5 0.0 copy-start.4
  1.6 0.0 slice-start.5
  1.6 0.0 slice-start.6
  1.6 0.0 slice-start.7
  1.6 17.5 %all_to_all.20.hs = bf16[16,8,1024]{2,1,0:T(8,128)(2,1)S(1)} all-to-all(bf16[16,8,1024]{2,1,0:T(8,128)(2,1)S(1)} %shard_map.104), channel_id=1, replica_groups=mesh['groups'=2,'attn'=16] {'attn'}, dimensions={0} | all-to-all | bytes 524288 | tf_op jit(solution)/shard_map/all_to_all | solution.py:33
  19.1 0.0 slice-done
  19.1 0.0 slice-done.2
  19.2 0.0 copy-start.1
  19.2 0.0 copy-start.2
  19.2 3.4 %shard_map.105 = (bf16[16,8,640]{2,1,0:T(8,128)(2,1)S(1)}, bf16[8,512]{1,0:T(8,128)(2,1)S(1)}, f32[2,128]{1,0:T(2,128)S(1)}, s32[1,128]{1,0:T(1,128)S(1)}, s32[1,128]{1,0:T(1,128)S(1)}) custom-call(s32[1]{0:T(128)} %bitcast.device, s32[8]{0:T(128)S(1)} %copy-done.5, s32[8,4,32]{2,1,0:T(4,128)S(1)} %copy-done.4, bf16[16,8,1024]{2,1,0:T(8,128)(2,1)S(1)} %all_to_all.20.hs, ...), custom_call_target="tpu_custom_call" | custom-call | tf_op jit(solution)/shard_map/pallas_call | solution.py:303
  22.7 11.2 %all_to_all.21.got = bf16[16,8,640]{2,1,0:T(8,128)(2,1)S(1)} all-to-all(bf16[16,8,640]{2,1,0:T(8,128)(2,1)S(1)} %get-tuple-element.11), channel_id=1, replica_groups=mesh['groups'=2,'attn'=16] {'attn'}, dimensions={0} | all-to-all | bytes 327680 | tf_op jit(solution)/shard_map/all_to_all | solution.py:33
  33.9 0.0 copy-done.1
  33.9 2.1 %shard_map.106 = bf16[16,8,640]{2,1,0:T(8,128)(2,1)S(1)} custom-call(s32[1,128]{1,0:T(1,128)S(1)} %get-tuple-element.9.pair_of, s32[1,128]{1,0:T(1,128)S(1)} %get-tuple-element.10.live, bf16[16,8,640]{2,1,0:T(8,128)(2,1)S(1)} %all_to_all.21.got, bf16[36,128,128]{2,1,0:T(8,128)(2,1)S(1)} %copy-done.1, bf16[36,128,128]{2,1,0:T(8,128)(2,1)S(1)} %copy-done.2, ...), custom_call_target="tpu_custom_call" | custom-call | tf_op jit(solution)/shard_map/pallas_call | solution.py:324
  36.0 11.1 %all_to_all.22.got = bf16[16,8,640]{2,1,0:T(8,128)(2,1)S(1)} all-to-all(bf16[16,8,640]{2,1,0:T(8,128)(2,1)S(1)} %shard_map.106), channel_id=1, replica_groups=mesh['groups'=2,'attn'=16] {'attn'}, dimensions={0} | all-to-all | bytes 327680 | tf_op jit(solution)/shard_map/all_to_all | solution.py:33
  47.1 0.0 slice-done.6
  47.1 0.0 slice-done.7
  47.1 2.7 %shard_map.107 = (bf16[16,8,1024]{2,1,0:T(8,128)(2,1)S(1)}, bf16[8,1024]{1,0:T(8,128)(2,1)}) custom-call(s32[1]{0:T(128)} %bitcast.device, bf16[16,8,640]{2,1,0:T(8,128)(2,1)S(1)} %all_to_all.22.got, bf16[8,512]{1,0:T(8,128)(2,1)S(1)} %get-tuple-element.13.query, bf16[512,16384]{1,0:T(8,128)(2,1)S(1)} %bitcast.5), custom_call_target="tpu_custom_call" | custom-call | tf_op jit(solution)/shard_map/pallas_call | solution.py:336
  49.8 12.6 %all_to_all.23.got = bf16[16,8,1024]{2,1,0:T(8,128)(2,1)S(1)} all-to-all(bf16[16,8,1024]{2,1,0:T(8,128)(2,1)S(1)} %get-tuple-element.14), channel_id=1, replica_groups=mesh['groups'=2,'attn'=16] {'attn'}, dimensions={0} | all-to-all | bytes 524288 | tf_op jit(solution)/shard_map/all_to_all | solution.py:33
  62.4 0.6 %shard_map.108 = bf16[8,1024]{1,0:T(8,128)(2,1)} custom-call(bf16[16,8,1024]{2,1,0:T(8,128)(2,1)S(1)} %all_to_all.23.got), custom_call_target="tpu_custom_call" | custom-call | tf_op jit(solution)/shard_map/pallas_call | solution.py:345
  (17 shorter events, 0.0 us)
Async XLA Ops:
  0.6 18.5 %slice-start = ((s8[16777216]{0:T(1024)(128)(4,1)}), s8[4194304]{0:T(1024)(128)(4,1)S(1)}, s32[]{:S(2)}) async-start(s8[16777216]{0:T(1024)(128)(4,1)} %bitcast.2), calls=%async_computation.4 | async-start | bytes 8388608
  0.6 46.4 %slice-start.4 = ((s8[16777216]{0:T(1024)(128)(4,1)}), s8[4194304]{0:T(1024)(128)(4,1)S(1)}, s32[]{:S(2)}) async-start(s8[16777216]{0:T(1024)(128)(4,1)} %bitcast.4), calls=%async_computation.8 | async-start | bytes 8388608
  0.7 0.9 %copy-start.6 = (bf16[8,1024]{1,0:T(8,128)(2,1)S(1)}, bf16[8,1024]{1,0:T(8,128)(2,1)}, u32[]{:S(2)}) copy-start(bf16[8,1024]{1,0:T(8,128)(2,1)} %hidden.1) | copy-start | bytes 49156
  1.5 17.6 %slice-start.1 = ((s8[16777216]{0:T(1024)(128)(4,1)}), s8[4194304]{0:T(1024)(128)(4,1)S(1)}, s32[]{:S(2)}) async-start(s8[16777216]{0:T(1024)(128)(4,1)} %bitcast.2), calls=%async_computation.5 | async-start | bytes 8388608
  1.5 17.6 %slice-start.2 = ((s8[16777216]{0:T(1024)(128)(4,1)}), s8[4194304]{0:T(1024)(128)(4,1)S(1)}, s32[]{:S(2)}) async-start(s8[16777216]{0:T(1024)(128)(4,1)} %bitcast.2), calls=%async_computation.6 | async-start | bytes 8388608
  1.5 17.6 %slice-start.3 = ((s8[16777216]{0:T(1024)(128)(4,1)}), s8[4194304]{0:T(1024)(128)(4,1)S(1)}, s32[]{:S(2)}) async-start(s8[16777216]{0:T(1024)(128)(4,1)} %bitcast.2), calls=%async_computation.7 | async-start | bytes 8388608
  1.5 17.6 %copy-start = (bf16[1024,1024]{1,0:T(8,128)(2,1)S(1)}, bf16[1024,1024]{1,0:T(8,128)(2,1)}, u32[]{:S(2)}) copy-start(bf16[1024,1024]{1,0:T(8,128)(2,1)} %w_kv.1) | copy-start | bytes 6291460
  1.5 17.6 %copy-start.3 = (f32[16384]{0:T(1024)S(1)}, f32[16384]{0:T(1024)}, u32[]{:S(2)}) copy-start(f32[16384]{0:T(1024)} %param.10) | copy-start | bytes 196612
  1.5 17.6 %copy-start.4 = (s32[8,4,32]{2,1,0:T(4,128)S(1)}, s32[8,4,32]{2,1,0:T(4,128)}, u32[]{:S(2)}) copy-start(s32[8,4,32]{2,1,0:T(4,128)} %table.1) | copy-start | bytes 12292
  1.6 17.6 %copy-start.5 = (s32[8]{0:T(128)S(1)}, s32[8]{0:T(128)}, u32[]{:S(2)}) copy-start(s32[8]{0:T(128)} %lengths.1) | copy-start | bytes 100
  1.6 45.5 %slice-start.5 = ((s8[16777216]{0:T(1024)(128)(4,1)}), s8[4194304]{0:T(1024)(128)(4,1)S(1)}, s32[]{:S(2)}) async-start(s8[16777216]{0:T(1024)(128)(4,1)} %bitcast.4), calls=%async_computation.9 | async-start | bytes 8388608
  1.6 45.5 %slice-start.6 = ((s8[16777216]{0:T(1024)(128)(4,1)}), s8[4194304]{0:T(1024)(128)(4,1)S(1)}, s32[]{:S(2)}) async-start(s8[16777216]{0:T(1024)(128)(4,1)} %bitcast.4), calls=%async_computation.10 | async-start | bytes 8388608
  1.6 45.5 %slice-start.7 = ((s8[16777216]{0:T(1024)(128)(4,1)}), s8[4194304]{0:T(1024)(128)(4,1)S(1)}, s32[]{:S(2)}) async-start(s8[16777216]{0:T(1024)(128)(4,1)} %bitcast.4), calls=%async_computation.11 | async-start | bytes 8388608
  19.2 14.7 %copy-start.1 = (bf16[36,128,128]{2,1,0:T(8,128)(2,1)S(1)}, bf16[36,128,128]{2,1,0:T(8,128)(2,1)}, u32[]{:S(2)}) copy-start(bf16[36,128,128]{2,1,0:T(8,128)(2,1)} %k_cache.1) | copy-start | bytes 3538948
  19.2 14.7 %copy-start.2 = (bf16[36,128,128]{2,1,0:T(8,128)(2,1)S(1)}, bf16[36,128,128]{2,1,0:T(8,128)(2,1)}, u32[]{:S(2)}) copy-start(bf16[36,128,128]{2,1,0:T(8,128)(2,1)} %v_cache.1) | copy-start | bytes 3538948

commit v4 on v3

--- a/solution.py
+++ b/solution.py
@@ -31,6 +31,17 @@
 
 def exchange(buffer):
     return lax.all_to_all(buffer, "attn", 0, 0, tiled=True)
+
+
+def exchange_same_core(buffer):
+    chips = buffer.shape[0]
+    groups = [[2 * chip + core for chip in range(chips)] for core in range(2)]
+    return lax.all_to_all(buffer, "attn", 0, 0, tiled=True, axis_index_groups=groups)
+
+
+def swap_cores(buffer):
+    n = lax.axis_size("attn")
+    return lax.ppermute(buffer, "attn", [(i, i ^ 1) for i in range(n)])
 
 
 def lane_of(shape):
@@ -68,44 +79,55 @@
     live[...] = alive
 
 
-def project_kernel(
-    device, lengths, table, hs, gain, w_query, w_kv,
-    send, query, own_tables, pair_of, live, normed, kv_rows, tables, *, slots,
+def prepare_kernel(
+    device, lengths, table, near, tables, own_tables, pair_of, live, square, *, slots
 ):
-    n, requests, width = hs.shape
-    columns = w_query.shape[1]
-    square = jnp.zeros((requests, width), f32)
-    for k in range(n):
-        values = hs[k].astype(f32)
-        square = square + values * values
-    scale = lax.rsqrt(jnp.sum(square, axis=1, keepdims=True) / (n * width) + 1e-05)
-
+    chips, requests, _ = near.shape
+    total = jnp.zeros(square.shape, f32)
+    for chip in range(chips):
+        values = near[chip].astype(f32)
+        total = total + values * values
+    square[...] = total
     row, lane = lax.broadcasted_iota(jnp.int32, (requests, HD), 0), lane_of((requests, HD))
     position = jnp.zeros((requests, HD), f32)
     for r in range(requests):
         position = jnp.where(row == r, (lengths[r] - 1).astype(f32), position)
     index = jnp.where(lane < HALF, lane, lane - HALF).astype(f32)
     angles = position * jnp.exp(index * (-2.0 * math.log(rope_base) / HD))
-    cosine = jnp.cos(angles)
     sine = jnp.sin(angles)
-    sine = jnp.where(lane < HALF, -sine, sine)
-    tables[:requests] = cosine
-    tables[requests:] = sine
+    tables[:requests] = jnp.cos(angles)
+    tables[requests:] = jnp.where(lane < HALF, -sine, sine)
     mine = lax.div(device[0], 2)
     keys_here = lax.rem(device[0], 2) == 0
     own_tables[0:1, :] = jnp.where(keys_here, tables[pl.ds(mine, 1), :], 1.0)
     own_tables[1:2, :] = jnp.where(keys_here, tables[pl.ds(requests + mine, 1), :], 0.0)
-    place_slots(device[0], lengths, table, pair_of, live, slots, n * slots)
-
+    place_slots(device[0], lengths, table, pair_of, live, slots, 2 * chips * slots)
+
+
+def project_kernel(
+    device, near, far, square, tables, gain, w_query, w_kv, send, query, kv_rows
+):
+    chips, requests, width = near.shape
+    n = 2 * chips
+    columns = w_query.shape[1]
+    core = lax.rem(device[0], 2)
+    total = square[...]
+    for chip in range(chips):
+        values = far[chip].astype(f32)
+        total = total + values * values
+    scale = lax.rsqrt(jnp.sum(total, axis=1, keepdims=True) / (n * width) + 1e-05)
     product = jnp.zeros((requests, columns), f32)
     for k in range(n):
-        part = hs[k].astype(f32) * scale * gain[:, k * width : (k + 1) * width]
-        part = part.astype(bf16)
-        normed[k] = part
+        chip, from_core = divmod(k, 2)
+        values = jnp.where(core == from_core, near[chip].astype(f32), far[chip].astype(f32))
+        part = (values * scale * gain[:, k * width : (k + 1) * width]).astype(bf16)
         product = product + jnp.dot(
             part, w_query[k * width : (k + 1) * width, :], preferred_element_type=f32
         )
-    kv = jnp.dot(normed[device[0]], w_kv[...], preferred_element_type=f32)
+    own_gain = gain[:, pl.ds(pl.multiple_of(device[0] * width, HD), width)]
+    own = (near[lax.div(device[0], 2)].astype(f32) * scale * own_gain).astype(bf16)
+    kv = jnp.dot(own, w_kv[...], preferred_element_type=f32)
+    cosine, sine = tables[:requests], tables[requests:]
     for i in range(2 * KVH):
         half, group = divmod(i, KVH)
         value = kv[:, i * HD : (i + 1) * HD]
@@ -206,11 +228,20 @@
         send[j, :, columns:] = jnp.where(kind < 6, stats, kv_block[...]).astype(bf16)
 
 
-def output_kernel(device, got, query, w_out, send, new_entries, entries, attention):
+def multiply_out(attention, w_out, result, core):
+    chips, _, width = result.shape
+    whole = attention[...]
+    for chip in range(chips):
+        columns = pl.ds(pl.multiple_of((2 * chip + core) * width, HD), width)
+        result[chip] = jnp.dot(
+            whole, w_out[:, columns], preferred_element_type=f32
+        ).astype(result.dtype)
+
+
+def combine_kernel(device, got, query, w_out, away, new_entries, attention, entries):
     n, requests, wide = got.shape
     columns = wide - HD
     heads = columns // HD
-    width = send.shape[2]
     lanes = lane_of((requests, HD))
     narrow = lane_of((2 * KVH, HD)) < HALF
     for row in range(n):
@@ -259,11 +290,16 @@
                 src, :, c * HD : (c + 1) * HD
             ].astype(f32)
         attention[:, c * HD : (c + 1) * HD] = mixed.astype(bf16)
-    whole = attention[...]
-    for j in range(n):
-        send[j] = jnp.dot(
-            whole, w_out[:, j * width : (j + 1) * width], preferred_element_type=f32
-        ).astype(bf16)
+    multiply_out(attention, w_out, away, 1 - lax.rem(device[0], 2))
+
+
+def keep_kernel(device, attention, w_out, kept):
+    multiply_out(attention, w_out, kept, lax.rem(device[0], 2))
+
+
+def join_kernel(kept, came, send):
+    for chip in range(send.shape[0]):
+        send[chip] = (kept[chip] + came[chip].astype(f32)).astype(bf16)
 
 
 def call(kernel, out_shape, in_spaces, out_spaces, scratch, limit, moved=None):
@@ -289,35 +325,41 @@
     assert 2 * requests == n
 
     shape = jax.ShapeDtypeStruct
+    halves = shape((n // 2, requests, width), bf16)
+    wide = shape((n, requests, columns + HD), bf16)
     (send,) = call(
         spread_kernel,
-        [shape((n, requests, width), bf16)],
+        [halves],
         [SMEM, VMEM],
         [VMEM],
         [],
         2,
         2 * (w_query.nbytes + w_kv.nbytes),
     )(device, hidden)
-    hs = exchange(send)
-    wide = shape((n, requests, columns + HD), bf16)
-    send, query, own_tables, pair_of, live = call(
-        functools.partial(project_kernel, slots=slots),
+    near = exchange_same_core(send)
+    far = swap_cores(near)
+    tables, own_tables, pair_of, live, square = call(
+        functools.partial(prepare_kernel, slots=slots),
         [
-            wide,
-            shape((requests, columns), bf16),
+            shape((2 * requests, HD), f32),
             shape((2, HD), f32),
             shape((1, HD), jnp.int32),
             shape((1, HD), jnp.int32),
+            shape((requests, width), f32),
         ],
-        [SMEM] * 3 + [VMEM] * 4,
+        [SMEM] * 3 + [VMEM],
         [VMEM] * 5,
-        [
-            pltpu.VMEM(hs.shape, bf16),
-            pltpu.VMEM((n * 2 * KVH, HD), f32),
-            pltpu.VMEM((2 * requests, HD), f32),
-        ],
+        [],
+        2,
+    )(device, lengths, block_table, near)
+    send, query = call(
+        project_kernel,
+        [wide, shape((requests, columns), bf16)],
+        [SMEM] + [VMEM] * 7,
+        [VMEM] * 2,
+        [pltpu.VMEM((n * 2 * KVH, HD), f32)],
         4,
-    )(device, lengths, block_table, hs, gain.reshape(1, n * width), w_query, w_kv)
+    )(device, near, far, square, tables, gain.reshape(1, n * width), w_query, w_kv)
     got = exchange(send)
     rows = pltpu.VMEM(((pairs + 1) * GH, HD), f32)
     slot_rows = pltpu.VMEM((slots, GH, HD), f32)
@@ -333,15 +375,20 @@
         8,
     )(pair_of, live, got, k_cache, v_cache, own_tables)
     got = exchange(send)
-    send, new_entries = call(
-        output_kernel,
-        [shape((n, requests, width), bf16), shape((requests, 2 * KV), bf16)],
+    away, new_entries, attention = call(
+        combine_kernel,
+        [halves, shape((requests, 2 * KV), bf16), shape((requests, columns), bf16)],
         [SMEM] + [VMEM] * 3,
-        [VMEM] * 2,
-        [pltpu.VMEM((2 * KVH * requests, HD), f32), pltpu.VMEM((requests, columns), bf16)],
+        [VMEM] * 3,
+        [pltpu.VMEM((2 * KVH * requests, HD), f32)],
         4,
     )(device, got, query, w_out)
-    got = exchange(send)
+    came = swap_cores(away)
+    (kept,) = call(
+        keep_kernel, [shape(halves.shape, f32)], [SMEM] + [VMEM] * 2, [VMEM], [], 4
+    )(device, attention, w_out)
+    (send,) = call(join_kernel, [halves], [VMEM] * 2, [VMEM], [], 4)(kept, came)
+    got = exchange_same_core(send)
     (attn_out,) = call(add_kernel, [shape((requests, width), bf16)], [VMEM], [VMEM], [], 4)(got)
     return attn_out, new_entries
 

time: 63.4 us -> 59.6 us (0.940)
  blocking collectives: 52.4 us -> 47.5 us
    all_to_all x4 -> x2, blocking collectives: 52.4 us -> 22.6 us  [exchange(): return lax.all_to_all(buffer, 'attn', 0, 0, tiled=True)]
    all_to_all x0 -> x2, blocking collectives: none -> 24.9 us  [exchange_same_core(): lax.all_to_all(buffer, 'attn', 0, 0, tiled=True, axis_index_groups=groups)]
    pallas_call x3 -> x6, Pallas kernels: 6.13 us -> 6.67 us  [the longest x1 2.65 us: local(): call(project_kernel, [wide, shape((requests, columns), bf16)], [SMEM] + [...]
  transfers between devices with their start and end apart: 0 -> 2, of which waited for: 0 -> 2; matrix products, arithmetic and copies ran while one was open for 0% -> 0% of each run, Pallas kernels for 0% -> 3%
where the time goes in v4:
time: 59.6 us; the launch traced here: 59.2 us
  blocking collectives  47.5 us (80%)
  Pallas kernels  9.39 us (16%)
  local copies, waits for them, and re-layouts  0.91 us (2%)
  between operations  0.78 us (1%)
  waiting for transfers between devices  0.61 us (1%)
    all_to_all x2, blocking collectives, exchange_same_core(): lax.all_to_all(buffer, 'attn', 0, 0, tiled=True, axis_index_groups=groups)  24.9 us
    all_to_all x2, blocking collectives, exchange(): return lax.all_to_all(buffer, 'attn', 0, 0, tiled=True)  22.6 us
    pallas_call x1, Pallas kernels, local(): call(project_kernel, [wide, shape((requests, columns), bf16)], [SMEM] + [...  2.65 us
    pallas_call x1, Pallas kernels, local(): call(attend_kernel, [wide], [SMEM] * 2 + [VMEM] * 4, [VMEM], [rows, slot_...  2.1 us
    pallas_call x1, Pallas kernels, local(): call(combine_kernel, [halves, shape((requests, 2 * KV), bf16), shape((req...  1.91 us
    pallas_call x1, Pallas kernels, local(): call(keep_kernel, [shape(halves.shape, f32)], [SMEM] + [VMEM] * 2, [VMEM]...  1.19 us
  transfers between devices with their start and end apart: 2, of which 2 were waited for; matrix products, arithmetic and copies ran while one was open for 0% of the time, Pallas kernels for 3%

profile of v4, /device:TPU:0, one launch (start us, length us, event | category | flops | bytes accessed | tf_op | source)
XLA Modules:
  0.0 59.2 jit_solution(13807226934235850749)
XLA Ops:
  0.6 0.0 slice-start
  0.6 0.0 copy-start.7
  0.7 0.9 %copy-done.7 = bf16[8,1024]{1,0:T(8,128)(2,1)S(1)} copy-done((bf16[8,1024]{1,0:T(8,128)(2,1)S(1)}, bf16[8,1024]{1,0:T(8,128)(2,1)}, u32[]{:S(2)}) %copy-start.7) | copy-done | bytes 16408
  1.5 0.0 slice-start.3
  1.5 0.0 copy-start.1
  1.6 14.7 %all_to_all.20.near = bf16[8,8,1024]{2,1,0:T(8,128)(2,1)S(1)} all-to-all(bf16[8,8,1024]{2,1,0:T(8,128)(2,1)S(1)} %shard_map.104), channel_id=1, replica_groups={{0,2,4,6,8,10,12,14},{1,3,5,7,9,11,13,15},{16,18,20,22,24,26,28,30},{17..., dimensions={0} | all-to-all | bytes 262144 | tf_op jit(solution)/shard_map/all_to_all | solution.py:39
  16.3 0.0 collective-permute-start
  16.3 0.0 copy-done.5
  16.3 0.9 %shard_map.105 = (f32[16,128]{1,0:T(8,128)S(1)}, f32[2,128]{1,0:T(2,128)S(1)}, s32[1,128]{1,0:T(1,128)S(1)}, s32[1,128]{1,0:T(1,128)S(1)}, f32[8,1024]{1,0:T(8,128)S(1)}) custom-call(s32[1]{0:T(128)} %bitcast.device, s32[8]{0:T(128)S(1)} %copy-done.6, s32[8,4,32]{2,1,0:T(4,128)S(1)} %copy-done.5, bf16[8,8,1024]{2,1,0:T(8,128)(2,1)S(1)} %all_to_all.20.near), custom_call_target="tpu_custom_call" | custom-call | tf_op jit(solution)/shard_map/pallas_call | solution.py:341
  17.1 0.5 collective-permute-done.far
  17.6 0.0 slice-done.1
  17.7 0.0 copy-start.2
  17.7 0.0 copy-start.3
  17.7 0.0 copy-start
  17.7 2.6 %shard_map.106 = (bf16[16,8,640]{2,1,0:T(8,128)(2,1)S(1)}, bf16[8,512]{1,0:T(8,128)(2,1)S(1)}) custom-call(s32[1]{0:T(128)} %bitcast.device, bf16[8,8,1024]{2,1,0:T(8,128)(2,1)S(1)} %all_to_all.20.near, bf16[8,8,1024]{2,1,0:T(8,128)(2,1)S(1)} %collective-permute-done.far, f32[8,1024]{1,0:T(8,128)S(1)} %get-tuple-element.14.square, ...), custom_call_target="tpu_custom_call" | custom-call | tf_op jit(solution)/shard_map/pallas_call | solution.py:355
  20.3 11.6 %all_to_all.21.got = bf16[16,8,640]{2,1,0:T(8,128)(2,1)S(1)} all-to-all(bf16[16,8,640]{2,1,0:T(8,128)(2,1)S(1)} %get-tuple-element.16), channel_id=1, replica_groups=mesh['groups'=2,'attn'=16] {'attn'}, dimensions={0} | all-to-all | bytes 327680 | tf_op jit(solution)/shard_map/all_to_all | solution.py:33
  31.9 2.1 %shard_map.107 = bf16[16,8,640]{2,1,0:T(8,128)(2,1)S(1)} custom-call(s32[1,128]{1,0:T(1,128)S(1)} %get-tuple-element.12.pair_of, s32[1,128]{1,0:T(1,128)S(1)} %get-tuple-element.13.live, bf16[16,8,640]{2,1,0:T(8,128)(2,1)S(1)} %all_to_all.21.got, bf16[36,128,128]{2,1,0:T(8,128)(2,1)S(1)} %copy-done.2, bf16[36,128,128]{2,1,0:T(8,128)(2,1)S(1)} %copy-done.3, ...), custom_call_target="tpu_custom_call" | custom-call | tf_op jit(solution)/shard_map/pallas_call | solution.py:366
  34.0 11.1 %all_to_all.22.got = bf16[16,8,640]{2,1,0:T(8,128)(2,1)S(1)} all-to-all(bf16[16,8,640]{2,1,0:T(8,128)(2,1)S(1)} %shard_map.107), channel_id=1, replica_groups=mesh['groups'=2,'attn'=16] {'attn'}, dimensions={0} | all-to-all | bytes 327680 | tf_op jit(solution)/shard_map/all_to_all | solution.py:33
  45.1 1.9 %shard_map.108 = (bf16[8,8,1024]{2,1,0:T(8,128)(2,1)S(1)}, bf16[8,1024]{1,0:T(8,128)(2,1)}, bf16[8,512]{1,0:T(8,128)(2,1)S(1)}) custom-call(s32[1]{0:T(128)} %bitcast.device, bf16[16,8,640]{2,1,0:T(8,128)(2,1)S(1)} %all_to_all.22.got, bf16[8,512]{1,0:T(8,128)(2,1)S(1)} %get-tuple-element.18.query, bf16[512,16384]{1,0:T(8,128)(2,1)S(1)} %copy-done), custom_call_target="tpu_custom_call" | custom-call | tf_op jit(solution)/shard_map/pallas_call | solution.py:378
  47.0 0.0 collective-permute-start.1
  47.0 1.2 %shard_map.109.kept = f32[8,8,1024]{2,1,0:T(8,128)S(1)} custom-call(s32[1]{0:T(128)} %bitcast.device, bf16[8,512]{1,0:T(8,128)(2,1)S(1)} %get-tuple-element.19.attention, bf16[512,16384]{1,0:T(8,128)(2,1)S(1)} %copy-done), custom_call_target="tpu_custom_call" | custom-call | tf_op jit(solution)/shard_map/pallas_call | solution.py:387
  48.2 0.2 collective-permute-done.1.came
  48.4 10.2 %all_to_all.23.got = bf16[8,8,1024]{2,1,0:T(8,128)(2,1)S(1)} all-to-all(bf16[8,8,1024]{2,1,0:T(8,128)(2,1)S(1)} %shard_map.110), channel_id=1, replica_groups={{0,2,4,6,8,10,12,14},{1,3,5,7,9,11,13,15},{16,18,20,22,24,26,28,30},{17..., dimensions={0} | all-to-all | bytes 262144 | tf_op jit(solution)/shard_map/all_to_all | solution.py:39
  58.6 0.6 %shard_map.111 = bf16[8,1024]{1,0:T(8,128)(2,1)} custom-call(bf16[8,8,1024]{2,1,0:T(8,128)(2,1)S(1)} %all_to_all.23.got), custom_call_target="tpu_custom_call" | custom-call | tf_op jit(solution)/shard_map/pallas_call | solution.py:392
  (17 shorter events, 0.1 us)
Async XLA Ops:
  0.6 17.0 %slice-start = ((s8[16777216]{0:T(1024)(128)(4,1)}), s8[4194304]{0:T(1024)(128)(4,1)S(1)}, s32[]{:S(2)}) async-start(s8[16777216]{0:T(1024)(128)(4,1)} %bitcast.2), calls=%async_computation.4 | async-start | bytes 8388608
  0.6 0.9 %copy-start.7 = (bf16[8,1024]{1,0:T(8,128)(2,1)S(1)}, bf16[8,1024]{1,0:T(8,128)(2,1)}, u32[]{:S(2)}) copy-start(bf16[8,1024]{1,0:T(8,128)(2,1)} %hidden.1) | copy-start | bytes 49156
  1.5 14.8 %copy-start.5 = (s32[8,4,32]{2,1,0:T(4,128)S(1)}, s32[8,4,32]{2,1,0:T(4,128)}, u32[]{:S(2)}) copy-start(s32[8,4,32]{2,1,0:T(4,128)} %table.1) | copy-start | bytes 12292
  1.5 14.8 %copy-start.6 = (s32[8]{0:T(128)S(1)}, s32[8]{0:T(128)}, u32[]{:S(2)}) copy-start(s32[8]{0:T(128)} %lengths.1) | copy-start | bytes 100
  1.5 16.1 %slice-start.1 = ((s8[16777216]{0:T(1024)(128)(4,1)}), s8[4194304]{0:T(1024)(128)(4,1)S(1)}, s32[]{:S(2)}) async-start(s8[16777216]{0:T(1024)(128)(4,1)} %bitcast.2), calls=%async_computation.5 | async-start | bytes 8388608
  1.5 16.1 %slice-start.2 = ((s8[16777216]{0:T(1024)(128)(4,1)}), s8[4194304]{0:T(1024)(128)(4,1)S(1)}, s32[]{:S(2)}) async-start(s8[16777216]{0:T(1024)(128)(4,1)} %bitcast.2), calls=%async_computation.6 | async-start | bytes 8388608
  1.5 16.1 %slice-start.3 = ((s8[16777216]{0:T(1024)(128)(4,1)}), s8[4194304]{0:T(1024)(128)(4,1)S(1)}, s32[]{:S(2)}) async-start(s8[16777216]{0:T(1024)(128)(4,1)} %bitcast.2), calls=%async_computation.7 | async-start | bytes 8388608
  1.5 16.1 %copy-start.1 = (bf16[1024,1024]{1,0:T(8,128)(2,1)S(1)}, bf16[1024,1024]{1,0:T(8,128)(2,1)}, u32[]{:S(2)}) copy-start(bf16[1024,1024]{1,0:T(8,128)(2,1)} %w_kv.1) | copy-start | bytes 6291460
  1.5 16.1 %copy-start.4 = (f32[16384]{0:T(1024)S(1)}, f32[16384]{0:T(1024)}, u32[]{:S(2)}) copy-start(f32[16384]{0:T(1024)} %param.10) | copy-start | bytes 196612
  16.3 1.3 %collective-permute-start = (bf16[8,8,1024]{2,1,0:T(8,128)(2,1)S(1)}, bf16[8,8,1024]{2,1,0:T(8,128)(2,1)S(1)}, u32[]{:S(2)}, u32[]{:S(2)}) collective-permute-start(bf16[8,8,1024]{2,1,0:T(8,128)(2,1)S(1)} %all_to_all.20.near), channel_id=1, source_target_pairs={{0,1},{1,0},{2,3},{3,2},{4,5},{5,4},{6,7},{7,6},{8,9},{9,8},{10,11... | collective-permute-start | bytes 393224 | tf_op jit(solution)/shard_map/ppermute | solution.py:44
  17.7 14.3 %copy-start.2 = (bf16[36,128,128]{2,1,0:T(8,128)(2,1)S(1)}, bf16[36,128,128]{2,1,0:T(8,128)(2,1)}, u32[]{:S(2)}) copy-start(bf16[36,128,128]{2,1,0:T(8,128)(2,1)} %k_cache.1) | copy-start | bytes 3538948
  17.7 14.3 %copy-start.3 = (bf16[36,128,128]{2,1,0:T(8,128)(2,1)S(1)}, bf16[36,128,128]{2,1,0:T(8,128)(2,1)}, u32[]{:S(2)}) copy-start(bf16[36,128,128]{2,1,0:T(8,128)(2,1)} %v_cache.1) | copy-start | bytes 3538948
  17.7 27.4 %copy-start = (bf16[512,16384]{1,0:T(8,128)(2,1)S(1)}, bf16[512,16384]{1,0:T(8,128)(2,1)}, u32[]{:S(2)}) copy-start(bf16[512,16384]{1,0:T(8,128)(2,1)} %w_out.3) | copy-start | bytes 50331652
  47.0 1.3 %collective-permute-start.1 = (bf16[8,8,1024]{2,1,0:T(8,128)(2,1)S(1)}, bf16[8,8,1024]{2,1,0:T(8,128)(2,1)S(1)}, u32[]{:S(2)}, u32[]{:S(2)}) collective-permute-start(bf16[8,8,1024]{2,1,0:T(8,128)(2,1)S(1)} %get-tuple-element.20), channel_id=1, source_target_pairs={{0,1},{1,0},{2,3},{3,2},{4,5},{5,4},{6,7},{7,6},{8,9},{9,8},{10,11... | collective-permute-start | bytes 393224 | tf_op jit(solution)/shard_map/ppermute | solution.py:44

commit v5 on v4

--- a/solution.py
+++ b/solution.py
@@ -12,6 +12,8 @@
 H = 64
 KVH = 4
 GH = H // KVH
+CORE_H = H // 2
+CORE_GH = GH // 2
 
 lowest = -1e30
 rope_base = 500000.0
@@ -30,10 +32,6 @@
 
 
 def exchange(buffer):
-    return lax.all_to_all(buffer, "attn", 0, 0, tiled=True)
-
-
-def exchange_same_core(buffer):
     chips = buffer.shape[0]
     groups = [[2 * chip + core for chip in range(chips)] for core in range(2)]
     return lax.all_to_all(buffer, "attn", 0, 0, tiled=True, axis_index_groups=groups)
@@ -62,7 +60,9 @@
 
 def place_slots(device, lengths, table, pair_of, live, slots, total):
     requests = table.shape[0]
-    slot = device * slots + lane_of((1, HD))
+    lane = lane_of((1, HD))
+    partner = device + 1 - 2 * lax.rem(device, 2)
+    slot = jnp.where(lane < slots, device * slots + lane, (partner - 1) * slots + lane)
     pair = jnp.full((1, HD), requests * KVH, jnp.int32)
     alive = jnp.zeros((1, HD), jnp.int32)
     for r in range(requests):
@@ -104,128 +104,170 @@
     place_slots(device[0], lengths, table, pair_of, live, slots, 2 * chips * slots)
 
 
-def project_kernel(
-    device, near, far, square, tables, gain, w_query, w_kv, send, query, kv_rows
-):
+def normalize_kernel(device, near, far, square, gain, w_kv, normed, kept, away):
     chips, requests, width = near.shape
     n = 2 * chips
-    columns = w_query.shape[1]
     core = lax.rem(device[0], 2)
     total = square[...]
     for chip in range(chips):
         values = far[chip].astype(f32)
         total = total + values * values
     scale = lax.rsqrt(jnp.sum(total, axis=1, keepdims=True) / (n * width) + 1e-05)
-    product = jnp.zeros((requests, columns), f32)
     for k in range(n):
         chip, from_core = divmod(k, 2)
         values = jnp.where(core == from_core, near[chip].astype(f32), far[chip].astype(f32))
-        part = (values * scale * gain[:, k * width : (k + 1) * width]).astype(bf16)
+        normed[k] = (values * scale * gain[:, k * width : (k + 1) * width]).astype(bf16)
+    own = normed[device[0]]
+    for result, half in ((kept, core), (away, 1 - core)):
+        columns = pl.ds(pl.multiple_of(half * KV, KV), KV)
+        result[...] = jnp.dot(own, w_kv[:, columns], preferred_element_type=f32)
+
+
+def query_kernel(normed, tables, w_query, query):
+    n, requests, width = normed.shape
+    columns = w_query.shape[1]
+    product = jnp.zeros((requests, columns), f32)
+    for k in range(n):
         product = product + jnp.dot(
-            part, w_query[k * width : (k + 1) * width, :], preferred_element_type=f32
+            normed[k], w_query[k * width : (k + 1) * width, :], preferred_element_type=f32
         )
-    own_gain = gain[:, pl.ds(pl.multiple_of(device[0] * width, HD), width)]
-    own = (near[lax.div(device[0], 2)].astype(f32) * scale * own_gain).astype(bf16)
-    kv = jnp.dot(own, w_kv[...], preferred_element_type=f32)
     cosine, sine = tables[:requests], tables[requests:]
-    for i in range(2 * KVH):
-        half, group = divmod(i, KVH)
-        value = kv[:, i * HD : (i + 1) * HD]
-        upper = value.astype(bf16).astype(f32)
-        start = half * 2 * KVH + group
-        kv_rows[pl.ds(start, requests, stride=4 * KVH), :] = upper
-        kv_rows[pl.ds(start + KVH, requests, stride=4 * KVH), :] = value - upper
     for c in range(columns // HD):
         turned = rotate(product[:, c * HD : (c + 1) * HD], cosine, sine)
         query[:, c * HD : (c + 1) * HD] = turned.astype(bf16)
+
+
+def gather_kernel(query, kept, came, send, kv_rows):
+    chips, requests, wide = send.shape
+    columns = wide - HD
+    for group in range(KVH):
+        part = slice(group * HD, (group + 1) * HD)
+        value = kept[:, part] + came[:, part]
+        upper = value.astype(bf16).astype(f32)
+        kv_rows[pl.ds(group, requests, stride=2 * KVH), :] = upper
+        kv_rows[pl.ds(KVH + group, requests, stride=2 * KVH), :] = value - upper
     whole = query[...]
-    for j in range(n):
-        send[j, :, :columns] = whole
-        rows = kv_rows[j * 2 * KVH : (j + 1) * 2 * KVH, :]
+    for chip in range(chips):
+        send[chip, :, :columns] = whole
+        rows = kv_rows[chip * 2 * KVH : (chip + 1) * 2 * KVH, :]
         if requests > 2 * KVH:
             rows = jnp.concatenate([rows, jnp.zeros((requests - 2 * KVH, HD), f32)], axis=0)
-        send[j, :, columns:] = rows.astype(bf16)
+        send[chip, :, columns:] = rows.astype(bf16)
+
+
+def entry_kernel(got, own_tables, row):
+    columns = got.shape[2] - HD
+    kv = jnp.zeros((2 * KVH, HD), f32)
+    for chip in range(got.shape[0]):
+        kv = kv + got[chip, : 2 * KVH, columns:].astype(f32)
+    kv = kv + pltpu.roll(kv, KVH, 0)
+    row[...] = rotate(kv, own_tables[0:1, :], own_tables[1:2, :]).astype(bf16)
 
 
 def attend_kernel(
-    pair_of, live, got, k_cache, v_cache, own_tables, send,
-    queries, slot_score, slot_weight, slot_out, slot_peak, slot_total, peak, total, mixed, kv_block,
+    pair_of, live, got, k_near, v_near, k_far, v_far, peak, total, mixed,
+    queries, slot_score, slot_out, slot_peak, slot_total, run_peak, run_total, run_mixed,
 ):
-    n, requests, wide = got.shape
-    columns = wide - HD
-    heads = columns // HD
-    slots, page = k_cache.shape[:2]
-    for h in range(H):
-        src, c = divmod(h, heads)
-        queries[pl.ds(h, requests, stride=H), :] = got[src, :, c * HD : (c + 1) * HD].astype(f32)
-    queries[requests * H :, :] = jnp.zeros((GH, HD), f32)
-    peak[...] = jnp.full_like(peak, lowest)
-    total[...] = jnp.zeros_like(total)
-    mixed[...] = jnp.zeros_like(mixed)
-
-    def rows_of(s):
-        return pl.ds(pl.multiple_of(pair_of[0, s] * GH, GH), GH)
-
-    for s in range(slots):
+    chips, requests, wide = got.shape
+    heads = (wide - HD) // HD
+    slots, page = k_near.shape[:2]
+    pairs = requests * KVH
+    for h in range(CORE_H):
+        chip, c = divmod(h, heads)
+        queries[pl.ds(h, requests, stride=CORE_H), :] = got[
+            chip, :, c * HD : (c + 1) * HD
+        ].astype(f32)
+    queries[pairs * CORE_GH :, :] = jnp.zeros((CORE_GH, HD), f32)
+    run_peak[...] = jnp.full_like(run_peak, lowest)
+    run_total[...] = jnp.zeros_like(run_total)
+    run_mixed[...] = jnp.zeros_like(run_mixed)
+
+    def rows_of(s, side=0):
+        start = (pair_of[0, s] + side * (pairs + 1)) * CORE_GH
+        return pl.ds(pl.multiple_of(start, CORE_GH), CORE_GH)
+
+    for s in range(2 * slots):
+        keys = k_near[s] if s < slots else k_far[s - slots]
         slot_score[s] = lax.dot_general(
-            queries[rows_of(s), :].astype(bf16), k_cache[s], (((1,), (1,)), ((), ())),
+            queries[rows_of(s), :].astype(bf16), keys, (((1,), (1,)), ((), ())),
             preferred_element_type=f32,
         )
-    places = lane_of((GH, page))
-    for s in range(slots):
+    shape = (CORE_GH, HD)
+    places = lane_of((CORE_GH, page))
+    for s in range(2 * slots):
         alive = places < live[0, s]
         scores = jnp.where(alive, slot_score[s] * score_scale, lowest)
         top = jnp.max(scores, axis=1, keepdims=True)
         weights = jnp.where(alive, jnp.exp(scores - top), 0.0)
-        slot_weight[s] = weights.astype(bf16)
-        slot_peak[s] = jnp.broadcast_to(top, (GH, HD))
-        slot_total[s] = jnp.broadcast_to(jnp.sum(weights, axis=1, keepdims=True), (GH, HD))
-    for s in range(slots):
-        slot_out[s] = jnp.dot(slot_weight[s], v_cache[s], preferred_element_type=f32)
-    running = slot_peak[0]
-    peak[rows_of(0), :] = running
-    for s in range(1, slots):
-        value = slot_peak[s]
-        same = pair_of[0, s] == pair_of[0, s - 1]
-        running = jnp.maximum(value, jnp.where(same, running, lowest))
-        peak[rows_of(s), :] = running
-    run_total = jnp.zeros((GH, HD), f32)
-    run_mixed = jnp.zeros((GH, HD), f32)
-    for s in range(slots):
-        factor = jnp.exp(slot_peak[s] - peak[rows_of(s), :])
-        keep = jnp.where(pair_of[0, s] == pair_of[0, max(s - 1, 0)], 1.0, 0.0)
-        run_total = keep * run_total + factor * slot_total[s]
-        run_mixed = keep * run_mixed + factor * slot_out[s]
-        total[rows_of(s), :] = run_total
-        mixed[rows_of(s), :] = run_mixed
-
-    kv = jnp.zeros((2 * KVH, HD), f32)
-    for src in range(n):
-        kv = kv + got[src, : 2 * KVH, columns:].astype(f32)
-    kv = kv + pltpu.roll(kv, KVH, 0)
-    kv = rotate(kv, own_tables[0:1, :], own_tables[1:2, :])
-    upper = lax.broadcasted_iota(jnp.int32, kv.shape, 0) < KVH
-    kv = jnp.where(upper, pltpu.roll(kv, HALF, 1), kv)
+        slot_score[s] = weights
+        slot_peak[s] = jnp.broadcast_to(top, shape)
+        slot_total[s] = jnp.broadcast_to(jnp.sum(weights, axis=1, keepdims=True), shape)
+    for s in range(2 * slots):
+        values = v_near[s] if s < slots else v_far[s - slots]
+        slot_out[s] = jnp.dot(slot_score[s].astype(bf16), values, preferred_element_type=f32)
+    for side in range(2):
+        running = jnp.full(shape, lowest, f32)
+        for s in range(side * slots, (side + 1) * slots):
+            if s > side * slots:
+                same = pair_of[0, s] == pair_of[0, s - 1]
+                running = jnp.where(same, running, lowest)
+            running = jnp.maximum(slot_peak[s], running)
+            run_peak[rows_of(s, side), :] = running
+    for side in range(2):
+        sum_total = jnp.zeros(shape, f32)
+        sum_mixed = jnp.zeros(shape, f32)
+        for s in range(side * slots, (side + 1) * slots):
+            if s > side * slots:
+                keep = jnp.where(pair_of[0, s] == pair_of[0, s - 1], 1.0, 0.0)
+                sum_total, sum_mixed = keep * sum_total, keep * sum_mixed
+            rows = rows_of(s, side)
+            factor = jnp.exp(slot_peak[s] - run_peak[rows, :])
+            sum_total = sum_total + factor * slot_total[s]
+            sum_mixed = sum_mixed + factor * slot_out[s]
+            run_total[rows, :] = sum_total
+            run_mixed[rows, :] = sum_mixed
+    for pair in range(pairs):
+        here = slice(pair * CORE_GH, (pair + 1) * CORE_GH)
+        first = run_peak[here, :]
+        there = slice((pairs + 1 + pair) * CORE_GH, (pairs + 2 + pair) * CORE_GH)
+        second = run_peak[there, :]
+        top = jnp.maximum(first, second)
+        first, second = jnp.exp(first - top), jnp.exp(second - top)
+        peak[here, :] = top
+        total[here, :] = first * run_total[here, :] + second * run_total[there, :]
+        mixed[here, :] = first * run_mixed[here, :] + second * run_mixed[there, :]
+
+
+def share_kernel(device, peak, total, mixed, near_row, far_row, send, kv_block):
+    chips, requests, wide = send.shape
+    columns = wide - 2 * HD
+    heads = columns // HD
+    core = lax.rem(device[0], 2)
+    near, far = near_row[...].astype(f32), far_row[...].astype(f32)
+    keys_here = lax.broadcasted_iota(jnp.int32, near.shape, 0) < KVH
+    own = jnp.where(core == 0, near, far)
+    other = jnp.where(core == 0, far, near)
     if requests > 2 * KVH:
         kv_block[...] = jnp.zeros_like(kv_block)
-    kv_block[: 2 * KVH, :] = kv
+    kv_block[: 2 * KVH, :] = jnp.where(keys_here, own, other)
     lanes = lane_of((requests, HD))
     order = lax.rem(lanes, heads)
     kind = lax.div(lanes, heads)
-    for j in range(n):
+    kinds = lax.rem(kind, 3)
+    for chip in range(chips):
         stats = jnp.zeros((requests, HD), f32)
         for c in range(heads):
-            rows = pl.ds(j * heads + c, requests, stride=H)
-            send[j, :, c * HD : (c + 1) * HD] = mixed[rows, :].astype(bf16)
+            rows = pl.ds(chip * heads + c, requests, stride=CORE_H)
+            send[chip, :, c * HD : (c + 1) * HD] = mixed[rows, :].astype(bf16)
             value = jnp.where(kind < 3, peak[rows, :], total[rows, :])
             stats = jnp.where(order == c, value, stats)
         first = stats.astype(bf16).astype(f32)
         stats = stats - first
         second = stats.astype(bf16).astype(f32)
         third = stats - second
-        kinds = lax.rem(kind, 3)
         stats = jnp.where(kinds == 0, first, jnp.where(kinds == 1, second, third))
-        send[j, :, columns:] = jnp.where(kind < 6, stats, kv_block[...]).astype(bf16)
+        send[chip, :, columns : columns + HD] = stats.astype(bf16)
+        send[chip, :, columns + HD :] = kv_block[...].astype(bf16)
 
 
 def multiply_out(attention, w_out, result, core):
@@ -239,17 +281,13 @@
 
 
 def combine_kernel(device, got, query, w_out, away, new_entries, attention, entries):
-    n, requests, wide = got.shape
-    columns = wide - HD
+    chips, requests, wide = got.shape
+    columns = wide - 2 * HD
     heads = columns // HD
     lanes = lane_of((requests, HD))
-    narrow = lane_of((2 * KVH, HD)) < HALF
-    for row in range(n):
-        request, half = divmod(row, 2)
-        block = got[row, : 2 * KVH, columns:].astype(f32)
-        block = jnp.where(narrow, pltpu.roll(block, HALF, 1), pltpu.roll(block, KVH, 0))
-        rows = pl.ds(half * KVH * requests + request, KVH, stride=requests)
-        entries[rows, :] = block[:KVH]
+    for request in range(requests):
+        block = got[request, : 2 * KVH, columns + HD :].astype(f32)
+        entries[pl.ds(request, 2 * KVH, stride=requests), :] = block
     for i in range(2 * KVH):
         new_entries[:, i * HD : (i + 1) * HD] = entries[
             i * requests : (i + 1) * requests, :
@@ -265,8 +303,8 @@
         score = jnp.sum(score, axis=1, keepdims=True) * score_scale
         new_score = jnp.where(lanes == c, score, new_score)
     peaks, totals = [], []
-    for src in range(n):
-        stats = got[src, :, columns:].astype(f32)
+    for src in range(chips):
+        stats = got[src, :, columns : columns + HD].astype(f32)
         stats = (
             stats + pltpu.roll(stats, HD - heads, 1) + pltpu.roll(stats, HD - 2 * heads, 1)
         )
@@ -285,7 +323,7 @@
     new_weight = new_weight * inverse
     for c in range(heads):
         mixed = new_weight[:, c : c + 1] * own(c, 1)
-        for src in range(n):
+        for src in range(chips):
             mixed = mixed + weights[src][:, c : c + 1] * got[
                 src, :, c * HD : (c + 1) * HD
             ].astype(f32)
@@ -326,7 +364,6 @@
 
     shape = jax.ShapeDtypeStruct
     halves = shape((n // 2, requests, width), bf16)
-    wide = shape((n, requests, columns + HD), bf16)
     (send,) = call(
         spread_kernel,
         [halves],
@@ -336,7 +373,7 @@
         2,
         2 * (w_query.nbytes + w_kv.nbytes),
     )(device, hidden)
-    near = exchange_same_core(send)
+    near = exchange(send)
     far = swap_cores(near)
     tables, own_tables, pair_of, live, square = call(
         functools.partial(prepare_kernel, slots=slots),
@@ -352,28 +389,52 @@
         [],
         2,
     )(device, lengths, block_table, near)
-    send, query = call(
-        project_kernel,
-        [wide, shape((requests, columns), bf16)],
-        [SMEM] + [VMEM] * 7,
-        [VMEM] * 2,
-        [pltpu.VMEM((n * 2 * KVH, HD), f32)],
+    half_kv = shape((requests, KV), f32)
+    normed, kept, away = call(
+        normalize_kernel,
+        [shape((n, requests, width), bf16), half_kv, half_kv],
+        [SMEM] + [VMEM] * 5,
+        [VMEM] * 3,
+        [],
         4,
-    )(device, near, far, square, tables, gain.reshape(1, n * width), w_query, w_kv)
+    )(device, near, far, square, gain.reshape(1, n * width), w_kv)
+    came = swap_cores(away)
+    (query,) = call(
+        query_kernel, [shape((requests, columns), bf16)], [VMEM] * 3, [VMEM], [], 4
+    )(normed, tables, w_query)
+    (send,) = call(
+        gather_kernel,
+        [shape((n // 2, requests, columns + HD), bf16)],
+        [VMEM] * 3,
+        [VMEM],
+        [pltpu.VMEM((requests * 2 * KVH, HD), f32)],
+        4,
+    )(query, kept, came)
+    k_far, v_far = swap_cores(k_cache), swap_cores(v_cache)
     got = exchange(send)
-    rows = pltpu.VMEM(((pairs + 1) * GH, HD), f32)
-    slot_rows = pltpu.VMEM((slots, GH, HD), f32)
+    (near_row,) = call(entry_kernel, [shape((2 * KVH, HD), bf16)], [VMEM] * 2, [VMEM], [], 2)(
+        got, own_tables
+    )
+    far_row = swap_cores(near_row)
+    rows = shape((pairs * CORE_GH, HD), f32)
+    slot_rows = pltpu.VMEM((2 * slots, CORE_GH, HD), f32)
+    run_rows = pltpu.VMEM((2 * (pairs + 1) * CORE_GH, HD), f32)
+    peak, total, mixed = call(
+        attend_kernel,
+        [rows] * 3,
+        [SMEM] * 2 + [VMEM] * 5,
+        [VMEM] * 3,
+        [pltpu.VMEM(((pairs + 1) * CORE_GH, HD), f32)] + [slot_rows] * 4 + [run_rows] * 3,
+        8,
+    )(pair_of, live, got, k_cache, v_cache, k_far, v_far)
     (send,) = call(
-        attend_kernel,
-        [wide],
-        [SMEM] * 2 + [VMEM] * 4,
+        share_kernel,
+        [shape((n // 2, requests, columns + 2 * HD), bf16)],
+        [SMEM] + [VMEM] * 5,
         [VMEM],
-        [rows, slot_rows, pltpu.VMEM((slots, GH, HD), bf16)]
-        + [slot_rows] * 3
-        + [rows] * 3
-        + [pltpu.VMEM((requests, HD), f32)],
-        8,
-    )(pair_of, live, got, k_cache, v_cache, own_tables)
+        [pltpu.VMEM((requests, HD), f32)],
+        4,
+    )(device, peak, total, mixed, near_row, far_row)
     got = exchange(send)
     away, new_entries, attention = call(
         combine_kernel,
@@ -388,7 +449,7 @@
         keep_kernel, [shape(halves.shape, f32)], [SMEM] + [VMEM] * 2, [VMEM], [], 4
     )(device, attention, w_out)
     (send,) = call(join_kernel, [halves], [VMEM] * 2, [VMEM], [], 4)(kept, came)
-    got = exchange_same_core(send)
+    got = exchange(send)
     (attn_out,) = call(add_kernel, [shape((requests, width), bf16)], [VMEM], [VMEM], [], 4)(got)
     return attn_out, new_entries
 

time: 59.6 us -> 58 us (0.973)
  blocking collectives: 47.5 us -> 44.1 us
  Pallas kernels: 9.39 us -> 10.6 us
  starting transfers between devices: 0.01 us -> 0.76 us
    all_to_all x4, blocking collectives: 47.5 us -> 44.1 us  [exchange(): lax.all_to_all(buffer, 'attn', 0, 0, tiled=True, axis_index_groups=groups)]
    pallas_call x2 -> x6, Pallas kernels: 4.75 us -> 5.91 us  [the longest x1 2.71 us: local(): call(attend_kernel, [rows] * 3, [SMEM] * 2 + [VMEM] * 5, [VMEM] * 3, [plt...]
    ppermute x2 -> x6, starting transfers between devices: 0.01 us -> 0.76 us  [swap_cores(): return lax.ppermute(buffer, 'attn', [(i, i ^ 1) for i in range(n)])]
  transfers between devices with their start and end apart: 2 -> 6, of which waited for: 2 -> 2; matrix products, arithmetic and copies ran while one was open for 0% -> 0% of each run, Pallas kernels for 3% -> 13%
where the time goes in v5:
time: 58 us; the launch traced here: 57.6 us
  blocking collectives  44.1 us (76%)
  Pallas kernels  10.6 us (18%)
  between operations  0.78 us (1%)
  starting transfers between devices  0.76 us (1%)
  local copies, waits for them, and re-layouts  0.76 us (1%)
  waiting for transfers between devices  0.62 us (1%)
    all_to_all x4, blocking collectives, exchange(): lax.all_to_all(buffer, 'attn', 0, 0, tiled=True, axis_index_groups=groups)  44.1 us
    pallas_call x1, Pallas kernels, local(): call(attend_kernel, [rows] * 3, [SMEM] * 2 + [VMEM] * 5, [VMEM] * 3, [plt...  2.71 us
    pallas_call x1, Pallas kernels, local(): call(query_kernel, [shape((requests, columns), bf16)], [VMEM] * 3, [VMEM]...  2.33 us
    pallas_call x1, Pallas kernels, local(): call(combine_kernel, [halves, shape((requests, 2 * KV), bf16), shape((req...  1.93 us
    pallas_call x1, Pallas kernels, local(): call(keep_kernel, [shape(halves.shape, f32)], [SMEM] + [VMEM] * 2, [VMEM]...  1.19 us
  transfers between devices with their start and end apart: 6, of which 2 were waited for; matrix products, arithmetic and copies ran while one was open for 0% of the time, Pallas kernels for 13%

profile of v5, /device:TPU:0, one launch (start us, length us, event | category | flops | bytes accessed | tf_op | source)
XLA Modules:
  0.0 57.6 jit_solution(4510437206742023388)
XLA Ops:
  0.6 0.5 collective-permute-start.2
  1.1 0.1 collective-permute-start.3
  1.2 0.7 %copy-done.7 = bf16[8,1024]{1,0:T(8,128)(2,1)S(1)} copy-done((bf16[8,1024]{1,0:T(8,128)(2,1)S(1)}, bf16[8,1024]{1,0:T(8,128)(2,1)}, u32[]{:S(2)}) %copy-start.7) | copy-done | bytes 16408
  2.0 0.0 slice-start
  2.0 0.0 slice-start.1
  2.0 0.0 slice-start.2
  2.0 14.7 %all_to_all.20.near = bf16[8,8,1024]{2,1,0:T(8,128)(2,1)S(1)} all-to-all(bf16[8,8,1024]{2,1,0:T(8,128)(2,1)S(1)} %shard_map.104), channel_id=1, replica_groups={{0,2,4,6,8,10,12,14},{1,3,5,7,9,11,13,15},{16,18,20,22,24,26,28,30},{17..., dimensions={0} | all-to-all | bytes 262144 | tf_op jit(solution)/shard_map/all_to_all | solution.py:37
  16.7 0.0 collective-permute-start
  16.7 0.9 %shard_map.105 = (f32[16,128]{1,0:T(8,128)S(1)}, f32[2,128]{1,0:T(2,128)S(1)}, s32[1,128]{1,0:T(1,128)S(1)}, s32[1,128]{1,0:T(1,128)S(1)}, f32[8,1024]{1,0:T(8,128)S(1)}) custom-call(s32[1]{0:T(128)} %bitcast.device, s32[8]{0:T(128)S(1)} %copy-done.6, s32[8,4,32]{2,1,0:T(4,128)S(1)} %copy-done.5, bf16[8,8,1024]{2,1,0:T(8,128)(2,1)S(1)} %all_to_all.20.near), custom_call_target="tpu_custom_call" | custom-call | tf_op jit(solution)/shard_map/pallas_call | solution.py:378
  17.6 0.5 collective-permute-done.far
  18.0 0.5 shard_map.106
  18.6 0.2 collective-permute-start.1
  18.7 2.3 %shard_map.107.query = bf16[8,512]{1,0:T(8,128)(2,1)S(1)} custom-call(bf16[16,8,1024]{2,1,0:T(8,128)(2,1)S(1)} %get-tuple-element.19.normed, f32[16,128]{1,0:T(8,128)S(1)} %get-tuple-element.20.tables, bf16[16384,512]{1,0:T(8,128)(2,1)S(1)} %copy-done), custom_call_target="tpu_custom_call" | custom-call | tf_op jit(solution)/shard_map/pallas_call | solution.py:402
  21.1 0.0 collective-permute-done.1.came
  21.1 9.4 %all_to_all.21.got = bf16[8,8,640]{2,1,0:T(8,128)(2,1)S(1)} all-to-all(bf16[8,8,640]{2,1,0:T(8,128)(2,1)S(1)} %shard_map.108), channel_id=1, replica_groups={{0,2,4,6,8,10,12,14},{1,3,5,7,9,11,13,15},{16,18,20,22,24,26,28,30},{17..., dimensions={0} | all-to-all | bytes 163840 | tf_op jit(solution)/shard_map/all_to_all | solution.py:37
  30.5 0.1 shard_map.110.near_row
  30.7 2.7 %shard_map.109 = (f32[256,128]{1,0:T(8,128)S(1)}, f32[256,128]{1,0:T(8,128)S(1)}, f32[256,128]{1,0:T(8,128)S(1)}) custom-call(s32[1,128]{1,0:T(1,128)S(1)} %get-tuple-element.16.pair_of, s32[1,128]{1,0:T(1,128)S(1)} %get-tuple-element.17.live, bf16[8,8,640]{2,1,0:T(8,128)(2,1)S(1)} %all_to_all.21.got, bf16[36,128,128]{2,1,0:T(8,128)(2,1)S(1)} %copy-done.2, ...), custom_call_target="tpu_custom_call" | custom-call | tf_op jit(solution)/shard_map/pallas_call | solution.py:422
  33.4 0.2 shard_map.111
  33.6 9.8 %all_to_all.22.got = bf16[8,8,768]{2,1,0:T(8,128)(2,1)S(1)} all-to-all(bf16[8,8,768]{2,1,0:T(8,128)(2,1)S(1)} %shard_map.111), channel_id=1, replica_groups={{0,2,4,6,8,10,12,14},{1,3,5,7,9,11,13,15},{16,18,20,22,24,26,28,30},{17..., dimensions={0} | all-to-all | bytes 196608 | tf_op jit(solution)/shard_map/all_to_all | solution.py:37
  43.5 1.9 %shard_map.112 = (bf16[8,8,1024]{2,1,0:T(8,128)(2,1)S(1)}, bf16[8,1024]{1,0:T(8,128)(2,1)}, bf16[8,512]{1,0:T(8,128)(2,1)S(1)}) custom-call(s32[1]{0:T(128)} %bitcast.device, bf16[8,8,768]{2,1,0:T(8,128)(2,1)S(1)} %all_to_all.22.got, bf16[8,512]{1,0:T(8,128)(2,1)S(1)} %shard_map.107.query, bf16[512,16384]{1,0:T(8,128)(2,1)S(1)} %bitcast.3), custom_call_target="tpu_custom_call" | custom-call | tf_op jit(solution)/shard_map/pallas_call | solution.py:439
  45.4 1.2 %shard_map.113.kept = f32[8,8,1024]{2,1,0:T(8,128)S(1)} custom-call(s32[1]{0:T(128)} %bitcast.device, bf16[8,512]{1,0:T(8,128)(2,1)S(1)} %get-tuple-element.27.attention, bf16[512,16384]{1,0:T(8,128)(2,1)S(1)} %bitcast.3), custom_call_target="tpu_custom_call" | custom-call | tf_op jit(solution)/shard_map/pallas_call | solution.py:448
  46.6 0.2 collective-permute-done.5.came
  46.8 10.2 %all_to_all.23.got = bf16[8,8,1024]{2,1,0:T(8,128)(2,1)S(1)} all-to-all(bf16[8,8,1024]{2,1,0:T(8,128)(2,1)S(1)} %shard_map.114), channel_id=1, replica_groups={{0,2,4,6,8,10,12,14},{1,3,5,7,9,11,13,15},{16,18,20,22,24,26,28,30},{17..., dimensions={0} | all-to-all | bytes 262144 | tf_op jit(solution)/shard_map/all_to_all | solution.py:37
  57.0 0.6 %shard_map.115 = bf16[8,1024]{1,0:T(8,128)(2,1)} custom-call(bf16[8,8,1024]{2,1,0:T(8,128)(2,1)S(1)} %all_to_all.23.got), custom_call_target="tpu_custom_call" | custom-call | tf_op jit(solution)/shard_map/pallas_call | solution.py:453
  (29 shorter events, 0.1 us)
Async XLA Ops:
  0.6 30.0 %collective-permute-start.2 = (bf16[36,128,128]{2,1,0:T(8,128)(2,1)}, bf16[36,128,128]{2,1,0:T(8,128)(2,1)S(1)}, u32[]{:S(2)}, u32[]{:S(2)}) collective-permute-start(bf16[36,128,128]{2,1,0:T(8,128)(2,1)} %k_near.1), channel_id=1, source_target_pairs={{0,1},{1,0},{2,3},{3,2},{4,5},{5,4},{6,7},{7,6},{8,9},{9,8},{10,11... | collective-permute-start | bytes 3538952 | tf_op jit(solution)/shard_map/ppermute | solution.py:42
  1.1 29.5 %collective-permute-start.3 = (bf16[36,128,128]{2,1,0:T(8,128)(2,1)}, bf16[36,128,128]{2,1,0:T(8,128)(2,1)S(1)}, u32[]{:S(2)}, u32[]{:S(2)}) collective-permute-start(bf16[36,128,128]{2,1,0:T(8,128)(2,1)} %v_near.1), channel_id=1, source_target_pairs={{0,1},{1,0},{2,3},{3,2},{4,5},{5,4},{6,7},{7,6},{8,9},{9,8},{10,11... | collective-permute-start | bytes 3538952 | tf_op jit(solution)/shard_map/ppermute | solution.py:42
  1.2 0.7 %copy-start.7 = (bf16[8,1024]{1,0:T(8,128)(2,1)S(1)}, bf16[8,1024]{1,0:T(8,128)(2,1)}, u32[]{:S(2)}) copy-start(bf16[8,1024]{1,0:T(8,128)(2,1)} %hidden.1) | copy-start | bytes 49156
  1.9 14.7 %copy-start.5 = (s32[8,4,32]{2,1,0:T(4,128)S(1)}, s32[8,4,32]{2,1,0:T(4,128)}, u32[]{:S(2)}) copy-start(s32[8,4,32]{2,1,0:T(4,128)} %table.1) | copy-start | bytes 12292
  2.0 14.7 %copy-start.6 = (s32[8]{0:T(128)S(1)}, s32[8]{0:T(128)}, u32[]{:S(2)}) copy-start(s32[8]{0:T(128)} %lengths.1) | copy-start | bytes 100
  2.0 16.1 %copy-start.1 = (bf16[1024,1024]{1,0:T(8,128)(2,1)S(1)}, bf16[1024,1024]{1,0:T(8,128)(2,1)}, u32[]{:S(2)}) copy-start(bf16[1024,1024]{1,0:T(8,128)(2,1)} %w_kv.1) | copy-start | bytes 6291460
  2.0 16.1 %copy-start.4 = (f32[16384]{0:T(1024)S(1)}, f32[16384]{0:T(1024)}, u32[]{:S(2)}) copy-start(f32[16384]{0:T(1024)} %param.10) | copy-start | bytes 196612
  2.0 16.8 %copy-start = (bf16[16384,512]{1,0:T(8,128)(2,1)S(1)}, bf16[16384,512]{1,0:T(8,128)(2,1)}, u32[]{:S(2)}) copy-start(bf16[16384,512]{1,0:T(8,128)(2,1)} %w_query.1) | copy-start | bytes 50331652
  2.0 41.5 %slice-start = ((s8[16777216]{0:T(1024)(128)(4,1)}), s8[4194304]{0:T(1024)(128)(4,1)S(1)}, s32[]{:S(2)}) async-start(s8[16777216]{0:T(1024)(128)(4,1)} %bitcast.2), calls=%async_computation.4 | async-start | bytes 8388608
  2.0 41.5 %slice-start.1 = ((s8[16777216]{0:T(1024)(128)(4,1)}), s8[4194304]{0:T(1024)(128)(4,1)S(1)}, s32[]{:S(2)}) async-start(s8[16777216]{0:T(1024)(128)(4,1)} %bitcast.2), calls=%async_computation.5 | async-start | bytes 8388608
  2.0 41.5 %slice-start.2 = ((s8[16777216]{0:T(1024)(128)(4,1)}), s8[4194304]{0:T(1024)(128)(4,1)S(1)}, s32[]{:S(2)}) async-start(s8[16777216]{0:T(1024)(128)(4,1)} %bitcast.2), calls=%async_computation.6 | async-start | bytes 8388608
  16.7 1.3 %collective-permute-start = (bf16[8,8,1024]{2,1,0:T(8,128)(2,1)S(1)}, bf16[8,8,1024]{2,1,0:T(8,128)(2,1)S(1)}, u32[]{:S(2)}, u32[]{:S(2)}) collective-permute-start(bf16[8,8,1024]{2,1,0:T(8,128)(2,1)S(1)} %all_to_all.20.near), channel_id=1, source_target_pairs={{0,1},{1,0},{2,3},{3,2},{4,5},{5,4},{6,7},{7,6},{8,9},{9,8},{10,11... | collective-permute-start | bytes 393224 | tf_op jit(solution)/shard_map/ppermute | solution.py:42
  18.0 25.4 %slice-start.3 = ((s8[16777216]{0:T(1024)(128)(4,1)}), s8[4194304]{0:T(1024)(128)(4,1)S(1)}, s32[]{:S(2)}) async-start(s8[16777216]{0:T(1024)(128)(4,1)} %bitcast.2), calls=%async_computation.7 | async-start | bytes 8388608
  18.6 2.5 %collective-permute-start.1 = (f32[8,512]{1,0:T(8,128)S(1)}, f32[8,512]{1,0:T(8,128)S(1)}, u32[]{:S(2)}, u32[]{:S(2)}) collective-permute-start(f32[8,512]{1,0:T(8,128)S(1)} %get-tuple-element.22), channel_id=1, source_target_pairs={{0,1},{1,0},{2,3},{3,2},{4,5},{5,4},{6,7},{7,6},{8,9},{9,8},{10,11... | collective-permute-start | bytes 49160 | tf_op jit(solution)/shard_map/ppermute | solution.py:42
  18.7 11.9 %copy-start.2 = (bf16[36,128,128]{2,1,0:T(8,128)(2,1)S(1)}, bf16[36,128,128]{2,1,0:T(8,128)(2,1)}, u32[]{:S(2)}) copy-start(bf16[36,128,128]{2,1,0:T(8,128)(2,1)} %k_near.1) | copy-start | bytes 3538948
  18.7 11.9 %copy-start.3 = (bf16[36,128,128]{2,1,0:T(8,128)(2,1)S(1)}, bf16[36,128,128]{2,1,0:T(8,128)(2,1)}, u32[]{:S(2)}) copy-start(bf16[36,128,128]{2,1,0:T(8,128)(2,1)} %v_near.1) | copy-start | bytes 3538948
  30.6 2.8 %collective-permute-start.4 = (bf16[8,128]{1,0:T(8,128)(2,1)S(1)}, bf16[8,128]{1,0:T(8,128)(2,1)S(1)}, u32[]{:S(2)}, u32[]{:S(2)}) collective-permute-start(bf16[8,128]{1,0:T(8,128)(2,1)S(1)} %shard_map.110.near_row), channel_id=1, source_target_pairs={{0,1},{1,0},{2,3},{3,2},{4,5},{5,4},{6,7},{7,6},{8,9},{9,8},{10,11... | collective-permute-start | bytes 6152 | tf_op jit(solution)/shard_map/ppermute | solution.py:42
  45.4 1.3 %collective-permute-start.5 = (bf16[8,8,1024]{2,1,0:T(8,128)(2,1)S(1)}, bf16[8,8,1024]{2,1,0:T(8,128)(2,1)S(1)}, u32[]{:S(2)}, u32[]{:S(2)}) collective-permute-start(bf16[8,8,1024]{2,1,0:T(8,128)(2,1)S(1)} %get-tuple-element.28), channel_id=1, source_target_pairs={{0,1},{1,0},{2,3},{3,2},{4,5},{5,4},{6,7},{7,6},{8,9},{9,8},{10,11... | collective-permute-start | bytes 393224 | tf_op jit(solution)/shard_map/ppermute | solution.py:42

commit v6 on v5

--- a/solution.py
+++ b/solution.py
@@ -51,11 +51,15 @@
         send[j] = hidden[...]
 
 
-def add_kernel(got, out):
+def add_kernel(got, entries, out, new_entries):
     total = got[0].astype(f32)
     for src in range(1, got.shape[0]):
         total = total + got[src].astype(f32)
     out[...] = total.astype(bf16)
+    requests = out.shape[0]
+    for i in range(2 * KVH):
+        rows = slice(i * requests, (i + 1) * requests)
+        new_entries[:, i * HD : (i + 1) * HD] = entries[rows, :].astype(bf16)
 
 
 def place_slots(device, lengths, table, pair_of, live, slots, total):
@@ -186,12 +190,15 @@
         start = (pair_of[0, s] + side * (pairs + 1)) * CORE_GH
         return pl.ds(pl.multiple_of(start, CORE_GH), CORE_GH)
 
-    for s in range(2 * slots):
-        keys = k_near[s] if s < slots else k_far[s - slots]
-        slot_score[s] = lax.dot_general(
-            queries[rows_of(s), :].astype(bf16), keys, (((1,), (1,)), ((), ())),
+    for s in range(0, 2 * slots, 2):
+        pages, at = (k_near, s) if s < slots else (k_far, s - slots)
+        both = jnp.concatenate([queries[rows_of(s), :], queries[rows_of(s + 1), :]], axis=0)
+        scores = lax.dot_general(
+            both.astype(bf16), pages[at : at + 2].reshape(2 * page, HD), (((1,), (1,)), ((), ())),
             preferred_element_type=f32,
         )
+        slot_score[s] = scores[:CORE_GH, :page]
+        slot_score[s + 1] = scores[CORE_GH:, page:]
     shape = (CORE_GH, HD)
     places = lane_of((CORE_GH, page))
     for s in range(2 * slots):
@@ -205,27 +212,30 @@
     for s in range(2 * slots):
         values = v_near[s] if s < slots else v_far[s - slots]
         slot_out[s] = jnp.dot(slot_score[s].astype(bf16), values, preferred_element_type=f32)
-    for side in range(2):
-        running = jnp.full(shape, lowest, f32)
-        for s in range(side * slots, (side + 1) * slots):
-            if s > side * slots:
+    running = [jnp.full(shape, lowest, f32)] * 2
+    for t in range(slots):
+        for side in range(2):
+            s = side * slots + t
+            if t:
                 same = pair_of[0, s] == pair_of[0, s - 1]
-                running = jnp.where(same, running, lowest)
-            running = jnp.maximum(slot_peak[s], running)
-            run_peak[rows_of(s, side), :] = running
-    for side in range(2):
-        sum_total = jnp.zeros(shape, f32)
-        sum_mixed = jnp.zeros(shape, f32)
-        for s in range(side * slots, (side + 1) * slots):
-            if s > side * slots:
+                running[side] = jnp.where(same, running[side], lowest)
+            running[side] = jnp.maximum(slot_peak[s], running[side])
+            run_peak[rows_of(s, side), :] = running[side]
+    for s in range(2 * slots):
+        slot_peak[s] = jnp.exp(slot_peak[s] - run_peak[rows_of(s, s // slots), :])
+    sum_total = [jnp.zeros(shape, f32)] * 2
+    sum_mixed = [jnp.zeros(shape, f32)] * 2
+    for t in range(slots):
+        for side in range(2):
+            s = side * slots + t
+            if t:
                 keep = jnp.where(pair_of[0, s] == pair_of[0, s - 1], 1.0, 0.0)
-                sum_total, sum_mixed = keep * sum_total, keep * sum_mixed
-            rows = rows_of(s, side)
-            factor = jnp.exp(slot_peak[s] - run_peak[rows, :])
-            sum_total = sum_total + factor * slot_total[s]
-            sum_mixed = sum_mixed + factor * slot_out[s]
-            run_total[rows, :] = sum_total
-            run_mixed[rows, :] = sum_mixed
+                sum_total[side], sum_mixed[side] = keep * sum_total[side], keep * sum_mixed[side]
+            rows, factor = rows_of(s, side), slot_peak[s]
+            sum_total[side] = sum_total[side] + factor * slot_total[s]
+            sum_mixed[side] = sum_mixed[side] + factor * slot_out[s]
+            run_total[rows, :] = sum_total[side]
+            run_mixed[rows, :] = sum_mixed[side]
     for pair in range(pairs):
         here = slice(pair * CORE_GH, (pair + 1) * CORE_GH)
         first = run_peak[here, :]
@@ -280,7 +290,7 @@
         ).astype(result.dtype)
 
 
-def combine_kernel(device, got, query, w_out, away, new_entries, attention, entries):
+def combine_kernel(device, got, query, w_out, away, attention, entries):
     chips, requests, wide = got.shape
     columns = wide - 2 * HD
     heads = columns // HD
@@ -288,10 +298,6 @@
     for request in range(requests):
         block = got[request, : 2 * KVH, columns + HD :].astype(f32)
         entries[pl.ds(request, 2 * KVH, stride=requests), :] = block
-    for i in range(2 * KVH):
-        new_entries[:, i * HD : (i + 1) * HD] = entries[
-            i * requests : (i + 1) * requests, :
-        ].astype(bf16)
 
     def own(c, half):
         start = (lax.div(device[0] * heads + c, GH) + half * KVH) * requests
@@ -360,10 +366,12 @@
     columns = w_query.shape[1]
     slots = k_cache.shape[0]
     pairs = requests * KVH
-    assert 2 * requests == n
+    assert 2 * requests == n and slots % 2 == 0 and 2 * slots <= HD
 
     shape = jax.ShapeDtypeStruct
     halves = shape((n // 2, requests, width), bf16)
+    device, k_cache, v_cache = lax.optimization_barrier((device, k_cache, v_cache))
+    k_far, v_far = swap_cores(k_cache), swap_cores(v_cache)
     (send,) = call(
         spread_kernel,
         [halves],
@@ -410,7 +418,6 @@
         [pltpu.VMEM((requests * 2 * KVH, HD), f32)],
         4,
     )(query, kept, came)
-    k_far, v_far = swap_cores(k_cache), swap_cores(v_cache)
     got = exchange(send)
     (near_row,) = call(entry_kernel, [shape((2 * KVH, HD), bf16)], [VMEM] * 2, [VMEM], [], 2)(
         got, own_tables
@@ -436,12 +443,16 @@
         4,
     )(device, peak, total, mixed, near_row, far_row)
     got = exchange(send)
-    away, new_entries, attention = call(
+    away, attention, entries = call(
         combine_kernel,
-        [halves, shape((requests, 2 * KV), bf16), shape((requests, columns), bf16)],
+        [
+            halves,
+            shape((requests, columns), bf16),
+            shape((2 * KVH * requests, HD), f32),
+        ],
         [SMEM] + [VMEM] * 3,
         [VMEM] * 3,
-        [pltpu.VMEM((2 * KVH * requests, HD), f32)],
+        [],
         4,
     )(device, got, query, w_out)
     came = swap_cores(away)
@@ -450,7 +461,14 @@
     )(device, attention, w_out)
     (send,) = call(join_kernel, [halves], [VMEM] * 2, [VMEM], [], 4)(kept, came)
     got = exchange(send)
-    (attn_out,) = call(add_kernel, [shape((requests, width), bf16)], [VMEM], [VMEM], [], 4)(got)
+    attn_out, new_entries = call(
+        add_kernel,
+        [shape((requests, width), bf16), shape((requests, 2 * KV), bf16)],
+        [VMEM] * 2,
+        [VMEM] * 2,
+        [],
+        4,
+    )(got, entries)
     return attn_out, new_entries
 
 

time: 58 us -> 56.9 us (0.981)
  Pallas kernels: 10.6 us -> 9.49 us
    pallas_call x1, Pallas kernels: 2.71 us -> 2.11 us  [local(): call(attend_kernel, [rows] * 3, [SMEM] * 2 + [VMEM] * 5, [VMEM] * 3, [plt...]
where the time goes in v6:
time: 56.9 us; the launch traced here: 56.5 us
  blocking collectives  44.1 us (78%)
  Pallas kernels  9.49 us (17%)
  between operations  0.78 us (1%)
  local copies, waits for them, and re-layouts  0.76 us (1%)
  starting transfers between devices  0.76 us (1%)
  waiting for transfers between devices  0.62 us (1%)
    all_to_all x4, blocking collectives, exchange(): lax.all_to_all(buffer, 'attn', 0, 0, tiled=True, axis_index_groups=groups)  44.1 us
    pallas_call x1, Pallas kernels, local(): call(query_kernel, [shape((requests, columns), bf16)], [VMEM] * 3, [VMEM]...  2.33 us
    pallas_call x1, Pallas kernels, local(): call(attend_kernel, [rows] * 3, [SMEM] * 2 + [VMEM] * 5, [VMEM] * 3, [plt...  2.11 us
    pallas_call x1, Pallas kernels, local(): call(combine_kernel, [halves, shape((requests, columns), bf16), shape((2...  1.43 us
    pallas_call x1, Pallas kernels, local(): call(keep_kernel, [shape(halves.shape, f32)], [SMEM] + [VMEM] * 2, [VMEM]...  1.2 us
  transfers between devices with their start and end apart: 6, of which 2 were waited for; matrix products, arithmetic and copies ran while one was open for 0% of the time, Pallas kernels for 13%

profile of v6, /device:TPU:0, one launch (start us, length us, event | category | flops | bytes accessed | tf_op | source)
XLA Modules:
  0.0 56.5 jit_solution(2653178958646419424)
XLA Ops:
  0.7 0.5 collective-permute-start.2
  1.2 0.1 collective-permute-start.3
  1.3 0.7 %copy-done.7 = bf16[8,1024]{1,0:T(8,128)(2,1)S(1)} copy-done((bf16[8,1024]{1,0:T(8,128)(2,1)S(1)}, bf16[8,1024]{1,0:T(8,128)(2,1)}, u32[]{:S(2)}) %copy-start.7) | copy-done | bytes 16408
  2.0 0.0 slice-start.2
  2.0 14.7 %all_to_all.20.near = bf16[8,8,1024]{2,1,0:T(8,128)(2,1)S(1)} all-to-all(bf16[8,8,1024]{2,1,0:T(8,128)(2,1)S(1)} %shard_map.104), channel_id=1, replica_groups={{0,2,4,6,8,10,12,14},{1,3,5,7,9,11,13,15},{16,18,20,22,24,26,28,30},{17..., dimensions={0} | all-to-all | bytes 262144 | tf_op jit(solution)/shard_map/all_to_all | solution.py:37
  16.7 0.0 collective-permute-start
  16.7 0.9 %shard_map.105 = (f32[16,128]{1,0:T(8,128)S(1)}, f32[2,128]{1,0:T(2,128)S(1)}, s32[1,128]{1,0:T(1,128)S(1)}, s32[1,128]{1,0:T(1,128)S(1)}, f32[8,1024]{1,0:T(8,128)S(1)}) custom-call(s32[1]{0:T(128)} %bitcast.device, s32[8]{0:T(128)S(1)} %copy-done.6, s32[8,4,32]{2,1,0:T(4,128)S(1)} %copy-done.5, bf16[8,8,1024]{2,1,0:T(8,128)(2,1)S(1)} %all_to_all.20.near), custom_call_target="tpu_custom_call" | custom-call | tf_op jit(solution)/shard_map/pallas_call | solution.py:386
  17.6 0.5 collective-permute-done.far
  18.0 0.5 shard_map.106
  18.6 0.2 collective-permute-start.1
  18.7 2.3 %shard_map.107.query = bf16[8,512]{1,0:T(8,128)(2,1)S(1)} custom-call(bf16[16,8,1024]{2,1,0:T(8,128)(2,1)S(1)} %get-tuple-element.23.normed, f32[16,128]{1,0:T(8,128)S(1)} %get-tuple-element.24.tables, bf16[16384,512]{1,0:T(8,128)(2,1)S(1)} %copy-done), custom_call_target="tpu_custom_call" | custom-call | tf_op jit(solution)/shard_map/pallas_call | solution.py:410
  21.1 0.0 collective-permute-done.1.came
  21.1 9.4 %all_to_all.21.got = bf16[8,8,640]{2,1,0:T(8,128)(2,1)S(1)} all-to-all(bf16[8,8,640]{2,1,0:T(8,128)(2,1)S(1)} %shard_map.108), channel_id=1, replica_groups={{0,2,4,6,8,10,12,14},{1,3,5,7,9,11,13,15},{16,18,20,22,24,26,28,30},{17..., dimensions={0} | all-to-all | bytes 163840 | tf_op jit(solution)/shard_map/all_to_all | solution.py:37
  30.5 0.1 shard_map.110.near_row
  30.6 0.0 collective-permute-start.4
  30.7 2.1 %shard_map.109 = (f32[256,128]{1,0:T(8,128)S(1)}, f32[256,128]{1,0:T(8,128)S(1)}, f32[256,128]{1,0:T(8,128)S(1)}) custom-call(s32[1,128]{1,0:T(1,128)S(1)} %get-tuple-element.20.pair_of, s32[1,128]{1,0:T(1,128)S(1)} %get-tuple-element.21.live, bf16[8,8,640]{2,1,0:T(8,128)(2,1)S(1)} %all_to_all.21.got, bf16[36,128,128]{2,1,0:T(8,128)(2,1)S(1)} %copy-done.2, ...), custom_call_target="tpu_custom_call" | custom-call | tf_op jit(solution)/shard_map/pallas_call | solution.py:429
  32.8 0.2 shard_map.111
  33.0 9.8 %all_to_all.22.got = bf16[8,8,768]{2,1,0:T(8,128)(2,1)S(1)} all-to-all(bf16[8,8,768]{2,1,0:T(8,128)(2,1)S(1)} %shard_map.111), channel_id=1, replica_groups={{0,2,4,6,8,10,12,14},{1,3,5,7,9,11,13,15},{16,18,20,22,24,26,28,30},{17..., dimensions={0} | all-to-all | bytes 196608 | tf_op jit(solution)/shard_map/all_to_all | solution.py:37
  42.9 1.4 %shard_map.112 = (bf16[8,8,1024]{2,1,0:T(8,128)(2,1)S(1)}, bf16[8,512]{1,0:T(8,128)(2,1)S(1)}, f32[64,128]{1,0:T(8,128)S(1)}) custom-call(s32[1]{0:T(128)} %bitcast.device, bf16[8,8,768]{2,1,0:T(8,128)(2,1)S(1)} %all_to_all.22.got, bf16[8,512]{1,0:T(8,128)(2,1)S(1)} %shard_map.107.query, bf16[512,16384]{1,0:T(8,128)(2,1)S(1)} %bitcast.3), custom_call_target="tpu_custom_call" | custom-call | tf_op jit(solution)/shard_map/pallas_call | solution.py:446
  44.3 0.0 collective-permute-start.5
  44.3 1.2 %shard_map.113.kept = f32[8,8,1024]{2,1,0:T(8,128)S(1)} custom-call(s32[1]{0:T(128)} %bitcast.device, bf16[8,512]{1,0:T(8,128)(2,1)S(1)} %get-tuple-element.33.attention, bf16[512,16384]{1,0:T(8,128)(2,1)S(1)} %bitcast.3), custom_call_target="tpu_custom_call" | custom-call | tf_op jit(solution)/shard_map/pallas_call | solution.py:459
  45.5 0.2 collective-permute-done.5.came
  45.7 10.2 %all_to_all.23.got = bf16[8,8,1024]{2,1,0:T(8,128)(2,1)S(1)} all-to-all(bf16[8,8,1024]{2,1,0:T(8,128)(2,1)S(1)} %shard_map.114), channel_id=1, replica_groups={{0,2,4,6,8,10,12,14},{1,3,5,7,9,11,13,15},{16,18,20,22,24,26,28,30},{17..., dimensions={0} | all-to-all | bytes 262144 | tf_op jit(solution)/shard_map/all_to_all | solution.py:37
  55.9 0.6 %shard_map.115 = (bf16[8,1024]{1,0:T(8,128)(2,1)}, bf16[8,1024]{1,0:T(8,128)(2,1)}) custom-call(bf16[8,8,1024]{2,1,0:T(8,128)(2,1)S(1)} %all_to_all.23.got, f32[64,128]{1,0:T(8,128)S(1)} %get-tuple-element.35.entries), custom_call_target="tpu_custom_call" | custom-call | tf_op jit(solution)/shard_map/pallas_call | solution.py:464
  (29 shorter events, 0.1 us)
Async XLA Ops:
  0.6 16.1 %copy-start.5 = (s32[8,4,32]{2,1,0:T(4,128)S(1)}, s32[8,4,32]{2,1,0:T(4,128)}, u32[]{:S(2)}) copy-start(s32[8,4,32]{2,1,0:T(4,128)} %table.1) | copy-start | bytes 12292
  0.6 16.0 %copy-start.6 = (s32[8]{0:T(128)S(1)}, s32[8]{0:T(128)}, u32[]{:S(2)}) copy-start(s32[8]{0:T(128)} %lengths.1) | copy-start | bytes 100
  0.7 17.4 %copy-start.4 = (f32[16384]{0:T(1024)S(1)}, f32[16384]{0:T(1024)}, u32[]{:S(2)}) copy-start(f32[16384]{0:T(1024)} %param.10) | copy-start | bytes 196612
  0.7 30.0 %collective-permute-start.2 = (bf16[36,128,128]{2,1,0:T(8,128)(2,1)}, bf16[36,128,128]{2,1,0:T(8,128)(2,1)S(1)}, u32[]{:S(2)}, u32[]{:S(2)}) collective-permute-start(bf16[36,128,128]{2,1,0:T(8,128)(2,1)} %k_near), channel_id=1, source_target_pairs={{0,1},{1,0},{2,3},{3,2},{4,5},{5,4},{6,7},{7,6},{8,9},{9,8},{10,11... | collective-permute-start | bytes 3538952 | tf_op jit(solution)/shard_map/ppermute | solution.py:42
  1.2 29.5 %collective-permute-start.3 = (bf16[36,128,128]{2,1,0:T(8,128)(2,1)}, bf16[36,128,128]{2,1,0:T(8,128)(2,1)S(1)}, u32[]{:S(2)}, u32[]{:S(2)}) collective-permute-start(bf16[36,128,128]{2,1,0:T(8,128)(2,1)} %v_near), channel_id=1, source_target_pairs={{0,1},{1,0},{2,3},{3,2},{4,5},{5,4},{6,7},{7,6},{8,9},{9,8},{10,11... | collective-permute-start | bytes 3538952 | tf_op jit(solution)/shard_map/ppermute | solution.py:42
  1.3 0.7 %copy-start.7 = (bf16[8,1024]{1,0:T(8,128)(2,1)S(1)}, bf16[8,1024]{1,0:T(8,128)(2,1)}, u32[]{:S(2)}) copy-start(bf16[8,1024]{1,0:T(8,128)(2,1)} %hidden.1) | copy-start | bytes 49156
  2.0 16.1 %copy-start.1 = (bf16[1024,1024]{1,0:T(8,128)(2,1)S(1)}, bf16[1024,1024]{1,0:T(8,128)(2,1)}, u32[]{:S(2)}) copy-start(bf16[1024,1024]{1,0:T(8,128)(2,1)} %w_kv.1) | copy-start | bytes 6291460
  2.0 16.7 %copy-start = (bf16[16384,512]{1,0:T(8,128)(2,1)S(1)}, bf16[16384,512]{1,0:T(8,128)(2,1)}, u32[]{:S(2)}) copy-start(bf16[16384,512]{1,0:T(8,128)(2,1)} %w_query.1) | copy-start | bytes 50331652
  2.0 40.9 %slice-start = ((s8[16777216]{0:T(1024)(128)(4,1)}), s8[4194304]{0:T(1024)(128)(4,1)S(1)}, s32[]{:S(2)}) async-start(s8[16777216]{0:T(1024)(128)(4,1)} %bitcast.2), calls=%async_computation.4 | async-start | bytes 8388608
  2.0 40.9 %slice-start.1 = ((s8[16777216]{0:T(1024)(128)(4,1)}), s8[4194304]{0:T(1024)(128)(4,1)S(1)}, s32[]{:S(2)}) async-start(s8[16777216]{0:T(1024)(128)(4,1)} %bitcast.2), calls=%async_computation.5 | async-start | bytes 8388608
  2.0 40.9 %slice-start.2 = ((s8[16777216]{0:T(1024)(128)(4,1)}), s8[4194304]{0:T(1024)(128)(4,1)S(1)}, s32[]{:S(2)}) async-start(s8[16777216]{0:T(1024)(128)(4,1)} %bitcast.2), calls=%async_computation.6 | async-start | bytes 8388608
  16.7 1.3 %collective-permute-start = (bf16[8,8,1024]{2,1,0:T(8,128)(2,1)S(1)}, bf16[8,8,1024]{2,1,0:T(8,128)(2,1)S(1)}, u32[]{:S(2)}, u32[]{:S(2)}) collective-permute-start(bf16[8,8,1024]{2,1,0:T(8,128)(2,1)S(1)} %all_to_all.20.near), channel_id=1, source_target_pairs={{0,1},{1,0},{2,3},{3,2},{4,5},{5,4},{6,7},{7,6},{8,9},{9,8},{10,11... | collective-permute-start | bytes 393224 | tf_op jit(solution)/shard_map/ppermute | solution.py:42
  18.0 24.8 %slice-start.3 = ((s8[16777216]{0:T(1024)(128)(4,1)}), s8[4194304]{0:T(1024)(128)(4,1)S(1)}, s32[]{:S(2)}) async-start(s8[16777216]{0:T(1024)(128)(4,1)} %bitcast.2), calls=%async_computation.7 | async-start | bytes 8388608
  18.6 2.5 %collective-permute-start.1 = (f32[8,512]{1,0:T(8,128)S(1)}, f32[8,512]{1,0:T(8,128)S(1)}, u32[]{:S(2)}, u32[]{:S(2)}) collective-permute-start(f32[8,512]{1,0:T(8,128)S(1)} %get-tuple-element.26), channel_id=1, source_target_pairs={{0,1},{1,0},{2,3},{3,2},{4,5},{5,4},{6,7},{7,6},{8,9},{9,8},{10,11... | collective-permute-start | bytes 49160 | tf_op jit(solution)/shard_map/ppermute | solution.py:42
  18.7 11.9 %copy-start.2 = (bf16[36,128,128]{2,1,0:T(8,128)(2,1)S(1)}, bf16[36,128,128]{2,1,0:T(8,128)(2,1)}, u32[]{:S(2)}) copy-start(bf16[36,128,128]{2,1,0:T(8,128)(2,1)} %k_near) | copy-start | bytes 3538948
  18.7 11.9 %copy-start.3 = (bf16[36,128,128]{2,1,0:T(8,128)(2,1)S(1)}, bf16[36,128,128]{2,1,0:T(8,128)(2,1)}, u32[]{:S(2)}) copy-start(bf16[36,128,128]{2,1,0:T(8,128)(2,1)} %v_near) | copy-start | bytes 3538948
  30.6 2.2 %collective-permute-start.4 = (bf16[8,128]{1,0:T(8,128)(2,1)S(1)}, bf16[8,128]{1,0:T(8,128)(2,1)S(1)}, u32[]{:S(2)}, u32[]{:S(2)}) collective-permute-start(bf16[8,128]{1,0:T(8,128)(2,1)S(1)} %shard_map.110.near_row), channel_id=1, source_target_pairs={{0,1},{1,0},{2,3},{3,2},{4,5},{5,4},{6,7},{7,6},{8,9},{9,8},{10,11... | collective-permute-start | bytes 6152 | tf_op jit(solution)/shard_map/ppermute | solution.py:42
  44.3 1.4 %collective-permute-start.5 = (bf16[8,8,1024]{2,1,0:T(8,128)(2,1)S(1)}, bf16[8,8,1024]{2,1,0:T(8,128)(2,1)S(1)}, u32[]{:S(2)}, u32[]{:S(2)}) collective-permute-start(bf16[8,8,1024]{2,1,0:T(8,128)(2,1)S(1)} %get-tuple-element.34), channel_id=1, source_target_pairs={{0,1},{1,0},{2,3},{3,2},{4,5},{5,4},{6,7},{7,6},{8,9},{9,8},{10,11... | collective-permute-start | bytes 393224 | tf_op jit(solution)/shard_map/ppermute | solution.py:42

commit v7 on v6

--- a/solution.py
+++ b/solution.py
@@ -209,9 +209,17 @@
         slot_score[s] = weights
         slot_peak[s] = jnp.broadcast_to(top, shape)
         slot_total[s] = jnp.broadcast_to(jnp.sum(weights, axis=1, keepdims=True), shape)
-    for s in range(2 * slots):
-        values = v_near[s] if s < slots else v_far[s - slots]
-        slot_out[s] = jnp.dot(slot_score[s].astype(bf16), values, preferred_element_type=f32)
+    nothing = jnp.zeros((CORE_GH, page), f32)
+    for s in range(0, 2 * slots, 2):
+        pages, at = (v_near, s) if s < slots else (v_far, s - slots)
+        upper = jnp.concatenate([slot_score[s], nothing], axis=1)
+        lower = jnp.concatenate([nothing, slot_score[s + 1]], axis=1)
+        both = jnp.concatenate([upper, lower], axis=0).astype(bf16)
+        out = jnp.dot(
+            both, pages[at : at + 2].reshape(2 * page, HD), preferred_element_type=f32
+        )
+        slot_out[s] = out[:CORE_GH]
+        slot_out[s + 1] = out[CORE_GH:]
     running = [jnp.full(shape, lowest, f32)] * 2
     for t in range(slots):
         for side in range(2):

time: 56.9 us -> 56.6 us (level)
  transfers between devices with their start and end apart: 6 -> 6, of which waited for: 2 -> 2; matrix products, arithmetic and copies ran while one was open for 0% -> 0% of each run, Pallas kernels for 13% -> 12%
where the time goes in v7:
time: 56.6 us; the launch traced here: 56.2 us
  blocking collectives  44.1 us (78%)
  Pallas kernels  9.19 us (16%)
  between operations  0.78 us (1%)
  local copies, waits for them, and re-layouts  0.76 us (1%)
  starting transfers between devices  0.76 us (1%)
  waiting for transfers between devices  0.62 us (1%)
    all_to_all x4, blocking collectives, exchange(): lax.all_to_all(buffer, 'attn', 0, 0, tiled=True, axis_index_groups=groups)  44.1 us
    pallas_call x1, Pallas kernels, local(): call(query_kernel, [shape((requests, columns), bf16)], [VMEM] * 3, [VMEM]...  2.33 us
    pallas_call x1, Pallas kernels, local(): call(attend_kernel, [rows] * 3, [SMEM] * 2 + [VMEM] * 5, [VMEM] * 3, [plt...  1.81 us
    pallas_call x1, Pallas kernels, local(): call(combine_kernel, [halves, shape((requests, columns), bf16), shape((2...  1.43 us
    pallas_call x1, Pallas kernels, local(): call(keep_kernel, [shape(halves.shape, f32)], [SMEM] + [VMEM] * 2, [VMEM]...  1.2 us
  transfers between devices with their start and end apart: 6, of which 2 were waited for; matrix products, arithmetic and copies ran while one was open for 0% of the time, Pallas kernels for 12%

profile of v7, /device:TPU:0, one launch (start us, length us, event | category | flops | bytes accessed | tf_op | source)
XLA Modules:
  0.0 56.2 jit_solution(15995141768859571571)
XLA Ops:
  0.7 0.5 collective-permute-start.2
  1.2 0.1 collective-permute-start.3
  1.3 0.7 %copy-done.7 = bf16[8,1024]{1,0:T(8,128)(2,1)S(1)} copy-done((bf16[8,1024]{1,0:T(8,128)(2,1)S(1)}, bf16[8,1024]{1,0:T(8,128)(2,1)}, u32[]{:S(2)}) %copy-start.7) | copy-done | bytes 16408
  2.0 0.0 slice-start.2
  2.0 14.7 %all_to_all.20.near = bf16[8,8,1024]{2,1,0:T(8,128)(2,1)S(1)} all-to-all(bf16[8,8,1024]{2,1,0:T(8,128)(2,1)S(1)} %shard_map.104), channel_id=1, replica_groups={{0,2,4,6,8,10,12,14},{1,3,5,7,9,11,13,15},{16,18,20,22,24,26,28,30},{17..., dimensions={0} | all-to-all | bytes 262144 | tf_op jit(solution)/shard_map/all_to_all | solution.py:37
  16.7 0.0 collective-permute-start
  16.7 0.9 %shard_map.105 = (f32[16,128]{1,0:T(8,128)S(1)}, f32[2,128]{1,0:T(2,128)S(1)}, s32[1,128]{1,0:T(1,128)S(1)}, s32[1,128]{1,0:T(1,128)S(1)}, f32[8,1024]{1,0:T(8,128)S(1)}) custom-call(s32[1]{0:T(128)} %bitcast.device, s32[8]{0:T(128)S(1)} %copy-done.6, s32[8,4,32]{2,1,0:T(4,128)S(1)} %copy-done.5, bf16[8,8,1024]{2,1,0:T(8,128)(2,1)S(1)} %all_to_all.20.near), custom_call_target="tpu_custom_call" | custom-call | tf_op jit(solution)/shard_map/pallas_call | solution.py:394
  17.6 0.5 collective-permute-done.far
  18.0 0.5 shard_map.106
  18.6 0.2 collective-permute-start.1
  18.7 2.3 %shard_map.107.query = bf16[8,512]{1,0:T(8,128)(2,1)S(1)} custom-call(bf16[16,8,1024]{2,1,0:T(8,128)(2,1)S(1)} %get-tuple-element.23.normed, f32[16,128]{1,0:T(8,128)S(1)} %get-tuple-element.24.tables, bf16[16384,512]{1,0:T(8,128)(2,1)S(1)} %copy-done), custom_call_target="tpu_custom_call" | custom-call | tf_op jit(solution)/shard_map/pallas_call | solution.py:418
  21.1 9.4 %all_to_all.21.got = bf16[8,8,640]{2,1,0:T(8,128)(2,1)S(1)} all-to-all(bf16[8,8,640]{2,1,0:T(8,128)(2,1)S(1)} %shard_map.108), channel_id=1, replica_groups={{0,2,4,6,8,10,12,14},{1,3,5,7,9,11,13,15},{16,18,20,22,24,26,28,30},{17..., dimensions={0} | all-to-all | bytes 163840 | tf_op jit(solution)/shard_map/all_to_all | solution.py:37
  30.5 0.1 shard_map.110.near_row
  30.6 0.0 collective-permute-start.4
  30.6 0.0 collective-permute-done.3.v_far
  30.7 1.8 %shard_map.109 = (f32[256,128]{1,0:T(8,128)S(1)}, f32[256,128]{1,0:T(8,128)S(1)}, f32[256,128]{1,0:T(8,128)S(1)}) custom-call(s32[1,128]{1,0:T(1,128)S(1)} %get-tuple-element.20.pair_of, s32[1,128]{1,0:T(1,128)S(1)} %get-tuple-element.21.live, bf16[8,8,640]{2,1,0:T(8,128)(2,1)S(1)} %all_to_all.21.got, bf16[36,128,128]{2,1,0:T(8,128)(2,1)S(1)} %copy-done.2, ...), custom_call_target="tpu_custom_call" | custom-call | tf_op jit(solution)/shard_map/pallas_call | solution.py:437
  32.5 0.2 shard_map.111
  32.7 9.8 %all_to_all.22.got = bf16[8,8,768]{2,1,0:T(8,128)(2,1)S(1)} all-to-all(bf16[8,8,768]{2,1,0:T(8,128)(2,1)S(1)} %shard_map.111), channel_id=1, replica_groups={{0,2,4,6,8,10,12,14},{1,3,5,7,9,11,13,15},{16,18,20,22,24,26,28,30},{17..., dimensions={0} | all-to-all | bytes 196608 | tf_op jit(solution)/shard_map/all_to_all | solution.py:37
  42.6 1.4 %shard_map.112 = (bf16[8,8,1024]{2,1,0:T(8,128)(2,1)S(1)}, bf16[8,512]{1,0:T(8,128)(2,1)S(1)}, f32[64,128]{1,0:T(8,128)S(1)}) custom-call(s32[1]{0:T(128)} %bitcast.device, bf16[8,8,768]{2,1,0:T(8,128)(2,1)S(1)} %all_to_all.22.got, bf16[8,512]{1,0:T(8,128)(2,1)S(1)} %shard_map.107.query, bf16[512,16384]{1,0:T(8,128)(2,1)S(1)} %bitcast.3), custom_call_target="tpu_custom_call" | custom-call | tf_op jit(solution)/shard_map/pallas_call | solution.py:454
  44.0 0.0 collective-permute-start.5
  44.0 1.2 %shard_map.113.kept = f32[8,8,1024]{2,1,0:T(8,128)S(1)} custom-call(s32[1]{0:T(128)} %bitcast.device, bf16[8,512]{1,0:T(8,128)(2,1)S(1)} %get-tuple-element.33.attention, bf16[512,16384]{1,0:T(8,128)(2,1)S(1)} %bitcast.3), custom_call_target="tpu_custom_call" | custom-call | tf_op jit(solution)/shard_map/pallas_call | solution.py:467
  45.2 0.2 collective-permute-done.5.came
  45.4 10.2 %all_to_all.23.got = bf16[8,8,1024]{2,1,0:T(8,128)(2,1)S(1)} all-to-all(bf16[8,8,1024]{2,1,0:T(8,128)(2,1)S(1)} %shard_map.114), channel_id=1, replica_groups={{0,2,4,6,8,10,12,14},{1,3,5,7,9,11,13,15},{16,18,20,22,24,26,28,30},{17..., dimensions={0} | all-to-all | bytes 262144 | tf_op jit(solution)/shard_map/all_to_all | solution.py:37
  55.6 0.6 %shard_map.115 = (bf16[8,1024]{1,0:T(8,128)(2,1)}, bf16[8,1024]{1,0:T(8,128)(2,1)}) custom-call(bf16[8,8,1024]{2,1,0:T(8,128)(2,1)S(1)} %all_to_all.23.got, f32[64,128]{1,0:T(8,128)S(1)} %get-tuple-element.35.entries), custom_call_target="tpu_custom_call" | custom-call | tf_op jit(solution)/shard_map/pallas_call | solution.py:472
  (29 shorter events, 0.1 us)
Async XLA Ops:
  0.6 16.1 %copy-start.5 = (s32[8,4,32]{2,1,0:T(4,128)S(1)}, s32[8,4,32]{2,1,0:T(4,128)}, u32[]{:S(2)}) copy-start(s32[8,4,32]{2,1,0:T(4,128)} %table.1) | copy-start | bytes 12292
  0.6 16.0 %copy-start.6 = (s32[8]{0:T(128)S(1)}, s32[8]{0:T(128)}, u32[]{:S(2)}) copy-start(s32[8]{0:T(128)} %lengths.1) | copy-start | bytes 100
  0.7 17.4 %copy-start.4 = (f32[16384]{0:T(1024)S(1)}, f32[16384]{0:T(1024)}, u32[]{:S(2)}) copy-start(f32[16384]{0:T(1024)} %param.10) | copy-start | bytes 196612
  0.7 30.0 %collective-permute-start.2 = (bf16[36,128,128]{2,1,0:T(8,128)(2,1)}, bf16[36,128,128]{2,1,0:T(8,128)(2,1)S(1)}, u32[]{:S(2)}, u32[]{:S(2)}) collective-permute-start(bf16[36,128,128]{2,1,0:T(8,128)(2,1)} %k_near), channel_id=1, source_target_pairs={{0,1},{1,0},{2,3},{3,2},{4,5},{5,4},{6,7},{7,6},{8,9},{9,8},{10,11... | collective-permute-start | bytes 3538952 | tf_op jit(solution)/shard_map/ppermute | solution.py:42
  1.2 29.5 %collective-permute-start.3 = (bf16[36,128,128]{2,1,0:T(8,128)(2,1)}, bf16[36,128,128]{2,1,0:T(8,128)(2,1)S(1)}, u32[]{:S(2)}, u32[]{:S(2)}) collective-permute-start(bf16[36,128,128]{2,1,0:T(8,128)(2,1)} %v_near), channel_id=1, source_target_pairs={{0,1},{1,0},{2,3},{3,2},{4,5},{5,4},{6,7},{7,6},{8,9},{9,8},{10,11... | collective-permute-start | bytes 3538952 | tf_op jit(solution)/shard_map/ppermute | solution.py:42
  1.3 0.7 %copy-start.7 = (bf16[8,1024]{1,0:T(8,128)(2,1)S(1)}, bf16[8,1024]{1,0:T(8,128)(2,1)}, u32[]{:S(2)}) copy-start(bf16[8,1024]{1,0:T(8,128)(2,1)} %hidden.1) | copy-start | bytes 49156
  2.0 16.1 %copy-start.1 = (bf16[1024,1024]{1,0:T(8,128)(2,1)S(1)}, bf16[1024,1024]{1,0:T(8,128)(2,1)}, u32[]{:S(2)}) copy-start(bf16[1024,1024]{1,0:T(8,128)(2,1)} %w_kv.1) | copy-start | bytes 6291460
  2.0 16.7 %copy-start = (bf16[16384,512]{1,0:T(8,128)(2,1)S(1)}, bf16[16384,512]{1,0:T(8,128)(2,1)}, u32[]{:S(2)}) copy-start(bf16[16384,512]{1,0:T(8,128)(2,1)} %w_query.1) | copy-start | bytes 50331652
  2.0 40.6 %slice-start = ((s8[16777216]{0:T(1024)(128)(4,1)}), s8[4194304]{0:T(1024)(128)(4,1)S(1)}, s32[]{:S(2)}) async-start(s8[16777216]{0:T(1024)(128)(4,1)} %bitcast.2), calls=%async_computation.4 | async-start | bytes 8388608
  2.0 40.6 %slice-start.1 = ((s8[16777216]{0:T(1024)(128)(4,1)}), s8[4194304]{0:T(1024)(128)(4,1)S(1)}, s32[]{:S(2)}) async-start(s8[16777216]{0:T(1024)(128)(4,1)} %bitcast.2), calls=%async_computation.5 | async-start | bytes 8388608
  2.0 40.6 %slice-start.2 = ((s8[16777216]{0:T(1024)(128)(4,1)}), s8[4194304]{0:T(1024)(128)(4,1)S(1)}, s32[]{:S(2)}) async-start(s8[16777216]{0:T(1024)(128)(4,1)} %bitcast.2), calls=%async_computation.6 | async-start | bytes 8388608
  16.7 1.3 %collective-permute-start = (bf16[8,8,1024]{2,1,0:T(8,128)(2,1)S(1)}, bf16[8,8,1024]{2,1,0:T(8,128)(2,1)S(1)}, u32[]{:S(2)}, u32[]{:S(2)}) collective-permute-start(bf16[8,8,1024]{2,1,0:T(8,128)(2,1)S(1)} %all_to_all.20.near), channel_id=1, source_target_pairs={{0,1},{1,0},{2,3},{3,2},{4,5},{5,4},{6,7},{7,6},{8,9},{9,8},{10,11... | collective-permute-start | bytes 393224 | tf_op jit(solution)/shard_map/ppermute | solution.py:42
  18.0 24.5 %slice-start.3 = ((s8[16777216]{0:T(1024)(128)(4,1)}), s8[4194304]{0:T(1024)(128)(4,1)S(1)}, s32[]{:S(2)}) async-start(s8[16777216]{0:T(1024)(128)(4,1)} %bitcast.2), calls=%async_computation.7 | async-start | bytes 8388608
  18.6 2.5 %collective-permute-start.1 = (f32[8,512]{1,0:T(8,128)S(1)}, f32[8,512]{1,0:T(8,128)S(1)}, u32[]{:S(2)}, u32[]{:S(2)}) collective-permute-start(f32[8,512]{1,0:T(8,128)S(1)} %get-tuple-element.26), channel_id=1, source_target_pairs={{0,1},{1,0},{2,3},{3,2},{4,5},{5,4},{6,7},{7,6},{8,9},{9,8},{10,11... | collective-permute-start | bytes 49160 | tf_op jit(solution)/shard_map/ppermute | solution.py:42
  18.7 11.9 %copy-start.2 = (bf16[36,128,128]{2,1,0:T(8,128)(2,1)S(1)}, bf16[36,128,128]{2,1,0:T(8,128)(2,1)}, u32[]{:S(2)}) copy-start(bf16[36,128,128]{2,1,0:T(8,128)(2,1)} %k_near) | copy-start | bytes 3538948
  18.7 11.9 %copy-start.3 = (bf16[36,128,128]{2,1,0:T(8,128)(2,1)S(1)}, bf16[36,128,128]{2,1,0:T(8,128)(2,1)}, u32[]{:S(2)}) copy-start(bf16[36,128,128]{2,1,0:T(8,128)(2,1)} %v_near) | copy-start | bytes 3538948
  30.6 1.9 %collective-permute-start.4 = (bf16[8,128]{1,0:T(8,128)(2,1)S(1)}, bf16[8,128]{1,0:T(8,128)(2,1)S(1)}, u32[]{:S(2)}, u32[]{:S(2)}) collective-permute-start(bf16[8,128]{1,0:T(8,128)(2,1)S(1)} %shard_map.110.near_row), channel_id=1, source_target_pairs={{0,1},{1,0},{2,3},{3,2},{4,5},{5,4},{6,7},{7,6},{8,9},{9,8},{10,11... | collective-permute-start | bytes 6152 | tf_op jit(solution)/shard_map/ppermute | solution.py:42
  44.0 1.4 %collective-permute-start.5 = (bf16[8,8,1024]{2,1,0:T(8,128)(2,1)S(1)}, bf16[8,8,1024]{2,1,0:T(8,128)(2,1)S(1)}, u32[]{:S(2)}, u32[]{:S(2)}) collective-permute-start(bf16[8,8,1024]{2,1,0:T(8,128)(2,1)S(1)} %get-tuple-element.34), channel_id=1, source_target_pairs={{0,1},{1,0},{2,3},{3,2},{4,5},{5,4},{6,7},{7,6},{8,9},{9,8},{10,11... | collective-permute-start | bytes 393224 | tf_op jit(solution)/shard_map/ppermute | solution.py:42

commit v8 on v7

--- a/solution.py
+++ b/solution.py
@@ -378,8 +378,6 @@
 
     shape = jax.ShapeDtypeStruct
     halves = shape((n // 2, requests, width), bf16)
-    device, k_cache, v_cache = lax.optimization_barrier((device, k_cache, v_cache))
-    k_far, v_far = swap_cores(k_cache), swap_cores(v_cache)
     (send,) = call(
         spread_kernel,
         [halves],
@@ -426,6 +424,8 @@
         [pltpu.VMEM((requests * 2 * KVH, HD), f32)],
         4,
     )(query, kept, came)
+    send, k_cache, v_cache = lax.optimization_barrier((send, k_cache, v_cache))
+    k_far, v_far = swap_cores(k_cache), swap_cores(v_cache)
     got = exchange(send)
     (near_row,) = call(entry_kernel, [shape((2 * KVH, HD), bf16)], [VMEM] * 2, [VMEM], [], 2)(
         got, own_tables

time: 56.6 us -> 56.6 us (level)
  transfers between devices with their start and end apart: 6 -> 6, of which waited for: 2 -> 2; matrix products, arithmetic and copies ran while one was open for 0% -> 0% of each run, Pallas kernels for 12% -> 11%
where the time goes in v8:
time: 56.6 us; the launch traced here: 56.2 us
  blocking collectives  44.1 us (78%)
  Pallas kernels  9.18 us (16%)
  between operations  0.78 us (1%)
  local copies, waits for them, and re-layouts  0.76 us (1%)
  starting transfers between devices  0.74 us (1%)
  waiting for transfers between devices  0.62 us (1%)
    all_to_all x4, blocking collectives, exchange(): lax.all_to_all(buffer, 'attn', 0, 0, tiled=True, axis_index_groups=groups)  44.1 us
    pallas_call x1, Pallas kernels, local(): call(query_kernel, [shape((requests, columns), bf16)], [VMEM] * 3, [VMEM]...  2.33 us
    pallas_call x1, Pallas kernels, local(): call(attend_kernel, [rows] * 3, [SMEM] * 2 + [VMEM] * 5, [VMEM] * 3, [plt...  1.8 us
    pallas_call x1, Pallas kernels, local(): call(combine_kernel, [halves, shape((requests, columns), bf16), shape((2...  1.43 us
    pallas_call x1, Pallas kernels, local(): call(keep_kernel, [shape(halves.shape, f32)], [SMEM] + [VMEM] * 2, [VMEM]...  1.2 us
  transfers between devices with their start and end apart: 6, of which 2 were waited for; matrix products, arithmetic and copies ran while one was open for 0% of the time, Pallas kernels for 11%

profile of v8, /device:TPU:0, one launch (start us, length us, event | category | flops | bytes accessed | tf_op | source)
XLA Modules:
  0.0 56.2 jit_solution(1399673760390827679)
XLA Ops:
  0.6 0.7 %copy-done.7 = bf16[8,1024]{1,0:T(8,128)(2,1)S(1)} copy-done((bf16[8,1024]{1,0:T(8,128)(2,1)S(1)}, bf16[8,1024]{1,0:T(8,128)(2,1)}, u32[]{:S(2)}) %copy-start.7) | copy-done | bytes 16408
  1.4 0.0 slice-start
  1.4 0.0 slice-start.1
  1.4 0.0 slice-start.2
  1.4 14.7 %all_to_all.20.near = bf16[8,8,1024]{2,1,0:T(8,128)(2,1)S(1)} all-to-all(bf16[8,8,1024]{2,1,0:T(8,128)(2,1)S(1)} %shard_map.104), channel_id=1, replica_groups={{0,2,4,6,8,10,12,14},{1,3,5,7,9,11,13,15},{16,18,20,22,24,26,28,30},{17..., dimensions={0} | all-to-all | bytes 262144 | tf_op jit(solution)/shard_map/all_to_all | solution.py:37
  16.1 0.0 collective-permute-start
  16.1 0.9 %shard_map.105 = (f32[16,128]{1,0:T(8,128)S(1)}, f32[2,128]{1,0:T(2,128)S(1)}, s32[1,128]{1,0:T(1,128)S(1)}, s32[1,128]{1,0:T(1,128)S(1)}, f32[8,1024]{1,0:T(8,128)S(1)}) custom-call(s32[1]{0:T(128)} %bitcast.device, s32[8]{0:T(128)S(1)} %copy-done.6, s32[8,4,32]{2,1,0:T(4,128)S(1)} %copy-done.5, bf16[8,8,1024]{2,1,0:T(8,128)(2,1)S(1)} %all_to_all.20.near), custom_call_target="tpu_custom_call" | custom-call | tf_op jit(solution)/shard_map/pallas_call | solution.py:392
  17.0 0.5 collective-permute-done.far
  17.5 0.5 shard_map.106
  18.0 0.2 collective-permute-start.1
  18.2 2.3 %shard_map.107.query = bf16[8,512]{1,0:T(8,128)(2,1)S(1)} custom-call(bf16[16,8,1024]{2,1,0:T(8,128)(2,1)S(1)} %get-tuple-element.22.normed, f32[16,128]{1,0:T(8,128)S(1)} %get-tuple-element.23.tables, bf16[16384,512]{1,0:T(8,128)(2,1)S(1)} %copy-done), custom_call_target="tpu_custom_call" | custom-call | tf_op jit(solution)/shard_map/pallas_call | solution.py:416
  20.5 0.4 collective-permute-start.2
  21.0 0.1 collective-permute-start.3
  21.1 9.4 %all_to_all.21.got = bf16[8,8,640]{2,1,0:T(8,128)(2,1)S(1)} all-to-all(bf16[8,8,640]{2,1,0:T(8,128)(2,1)S(1)} %shard_map.108), channel_id=1, replica_groups={{0,2,4,6,8,10,12,14},{1,3,5,7,9,11,13,15},{16,18,20,22,24,26,28,30},{17..., dimensions={0} | all-to-all | bytes 163840 | tf_op jit(solution)/shard_map/all_to_all | solution.py:37
  30.5 0.1 shard_map.110.near_row
  30.6 0.0 collective-permute-done.2.k_far
  30.7 1.8 %shard_map.109 = (f32[256,128]{1,0:T(8,128)S(1)}, f32[256,128]{1,0:T(8,128)S(1)}, f32[256,128]{1,0:T(8,128)S(1)}) custom-call(s32[1,128]{1,0:T(1,128)S(1)} %get-tuple-element.19.pair_of, s32[1,128]{1,0:T(1,128)S(1)} %get-tuple-element.20.live, bf16[8,8,640]{2,1,0:T(8,128)(2,1)S(1)} %all_to_all.21.got, bf16[36,128,128]{2,1,0:T(8,128)(2,1)S(1)} %copy-done.2, ...), custom_call_target="tpu_custom_call" | custom-call | tf_op jit(solution)/shard_map/pallas_call | solution.py:437
  32.5 0.2 shard_map.111
  32.7 9.8 %all_to_all.22.got = bf16[8,8,768]{2,1,0:T(8,128)(2,1)S(1)} all-to-all(bf16[8,8,768]{2,1,0:T(8,128)(2,1)S(1)} %shard_map.111), channel_id=1, replica_groups={{0,2,4,6,8,10,12,14},{1,3,5,7,9,11,13,15},{16,18,20,22,24,26,28,30},{17..., dimensions={0} | all-to-all | bytes 196608 | tf_op jit(solution)/shard_map/all_to_all | solution.py:37
  42.6 1.4 %shard_map.112 = (bf16[8,8,1024]{2,1,0:T(8,128)(2,1)S(1)}, bf16[8,512]{1,0:T(8,128)(2,1)S(1)}, f32[64,128]{1,0:T(8,128)S(1)}) custom-call(s32[1]{0:T(128)} %bitcast.device, bf16[8,8,768]{2,1,0:T(8,128)(2,1)S(1)} %all_to_all.22.got, bf16[8,512]{1,0:T(8,128)(2,1)S(1)} %shard_map.107.query, bf16[512,16384]{1,0:T(8,128)(2,1)S(1)} %bitcast.3), custom_call_target="tpu_custom_call" | custom-call | tf_op jit(solution)/shard_map/pallas_call | solution.py:454
  44.0 1.2 %shard_map.113.kept = f32[8,8,1024]{2,1,0:T(8,128)S(1)} custom-call(s32[1]{0:T(128)} %bitcast.device, bf16[8,512]{1,0:T(8,128)(2,1)S(1)} %get-tuple-element.33.attention, bf16[512,16384]{1,0:T(8,128)(2,1)S(1)} %bitcast.3), custom_call_target="tpu_custom_call" | custom-call | tf_op jit(solution)/shard_map/pallas_call | solution.py:467
  45.2 0.2 collective-permute-done.5.came
  45.4 10.2 %all_to_all.23.got = bf16[8,8,1024]{2,1,0:T(8,128)(2,1)S(1)} all-to-all(bf16[8,8,1024]{2,1,0:T(8,128)(2,1)S(1)} %shard_map.114), channel_id=1, replica_groups={{0,2,4,6,8,10,12,14},{1,3,5,7,9,11,13,15},{16,18,20,22,24,26,28,30},{17..., dimensions={0} | all-to-all | bytes 262144 | tf_op jit(solution)/shard_map/all_to_all | solution.py:37
  55.6 0.6 %shard_map.115 = (bf16[8,1024]{1,0:T(8,128)(2,1)}, bf16[8,1024]{1,0:T(8,128)(2,1)}) custom-call(bf16[8,8,1024]{2,1,0:T(8,128)(2,1)S(1)} %all_to_all.23.got, f32[64,128]{1,0:T(8,128)S(1)} %get-tuple-element.35.entries), custom_call_target="tpu_custom_call" | custom-call | tf_op jit(solution)/shard_map/pallas_call | solution.py:472
  (29 shorter events, 0.1 us)
Async XLA Ops:
  0.6 0.7 %copy-start.7 = (bf16[8,1024]{1,0:T(8,128)(2,1)S(1)}, bf16[8,1024]{1,0:T(8,128)(2,1)}, u32[]{:S(2)}) copy-start(bf16[8,1024]{1,0:T(8,128)(2,1)} %hidden.1) | copy-start | bytes 49156
  1.4 14.8 %copy-start.5 = (s32[8,4,32]{2,1,0:T(4,128)S(1)}, s32[8,4,32]{2,1,0:T(4,128)}, u32[]{:S(2)}) copy-start(s32[8,4,32]{2,1,0:T(4,128)} %table.1) | copy-start | bytes 12292
  1.4 14.8 %copy-start.6 = (s32[8]{0:T(128)S(1)}, s32[8]{0:T(128)}, u32[]{:S(2)}) copy-start(s32[8]{0:T(128)} %lengths.1) | copy-start | bytes 100
  1.4 16.1 %copy-start.1 = (bf16[1024,1024]{1,0:T(8,128)(2,1)S(1)}, bf16[1024,1024]{1,0:T(8,128)(2,1)}, u32[]{:S(2)}) copy-start(bf16[1024,1024]{1,0:T(8,128)(2,1)} %w_kv.1) | copy-start | bytes 6291460
  1.4 16.1 %copy-start.4 = (f32[16384]{0:T(1024)S(1)}, f32[16384]{0:T(1024)}, u32[]{:S(2)}) copy-start(f32[16384]{0:T(1024)} %param.10) | copy-start | bytes 196612
  1.4 16.8 %copy-start = (bf16[16384,512]{1,0:T(8,128)(2,1)S(1)}, bf16[16384,512]{1,0:T(8,128)(2,1)}, u32[]{:S(2)}) copy-start(bf16[16384,512]{1,0:T(8,128)(2,1)} %w_query.1) | copy-start | bytes 50331652
  1.4 41.2 %slice-start = ((s8[16777216]{0:T(1024)(128)(4,1)}), s8[4194304]{0:T(1024)(128)(4,1)S(1)}, s32[]{:S(2)}) async-start(s8[16777216]{0:T(1024)(128)(4,1)} %bitcast.2), calls=%async_computation.4 | async-start | bytes 8388608
  1.4 41.1 %slice-start.1 = ((s8[16777216]{0:T(1024)(128)(4,1)}), s8[4194304]{0:T(1024)(128)(4,1)S(1)}, s32[]{:S(2)}) async-start(s8[16777216]{0:T(1024)(128)(4,1)} %bitcast.2), calls=%async_computation.5 | async-start | bytes 8388608
  1.4 41.1 %slice-start.2 = ((s8[16777216]{0:T(1024)(128)(4,1)}), s8[4194304]{0:T(1024)(128)(4,1)S(1)}, s32[]{:S(2)}) async-start(s8[16777216]{0:T(1024)(128)(4,1)} %bitcast.2), calls=%async_computation.6 | async-start | bytes 8388608
  16.1 1.3 %collective-permute-start = (bf16[8,8,1024]{2,1,0:T(8,128)(2,1)S(1)}, bf16[8,8,1024]{2,1,0:T(8,128)(2,1)S(1)}, u32[]{:S(2)}, u32[]{:S(2)}) collective-permute-start(bf16[8,8,1024]{2,1,0:T(8,128)(2,1)S(1)} %all_to_all.20.near), channel_id=1, source_target_pairs={{0,1},{1,0},{2,3},{3,2},{4,5},{5,4},{6,7},{7,6},{8,9},{9,8},{10,11... | collective-permute-start | bytes 393224 | tf_op jit(solution)/shard_map/ppermute | solution.py:42
  17.5 25.1 %slice-start.3 = ((s8[16777216]{0:T(1024)(128)(4,1)}), s8[4194304]{0:T(1024)(128)(4,1)S(1)}, s32[]{:S(2)}) async-start(s8[16777216]{0:T(1024)(128)(4,1)} %bitcast.2), calls=%async_computation.7 | async-start | bytes 8388608
  18.0 2.5 %collective-permute-start.1 = (f32[8,512]{1,0:T(8,128)S(1)}, f32[8,512]{1,0:T(8,128)S(1)}, u32[]{:S(2)}, u32[]{:S(2)}) collective-permute-start(f32[8,512]{1,0:T(8,128)S(1)} %get-tuple-element.25), channel_id=1, source_target_pairs={{0,1},{1,0},{2,3},{3,2},{4,5},{5,4},{6,7},{7,6},{8,9},{9,8},{10,11... | collective-permute-start | bytes 49160 | tf_op jit(solution)/shard_map/ppermute | solution.py:42
  18.2 2.4 %copy-start.2 = (bf16[36,128,128]{2,1,0:T(8,128)(2,1)S(1)}, bf16[36,128,128]{2,1,0:T(8,128)(2,1)}, u32[]{:S(2)}) copy-start(bf16[36,128,128]{2,1,0:T(8,128)(2,1)} %k_near) | copy-start | bytes 3538948
  18.2 2.8 %copy-start.3 = (bf16[36,128,128]{2,1,0:T(8,128)(2,1)S(1)}, bf16[36,128,128]{2,1,0:T(8,128)(2,1)}, u32[]{:S(2)}) copy-start(bf16[36,128,128]{2,1,0:T(8,128)(2,1)} %v_near) | copy-start | bytes 3538948
  20.5 10.1 %collective-permute-start.2 = (bf16[36,128,128]{2,1,0:T(8,128)(2,1)S(1)}, bf16[36,128,128]{2,1,0:T(8,128)(2,1)S(1)}, u32[]{:S(2)}, u32[]{:S(2)}) collective-permute-start(bf16[36,128,128]{2,1,0:T(8,128)(2,1)S(1)} %copy-done.2), channel_id=1, source_target_pairs={{0,1},{1,0},{2,3},{3,2},{4,5},{5,4},{6,7},{7,6},{8,9},{9,8},{10,11... | collective-permute-start | bytes 3538952 | tf_op jit(solution)/shard_map/ppermute | solution.py:42
  21.0 9.7 %collective-permute-start.3 = (bf16[36,128,128]{2,1,0:T(8,128)(2,1)S(1)}, bf16[36,128,128]{2,1,0:T(8,128)(2,1)S(1)}, u32[]{:S(2)}, u32[]{:S(2)}) collective-permute-start(bf16[36,128,128]{2,1,0:T(8,128)(2,1)S(1)} %copy-done.3), channel_id=1, source_target_pairs={{0,1},{1,0},{2,3},{3,2},{4,5},{5,4},{6,7},{7,6},{8,9},{9,8},{10,11... | collective-permute-start | bytes 3538952 | tf_op jit(solution)/shard_map/ppermute | solution.py:42
  30.6 1.8 %collective-permute-start.4 = (bf16[8,128]{1,0:T(8,128)(2,1)S(1)}, bf16[8,128]{1,0:T(8,128)(2,1)S(1)}, u32[]{:S(2)}, u32[]{:S(2)}) collective-permute-start(bf16[8,128]{1,0:T(8,128)(2,1)S(1)} %shard_map.110.near_row), channel_id=1, source_target_pairs={{0,1},{1,0},{2,3},{3,2},{4,5},{5,4},{6,7},{7,6},{8,9},{9,8},{10,11... | collective-permute-start | bytes 6152 | tf_op jit(solution)/shard_map/ppermute | solution.py:42
  44.0 1.4 %collective-permute-start.5 = (bf16[8,8,1024]{2,1,0:T(8,128)(2,1)S(1)}, bf16[8,8,1024]{2,1,0:T(8,128)(2,1)S(1)}, u32[]{:S(2)}, u32[]{:S(2)}) collective-permute-start(bf16[8,8,1024]{2,1,0:T(8,128)(2,1)S(1)} %get-tuple-element.34), channel_id=1, source_target_pairs={{0,1},{1,0},{2,3},{3,2},{4,5},{5,4},{6,7},{7,6},{8,9},{9,8},{10,11... | collective-permute-start | bytes 393224 | tf_op jit(solution)/shard_map/ppermute | solution.py:42

commit v9 on v7

--- a/solution.py
+++ b/solution.py
@@ -62,7 +62,7 @@
         new_entries[:, i * HD : (i + 1) * HD] = entries[rows, :].astype(bf16)
 
 
-def place_slots(device, lengths, table, pair_of, live, slots, total):
+def place_slots(device, lengths, table, placed, slots, total):
     requests = table.shape[0]
     lane = lane_of((1, HD))
     partner = device + 1 - 2 * lax.rem(device, 2)
@@ -79,12 +79,12 @@
             group = group + (offset >= g * pages).astype(jnp.int32)
         pair = jnp.where(here, r * KVH + group, pair)
         alive = jnp.where(here, lengths[r] - 1 - (offset - group * pages) * PAGE, alive)
-    pair_of[...] = pair
-    live[...] = alive
+    placed[0:1, :] = pair
+    placed[1:2, :] = alive
 
 
 def prepare_kernel(
-    device, lengths, table, near, tables, own_tables, pair_of, live, square, *, slots
+    device, lengths, table, near, tables, own_tables, placed, square, *, slots
 ):
     chips, requests, _ = near.shape
     total = jnp.zeros(square.shape, f32)
@@ -105,7 +105,7 @@
     keys_here = lax.rem(device[0], 2) == 0
     own_tables[0:1, :] = jnp.where(keys_here, tables[pl.ds(mine, 1), :], 1.0)
     own_tables[1:2, :] = jnp.where(keys_here, tables[pl.ds(requests + mine, 1), :], 0.0)
-    place_slots(device[0], lengths, table, pair_of, live, slots, 2 * chips * slots)
+    place_slots(device[0], lengths, table, placed, slots, 2 * chips * slots)
 
 
 def normalize_kernel(device, near, far, square, gain, w_kv, normed, kept, away):
@@ -169,7 +169,7 @@
 
 
 def attend_kernel(
-    pair_of, live, got, k_near, v_near, k_far, v_far, peak, total, mixed,
+    placed, got, k_near, v_near, k_far, v_far, peak, total, mixed,
     queries, slot_score, slot_out, slot_peak, slot_total, run_peak, run_total, run_mixed,
 ):
     chips, requests, wide = got.shape
@@ -187,7 +187,7 @@
     run_mixed[...] = jnp.zeros_like(run_mixed)
 
     def rows_of(s, side=0):
-        start = (pair_of[0, s] + side * (pairs + 1)) * CORE_GH
+        start = (placed[0, s] + side * (pairs + 1)) * CORE_GH
         return pl.ds(pl.multiple_of(start, CORE_GH), CORE_GH)
 
     for s in range(0, 2 * slots, 2):
@@ -202,7 +202,7 @@
     shape = (CORE_GH, HD)
     places = lane_of((CORE_GH, page))
     for s in range(2 * slots):
-        alive = places < live[0, s]
+        alive = places < placed[1, s]
         scores = jnp.where(alive, slot_score[s] * score_scale, lowest)
         top = jnp.max(scores, axis=1, keepdims=True)
         weights = jnp.where(alive, jnp.exp(scores - top), 0.0)
@@ -225,7 +225,7 @@
         for side in range(2):
             s = side * slots + t
             if t:
-                same = pair_of[0, s] == pair_of[0, s - 1]
+                same = placed[0, s] == placed[0, s - 1]
                 running[side] = jnp.where(same, running[side], lowest)
             running[side] = jnp.maximum(slot_peak[s], running[side])
             run_peak[rows_of(s, side), :] = running[side]
@@ -237,7 +237,7 @@
         for side in range(2):
             s = side * slots + t
             if t:
-                keep = jnp.where(pair_of[0, s] == pair_of[0, s - 1], 1.0, 0.0)
+                keep = jnp.where(placed[0, s] == placed[0, s - 1], 1.0, 0.0)
                 sum_total[side], sum_mixed[side] = keep * sum_total[side], keep * sum_mixed[side]
             rows, factor = rows_of(s, side), slot_peak[s]
             sum_total[side] = sum_total[side] + factor * slot_total[s]
@@ -391,17 +391,16 @@
     )(device, hidden)
     near = exchange(send)
     far = swap_cores(near)
-    tables, own_tables, pair_of, live, square = call(
+    tables, own_tables, placed, square = call(
         functools.partial(prepare_kernel, slots=slots),
         [
             shape((2 * requests, HD), f32),
             shape((2, HD), f32),
-            shape((1, HD), jnp.int32),
-            shape((1, HD), jnp.int32),
+            shape((2, HD), jnp.int32),
             shape((requests, width), f32),
         ],
         [SMEM] * 3 + [VMEM],
-        [VMEM] * 5,
+        [VMEM] * 4,
         [],
         2,
     )(device, lengths, block_table, near)
@@ -437,11 +436,11 @@
     peak, total, mixed = call(
         attend_kernel,
         [rows] * 3,
-        [SMEM] * 2 + [VMEM] * 5,
+        [SMEM] + [VMEM] * 5,
         [VMEM] * 3,
         [pltpu.VMEM(((pairs + 1) * CORE_GH, HD), f32)] + [slot_rows] * 4 + [run_rows] * 3,
         8,
-    )(pair_of, live, got, k_cache, v_cache, k_far, v_far)
+    )(placed, got, k_cache, v_cache, k_far, v_far)
     (send,) = call(
         share_kernel,
         [shape((n // 2, requests, columns + 2 * HD), bf16)],

time: 56.6 us -> 56.6 us (level)
  no operation moved by 1% of the time
where the time goes in v9:
time: 56.6 us; the launch traced here: 56.2 us
  blocking collectives  44.1 us (78%)
  Pallas kernels  9.19 us (16%)
  between operations  0.78 us (1%)
  local copies, waits for them, and re-layouts  0.76 us (1%)
  starting transfers between devices  0.76 us (1%)
  waiting for transfers between devices  0.62 us (1%)
    all_to_all x4, blocking collectives, exchange(): lax.all_to_all(buffer, 'attn', 0, 0, tiled=True, axis_index_groups=groups)  44.1 us
    pallas_call x1, Pallas kernels, local(): call(query_kernel, [shape((requests, columns), bf16)], [VMEM] * 3, [VMEM]...  2.33 us
    pallas_call x1, Pallas kernels, local(): call(attend_kernel, [rows] * 3, [SMEM] + [VMEM] * 5, [VMEM] * 3, [pltpu.V...  1.8 us
    pallas_call x1, Pallas kernels, local(): call(combine_kernel, [halves, shape((requests, columns), bf16), shape((2...  1.43 us
    pallas_call x1, Pallas kernels, local(): call(keep_kernel, [shape(halves.shape, f32)], [SMEM] + [VMEM] * 2, [VMEM]...  1.2 us
  transfers between devices with their start and end apart: 6, of which 2 were waited for; matrix products, arithmetic and copies ran while one was open for 0% of the time, Pallas kernels for 12%

profile of v9, /device:TPU:0, one launch (start us, length us, event | category | flops | bytes accessed | tf_op | source)
XLA Modules:
  0.0 56.2 jit_solution(12727419183402682339)
XLA Ops:
  0.7 0.5 collective-permute-start.2
  1.2 0.1 collective-permute-start.3
  1.3 0.7 %copy-done.7 = bf16[8,1024]{1,0:T(8,128)(2,1)S(1)} copy-done((bf16[8,1024]{1,0:T(8,128)(2,1)S(1)}, bf16[8,1024]{1,0:T(8,128)(2,1)}, u32[]{:S(2)}) %copy-start.7) | copy-done | bytes 16408
  2.0 0.0 slice-start.2
  2.0 14.7 %all_to_all.20.near = bf16[8,8,1024]{2,1,0:T(8,128)(2,1)S(1)} all-to-all(bf16[8,8,1024]{2,1,0:T(8,128)(2,1)S(1)} %shard_map.104), channel_id=1, replica_groups={{0,2,4,6,8,10,12,14},{1,3,5,7,9,11,13,15},{16,18,20,22,24,26,28,30},{17..., dimensions={0} | all-to-all | bytes 262144 | tf_op jit(solution)/shard_map/all_to_all | solution.py:37
  16.7 0.0 collective-permute-start
  16.7 0.9 %shard_map.105 = (f32[16,128]{1,0:T(8,128)S(1)}, f32[2,128]{1,0:T(2,128)S(1)}, s32[2,128]{1,0:T(2,128)S(1)}, f32[8,1024]{1,0:T(8,128)S(1)}) custom-call(s32[1]{0:T(128)} %bitcast.device, s32[8]{0:T(128)S(1)} %copy-done.6, s32[8,4,32]{2,1,0:T(4,128)S(1)} %copy-done.5, bf16[8,8,1024]{2,1,0:T(8,128)(2,1)S(1)} %all_to_all.20.near), custom_call_target="tpu_custom_call" | custom-call | tf_op jit(solution)/shard_map/pallas_call | solution.py:394
  17.6 0.5 collective-permute-done.far
  18.0 0.5 shard_map.106
  18.6 0.2 collective-permute-start.1
  18.7 2.3 %shard_map.107.query = bf16[8,512]{1,0:T(8,128)(2,1)S(1)} custom-call(bf16[16,8,1024]{2,1,0:T(8,128)(2,1)S(1)} %get-tuple-element.21.normed, f32[16,128]{1,0:T(8,128)S(1)} %get-tuple-element.22.tables, bf16[16384,512]{1,0:T(8,128)(2,1)S(1)} %copy-done), custom_call_target="tpu_custom_call" | custom-call | tf_op jit(solution)/shard_map/pallas_call | solution.py:417
  21.1 0.0 collective-permute-done.1.came
  21.1 9.4 %all_to_all.21.got = bf16[8,8,640]{2,1,0:T(8,128)(2,1)S(1)} all-to-all(bf16[8,8,640]{2,1,0:T(8,128)(2,1)S(1)} %shard_map.108), channel_id=1, replica_groups={{0,2,4,6,8,10,12,14},{1,3,5,7,9,11,13,15},{16,18,20,22,24,26,28,30},{17..., dimensions={0} | all-to-all | bytes 163840 | tf_op jit(solution)/shard_map/all_to_all | solution.py:37
  30.5 0.1 shard_map.110.near_row
  30.6 0.0 collective-permute-done.2.k_far
  30.7 1.8 %shard_map.109 = (f32[256,128]{1,0:T(8,128)S(1)}, f32[256,128]{1,0:T(8,128)S(1)}, f32[256,128]{1,0:T(8,128)S(1)}) custom-call(s32[2,128]{1,0:T(2,128)S(1)} %get-tuple-element.19.placed, bf16[8,8,640]{2,1,0:T(8,128)(2,1)S(1)} %all_to_all.21.got, bf16[36,128,128]{2,1,0:T(8,128)(2,1)S(1)} %copy-done.2, bf16[36,128,128]{2,1,0:T(8,128)(2,1)S(1)} %copy-done.3, ...), custom_call_target="tpu_custom_call" | custom-call | tf_op jit(solution)/shard_map/pallas_call | solution.py:436
  32.5 0.0 collective-permute-done.4.far_row
  32.5 0.2 shard_map.111
  32.7 9.8 %all_to_all.22.got = bf16[8,8,768]{2,1,0:T(8,128)(2,1)S(1)} all-to-all(bf16[8,8,768]{2,1,0:T(8,128)(2,1)S(1)} %shard_map.111), channel_id=1, replica_groups={{0,2,4,6,8,10,12,14},{1,3,5,7,9,11,13,15},{16,18,20,22,24,26,28,30},{17..., dimensions={0} | all-to-all | bytes 196608 | tf_op jit(solution)/shard_map/all_to_all | solution.py:37
  42.6 1.4 %shard_map.112 = (bf16[8,8,1024]{2,1,0:T(8,128)(2,1)S(1)}, bf16[8,512]{1,0:T(8,128)(2,1)S(1)}, f32[64,128]{1,0:T(8,128)S(1)}) custom-call(s32[1]{0:T(128)} %bitcast.device, bf16[8,8,768]{2,1,0:T(8,128)(2,1)S(1)} %all_to_all.22.got, bf16[8,512]{1,0:T(8,128)(2,1)S(1)} %shard_map.107.query, bf16[512,16384]{1,0:T(8,128)(2,1)S(1)} %bitcast.3), custom_call_target="tpu_custom_call" | custom-call | tf_op jit(solution)/shard_map/pallas_call | solution.py:453
  44.0 1.2 %shard_map.113.kept = f32[8,8,1024]{2,1,0:T(8,128)S(1)} custom-call(s32[1]{0:T(128)} %bitcast.device, bf16[8,512]{1,0:T(8,128)(2,1)S(1)} %get-tuple-element.31.attention, bf16[512,16384]{1,0:T(8,128)(2,1)S(1)} %bitcast.3), custom_call_target="tpu_custom_call" | custom-call | tf_op jit(solution)/shard_map/pallas_call | solution.py:466
  45.2 0.2 collective-permute-done.5.came
  45.4 10.2 %all_to_all.23.got = bf16[8,8,1024]{2,1,0:T(8,128)(2,1)S(1)} all-to-all(bf16[8,8,1024]{2,1,0:T(8,128)(2,1)S(1)} %shard_map.114), channel_id=1, replica_groups={{0,2,4,6,8,10,12,14},{1,3,5,7,9,11,13,15},{16,18,20,22,24,26,28,30},{17..., dimensions={0} | all-to-all | bytes 262144 | tf_op jit(solution)/shard_map/all_to_all | solution.py:37
  55.6 0.6 %shard_map.115 = (bf16[8,1024]{1,0:T(8,128)(2,1)}, bf16[8,1024]{1,0:T(8,128)(2,1)}) custom-call(bf16[8,8,1024]{2,1,0:T(8,128)(2,1)S(1)} %all_to_all.23.got, f32[64,128]{1,0:T(8,128)S(1)} %get-tuple-element.33.entries), custom_call_target="tpu_custom_call" | custom-call | tf_op jit(solution)/shard_map/pallas_call | solution.py:471
  (29 shorter events, 0.1 us)
Async XLA Ops:
  0.6 16.1 %copy-start.5 = (s32[8,4,32]{2,1,0:T(4,128)S(1)}, s32[8,4,32]{2,1,0:T(4,128)}, u32[]{:S(2)}) copy-start(s32[8,4,32]{2,1,0:T(4,128)} %table.1) | copy-start | bytes 12292
  0.6 16.0 %copy-start.6 = (s32[8]{0:T(128)S(1)}, s32[8]{0:T(128)}, u32[]{:S(2)}) copy-start(s32[8]{0:T(128)} %lengths.1) | copy-start | bytes 100
  0.7 17.4 %copy-start.4 = (f32[16384]{0:T(1024)S(1)}, f32[16384]{0:T(1024)}, u32[]{:S(2)}) copy-start(f32[16384]{0:T(1024)} %param.10) | copy-start | bytes 196612
  0.7 30.0 %collective-permute-start.2 = (bf16[36,128,128]{2,1,0:T(8,128)(2,1)}, bf16[36,128,128]{2,1,0:T(8,128)(2,1)S(1)}, u32[]{:S(2)}, u32[]{:S(2)}) collective-permute-start(bf16[36,128,128]{2,1,0:T(8,128)(2,1)} %k_near), channel_id=1, source_target_pairs={{0,1},{1,0},{2,3},{3,2},{4,5},{5,4},{6,7},{7,6},{8,9},{9,8},{10,11... | collective-permute-start | bytes 3538952 | tf_op jit(solution)/shard_map/ppermute | solution.py:42
  1.2 29.5 %collective-permute-start.3 = (bf16[36,128,128]{2,1,0:T(8,128)(2,1)}, bf16[36,128,128]{2,1,0:T(8,128)(2,1)S(1)}, u32[]{:S(2)}, u32[]{:S(2)}) collective-permute-start(bf16[36,128,128]{2,1,0:T(8,128)(2,1)} %v_near), channel_id=1, source_target_pairs={{0,1},{1,0},{2,3},{3,2},{4,5},{5,4},{6,7},{7,6},{8,9},{9,8},{10,11... | collective-permute-start | bytes 3538952 | tf_op jit(solution)/shard_map/ppermute | solution.py:42
  1.3 0.7 %copy-start.7 = (bf16[8,1024]{1,0:T(8,128)(2,1)S(1)}, bf16[8,1024]{1,0:T(8,128)(2,1)}, u32[]{:S(2)}) copy-start(bf16[8,1024]{1,0:T(8,128)(2,1)} %hidden.1) | copy-start | bytes 49156
  2.0 16.1 %copy-start.1 = (bf16[1024,1024]{1,0:T(8,128)(2,1)S(1)}, bf16[1024,1024]{1,0:T(8,128)(2,1)}, u32[]{:S(2)}) copy-start(bf16[1024,1024]{1,0:T(8,128)(2,1)} %w_kv.1) | copy-start | bytes 6291460
  2.0 16.7 %copy-start = (bf16[16384,512]{1,0:T(8,128)(2,1)S(1)}, bf16[16384,512]{1,0:T(8,128)(2,1)}, u32[]{:S(2)}) copy-start(bf16[16384,512]{1,0:T(8,128)(2,1)} %w_query.1) | copy-start | bytes 50331652
  2.0 40.6 %slice-start = ((s8[16777216]{0:T(1024)(128)(4,1)}), s8[4194304]{0:T(1024)(128)(4,1)S(1)}, s32[]{:S(2)}) async-start(s8[16777216]{0:T(1024)(128)(4,1)} %bitcast.2), calls=%async_computation.4 | async-start | bytes 8388608
  2.0 40.6 %slice-start.1 = ((s8[16777216]{0:T(1024)(128)(4,1)}), s8[4194304]{0:T(1024)(128)(4,1)S(1)}, s32[]{:S(2)}) async-start(s8[16777216]{0:T(1024)(128)(4,1)} %bitcast.2), calls=%async_computation.5 | async-start | bytes 8388608
  2.0 40.6 %slice-start.2 = ((s8[16777216]{0:T(1024)(128)(4,1)}), s8[4194304]{0:T(1024)(128)(4,1)S(1)}, s32[]{:S(2)}) async-start(s8[16777216]{0:T(1024)(128)(4,1)} %bitcast.2), calls=%async_computation.6 | async-start | bytes 8388608
  16.7 1.3 %collective-permute-start = (bf16[8,8,1024]{2,1,0:T(8,128)(2,1)S(1)}, bf16[8,8,1024]{2,1,0:T(8,128)(2,1)S(1)}, u32[]{:S(2)}, u32[]{:S(2)}) collective-permute-start(bf16[8,8,1024]{2,1,0:T(8,128)(2,1)S(1)} %all_to_all.20.near), channel_id=1, source_target_pairs={{0,1},{1,0},{2,3},{3,2},{4,5},{5,4},{6,7},{7,6},{8,9},{9,8},{10,11... | collective-permute-start | bytes 393224 | tf_op jit(solution)/shard_map/ppermute | solution.py:42
  18.0 24.5 %slice-start.3 = ((s8[16777216]{0:T(1024)(128)(4,1)}), s8[4194304]{0:T(1024)(128)(4,1)S(1)}, s32[]{:S(2)}) async-start(s8[16777216]{0:T(1024)(128)(4,1)} %bitcast.2), calls=%async_computation.7 | async-start | bytes 8388608
  18.6 2.5 %collective-permute-start.1 = (f32[8,512]{1,0:T(8,128)S(1)}, f32[8,512]{1,0:T(8,128)S(1)}, u32[]{:S(2)}, u32[]{:S(2)}) collective-permute-start(f32[8,512]{1,0:T(8,128)S(1)} %get-tuple-element.24), channel_id=1, source_target_pairs={{0,1},{1,0},{2,3},{3,2},{4,5},{5,4},{6,7},{7,6},{8,9},{9,8},{10,11... | collective-permute-start | bytes 49160 | tf_op jit(solution)/shard_map/ppermute | solution.py:42
  18.7 11.9 %copy-start.2 = (bf16[36,128,128]{2,1,0:T(8,128)(2,1)S(1)}, bf16[36,128,128]{2,1,0:T(8,128)(2,1)}, u32[]{:S(2)}) copy-start(bf16[36,128,128]{2,1,0:T(8,128)(2,1)} %k_near) | copy-start | bytes 3538948
  18.7 11.9 %copy-start.3 = (bf16[36,128,128]{2,1,0:T(8,128)(2,1)S(1)}, bf16[36,128,128]{2,1,0:T(8,128)(2,1)}, u32[]{:S(2)}) copy-start(bf16[36,128,128]{2,1,0:T(8,128)(2,1)} %v_near) | copy-start | bytes 3538948
  30.6 1.9 %collective-permute-start.4 = (bf16[8,128]{1,0:T(8,128)(2,1)S(1)}, bf16[8,128]{1,0:T(8,128)(2,1)S(1)}, u32[]{:S(2)}, u32[]{:S(2)}) collective-permute-start(bf16[8,128]{1,0:T(8,128)(2,1)S(1)} %shard_map.110.near_row), channel_id=1, source_target_pairs={{0,1},{1,0},{2,3},{3,2},{4,5},{5,4},{6,7},{7,6},{8,9},{9,8},{10,11... | collective-permute-start | bytes 6152 | tf_op jit(solution)/shard_map/ppermute | solution.py:42
  44.0 1.4 %collective-permute-start.5 = (bf16[8,8,1024]{2,1,0:T(8,128)(2,1)S(1)}, bf16[8,8,1024]{2,1,0:T(8,128)(2,1)S(1)}, u32[]{:S(2)}, u32[]{:S(2)}) collective-permute-start(bf16[8,8,1024]{2,1,0:T(8,128)(2,1)S(1)} %get-tuple-element.32), channel_id=1, source_target_pairs={{0,1},{1,0},{2,3},{3,2},{4,5},{5,4},{6,7},{7,6},{8,9},{9,8},{10,11... | collective-permute-start | bytes 393224 | tf_op jit(solution)/shard_map/ppermute | solution.py:42
